TPU v7x, 128 devices: a whole 4x4x4 slice. The times are simulated.
128 devices in a mesh: dp: 4 (over y_hi, core), fsdp: 32 (over z, y_lo, x).
Axes of the slice: x: 4, y: 4 (y_hi: 2, y_lo: 2; y = y_hi * 2 + y_lo), z: 4, core: 2. Of those that a mesh axis runs over, the one named last changes fastest.
Arguments:
- images: bfloat16 [512, 16, 16, 512], P(('dp', 'fsdp')), may hold values from -6 to 6
- routes: int32 [512, 1], P(('dp', 'fsdp')), may hold values from 0 to 3; in each aligned block of 4 rows (0 to 3, 4 to 7, ...) at most 2 rows name the same one
- bucket: int32 [512], P(('dp', 'fsdp')), may hold values from 0 to 7
- heights: int32 [8], replicated, may hold values from 8 to 16, as said below
- widths: int32 [8], replicated, may hold values from 8 to 16, as said below
- w_conv: bfloat16 [512, 9, 512], P('fsdp'), may hold values from -0.09375 to 0.09375
- w_down: bfloat16 [2048, 512], P('fsdp'), may hold values from -0.125 to 0.125
- w_up: bfloat16 [512, 2048], P('fsdp'), may hold values from -0.25 to 0.25
- norm_gain: float32 [512], replicated, may hold values from 0.1 to 1.9
- norm_shift: float32 [512], replicated, may hold values from -3 to 3
- cotangent: bfloat16 [1024, 16, 16, 512], P(('dp', 'fsdp')), may hold values from -6 to 6
Outputs:
- block_out: float32 [1024, 16, 16, 512], P(('dp', 'fsdp'))
- grad_conv: float32 [512, 9, 512], P('fsdp')
- grad_down: float32 [2048, 512], P('fsdp')
- grad_up: float32 [512, 2048], P('fsdp')
Inputs may be any that keep to these rules, and one draw needn't show every extreme that they name: Even heights; one bucket is 16 high and one is 8 high. Even widths; one bucket is 16 wide and one is 8 wide. `routes`: the rows of one device name one owner at most 2 times.
All inputs are finite; a program needn't handle non-finite values.
Results may differ from a plain program's by a relative error of at most 0.0052.
Values may be sent and summed in bfloat16 or wider, within the bound.
No kernel may reach another device: no remote copies, remote signals or barrier semaphores. Data moves between devices by JAX's collectives and lax.ppermute only.
A program may use at most 128 MiB of HBM per device.

v0:
```python
import math

import jax
import jax.numpy as jnp
from jax import lax
from jax.sharding import PartitionSpec as P

GROUPS = 32


epsilon = 1e-05


def make_masks(slot_ids, heights, widths, extent):
    bucket_ids = jnp.arange(heights.shape[0], dtype=jnp.int32)
    chosen = (slot_ids[:, None] == bucket_ids[None, :]).astype(jnp.int32)
    heights_of = jnp.sum(chosen * heights[None, :], axis=1)
    widths_of = jnp.sum(chosen * widths[None, :], axis=1)
    position = jnp.arange(extent, dtype=jnp.int32)
    inside = (position[None, :, None] < heights_of[:, None, None]) & (
        position[None, None, :] < widths_of[:, None, None]
    )
    return inside.astype(jnp.float32)[..., None]


def space_to_depth(values):
    batch, extent, _, channels = values.shape
    values = values.reshape(batch, extent // 2, 2, extent // 2, 2, channels).transpose(
        0, 1, 3, 2, 4, 5
    )
    return values.reshape(batch, extent // 2, extent // 2, 4 * channels)


def depth_to_space(values):
    batch, half, _, folded = values.shape
    channels = folded // 4
    values = values.reshape(batch, half, half, 2, 2, channels).transpose(0, 1, 3, 2, 4, 5)
    return values.reshape(batch, 2 * half, 2 * half, channels)


def group_stats(values, masks):
    batch = values.shape[0]
    channels = values.shape[-1]
    group_width = channels // GROUPS
    counted = jnp.maximum(jnp.sum(masks, axis=(1, 2, 3)) * group_width, 1.0)
    per_chan = jnp.sum(values * masks, axis=(1, 2))
    centre = jnp.sum(per_chan.reshape(batch, GROUPS, group_width), axis=2) / counted[:, None]
    mean_chan = jnp.repeat(centre, group_width, axis=1)
    centred = (values - mean_chan[:, None, None, :]) * masks
    squares = jnp.sum(centred * centred, axis=(1, 2)).reshape(batch, GROUPS, group_width)
    variance = jnp.sum(squares, axis=2) / counted[:, None]
    inverse = lax.rsqrt(variance + epsilon)
    return (mean_chan, jnp.repeat(inverse, group_width, axis=1))


def contract_rows(left, right):
    return lax.dot_general(
        left, right, (((0,), (0,)), ((), ())), preferred_element_type=jnp.float32
    )


def block_pass(slabs, masks, cot_slabs, w_conv, w_down, w_up, norm_gain, norm_shift, loss_scale):
    batch, extent, _, channels = slabs.shape
    half = extent // 2
    inputs = slabs.astype(jnp.float32)
    mean_chan, inv_chan = group_stats(inputs, masks)
    normed = (inputs - mean_chan[:, None, None, :]) * inv_chan[
        :, None, None, :
    ] * norm_gain + norm_shift
    activated = (jax.nn.silu(normed) * masks).astype(jnp.bfloat16)
    padded = jnp.pad(activated, ((0, 0), (1, 1), (1, 1), (0, 0)))
    windows = [
        padded[:, row_off : row_off + extent, col_off : col_off + extent, :].reshape(-1, channels)
        for row_off in range(3)
        for col_off in range(3)
    ]
    convolved = jnp.zeros((batch * extent * extent, channels), jnp.float32)
    for tap in range(9):
        convolved = convolved + jnp.dot(
            windows[tap], w_conv[:, tap, :], preferred_element_type=jnp.float32
        )
    convolved = convolved.reshape(batch, extent, extent, channels)
    skip_wide = (inputs + convolved) * masks
    skipped = skip_wide.astype(jnp.bfloat16)
    folded = space_to_depth(skipped).reshape(-1, 4 * channels)
    lowered = jnp.dot(folded, w_down, preferred_element_type=jnp.float32).astype(jnp.bfloat16)
    raised = jnp.dot(lowered, w_up, preferred_element_type=jnp.float32).reshape(
        batch, half, half, 4 * channels
    )
    outputs = (skip_wide + depth_to_space(raised)) * masks
    grad_out = cot_slabs.astype(jnp.float32) * masks * loss_scale
    grad_rounded = grad_out.astype(jnp.bfloat16)
    grad_folded = space_to_depth(grad_rounded).reshape(-1, 4 * channels)
    grad_up = contract_rows(lowered, grad_folded)
    grad_low = lax.dot_general(
        grad_folded, w_up, (((1,), (1,)), ((), ())), preferred_element_type=jnp.float32
    ).astype(jnp.bfloat16)
    grad_down = contract_rows(folded, grad_low)
    returned_grad = lax.dot_general(
        grad_low, w_down, (((1,), (1,)), ((), ())), preferred_element_type=jnp.float32
    ).reshape(batch, half, half, 4 * channels)
    grad_skip = (
        ((grad_out + depth_to_space(returned_grad)) * masks)
        .astype(jnp.bfloat16)
        .reshape(-1, channels)
    )
    grad_conv = jnp.stack([contract_rows(windows[tap], grad_skip) for tap in range(9)], axis=1)
    return (outputs, grad_conv, grad_down, grad_up)


def per_device(
    images, routes, bucket, heights, widths, w_conv, w_down, w_up, norm_gain, norm_shift, cotangent
):
    local_count = images.shape[0]
    extent = images.shape[1]
    replicas = lax.axis_size("dp")
    capacity = cotangent.shape[0] // replicas
    slot_total = replicas * capacity
    loss_scale = 1.0 / math.sqrt(local_count * replicas * lax.axis_size("fsdp") * extent * extent)
    target = routes[:, 0]
    position = jnp.arange(local_count, dtype=jnp.int32)
    earlier = position[None, :] < position[:, None]
    same_owner = target[:, None] == target[None, :]
    order_in = jnp.sum((same_owner & earlier).astype(jnp.int32), axis=1)
    slot_of = target * capacity + order_in
    placing = jnp.arange(slot_total, dtype=jnp.int32)[:, None] == slot_of[None, :]
    placing_bf = placing.astype(jnp.bfloat16)
    full_conv, full_down, full_up = (
        lax.all_gather(w_conv, "fsdp", axis=0, tiled=True),
        lax.all_gather(w_down, "fsdp", axis=0, tiled=True),
        lax.all_gather(w_up, "fsdp", axis=0, tiled=True),
    )
    flattened = images.reshape(local_count, -1)
    outgoing = jnp.dot(placing_bf, flattened, preferred_element_type=jnp.float32)
    outgoing = outgoing.astype(jnp.bfloat16).reshape((slot_total,) + images.shape[1:])
    outgoing_ids = jnp.sum(placing.astype(jnp.int32) * (bucket[None, :] + 1), axis=1) - 1
    arrived, arrived_ids = (
        lax.all_to_all(outgoing, "dp", split_axis=0, concat_axis=0, tiled=True),
        lax.all_to_all(outgoing_ids, "dp", split_axis=0, concat_axis=0, tiled=True),
    )
    masks = make_masks(arrived_ids, heights, widths, extent)
    block_out, grad_conv, grad_down, grad_up = block_pass(
        arrived, masks, cotangent, full_conv, full_down, full_up, norm_gain, norm_shift, loss_scale
    )
    gradients = (grad_conv, grad_down, grad_up)
    summed = lax.psum((gradients[0], gradients[1], gradients[2]), "dp")
    shares = (
        lax.psum_scatter(summed[0], "fsdp", scatter_dimension=0, tiled=True),
        lax.psum_scatter(summed[1], "fsdp", scatter_dimension=0, tiled=True),
        lax.psum_scatter(summed[2], "fsdp", scatter_dimension=0, tiled=True),
    )
    return (block_out, shares[0], shares[1], shares[2])


def solution(mesh):
    return jax.shard_map(
        per_device,
        mesh=mesh,
        in_specs=(
            P(("dp", "fsdp"), None, None, None),
            P(("dp", "fsdp"), None),
            P(("dp", "fsdp")),
            P(),
            P(),
            P("fsdp", None, None),
            P("fsdp", None),
            P("fsdp", None),
            P(),
            P(),
            P(("dp", "fsdp"), None, None, None),
        ),
        out_specs=(
            P(("dp", "fsdp"), None, None, None),
            P("fsdp", None, None),
            P("fsdp", None),
            P("fsdp", None),
        ),
        check_vma=False,
    )
```

profile of v0, /device:TPU:1, one launch (start us, length us, event | category | flops | bytes accessed | tf_op | source)
XLA Modules:
  0.0 1112.3 jit_solution(4653418553721609791)
XLA Ops:
  11.7 6.0 all-to-all-start.1
  23.0 4.8 all-to-all-start
  29.7 29.3 %all-to-all-done = bf16[8,16,16,512]{3,2,1,0:T(8,128)(2,1)S(1)} async-done(((bf16[8,16,16,512]{3,2,1,0:T(8,128)(2,1)}), bf16[8,16,16,512]{3,2,1,0:T(8,128)(2,1)S(1)}, u32[]{:S(2)}, u32[]{:S(2)}) %all-to-all-start) | async-done | bytes 2097184 | tf_op jit(solution)/shard_map/all_to_all | solution.py:138
  58.9 3.9 fusion.15
  62.8 4.3 reshape.168
  67.1 4.9 copy.47
  72.0 4.6 reshape_reshape.14
  77.1 68.2 %all-gather.8.cloned.1.call-done = bf16[512,2048]{1,0:T(8,128)(2,1)} async-done(((bf16[16,2048]{1,0:T(8,128)(2,1)}), bf16[512,2048]{1,0:T(8,128)(2,1)}) %all-gather.8.cloned.1.call-update) | async-done | bytes 2097168 | tf_op jit(solution)/shard_map/all_gather | solution.py:131
  145.3 3.5 convolution_convert_fusion.1
  148.8 151.7 %all-gather.6.cloned.1.call-done = bf16[2048,512]{1,0:T(8,128)(2,1)} async-done(((bf16[64,512]{1,0:T(8,128)(2,1)}), bf16[2048,512]{1,0:T(8,128)(2,1)}) %all-gather.6.cloned.1.call-update) | async-done | bytes 2097168 | tf_op jit(solution)/shard_map/all_gather | solution.py:130
  303.4 6.1 copy.34
  309.5 6.1 reshape.169
  315.6 4.6 multiply_convert_fusion
  323.8 8.1 pad_slice_fusion
  331.9 131.9 %all-gather.4.cloned.1.call-done = bf16[512,9,512]{2,0,1:T(8,128)(2,1)} async-done(((bf16[16,9,512]{2,0,1:T(8,128)(2,1)}), bf16[512,9,512]{2,0,1:T(8,128)(2,1)}) %all-gather.4.cloned.1.call-update) | async-done | bytes 4718608 | tf_op jit(solution)/shard_map/all_gather | solution.py:129
  470.8 3.3 fusion.31
  487.1 3.3 fusion.33
  490.4 11.8 %add_add_fusion = f32[2048,512]{1,0:T(8,128)S(1)} fusion(f32[2048,512]{1,0:T(8,128)} %fusion.26, f32[2048,512]{1,0:T(8,128)} %fusion.27, f32[2048,512]{1,0:T(8,128)} %fusion.28, f32[2048,512]{1,0:T(8,128)S(1)} %fusion.29, f32[2048,512]{1,0:T(8,128)} %fusion.30, f32[2048,512]{1,0:T(8,128)} %fusion.31, f32[2048,512]{1,0:T(8,128)} %fusion.33, ...), kind=kOutput, calls=%fused_computation.31 | convolution fusion | flops 1082130432 | bytes 40370176 | tf_op jit(solution)/shard_map/dot_general | solution.py:79
  506.1 4.1 reshape.166
  510.3 4.9 copy.48
  515.2 4.9 reshape_reshape.12
  520.0 4.8 fusion.38
  525.0 3.6 fusion.25
  537.3 3.3 fusion.39
  540.8 4.6 fusion.21
  557.7 6.1 copy.32
  563.7 6.2 reshape.167
  569.9 118.3 %reduce-scatter.6.cloned.1.call-done = f32[64,512]{1,0:T(8,128)} async-done(((f32[2048,512]{1,0:T(8,128)}), f32[64,512]{1,0:T(8,128)}) %reduce-scatter.6.cloned.1.call-update) | async-done | bytes 131088 | tf_op jit(solution)/shard_map/reduce_scatter | solution.py:149
  688.2 165.4 %reduce-scatter.8.cloned.1.call-done = f32[16,2048]{1,0:T(8,128)} async-done(((f32[512,2048]{1,0:T(8,128)}), f32[16,2048]{1,0:T(8,128)}) %reduce-scatter.8.cloned.1.call-update) | async-done | bytes 131088 | tf_op jit(solution)/shard_map/reduce_scatter | solution.py:150
  853.6 183.0 %reduce-scatter.4.cloned.1.call-done = f32[16,9,512]{2,0,1:T(8,128)} async-done(((f32[512,9,512]{2,0,1:T(8,128)}), f32[16,9,512]{2,0,1:T(8,128)}) %reduce-scatter.4.cloned.1.call-update) | async-done | bytes 294928 | tf_op jit(solution)/shard_map/reduce_scatter | solution.py:148
  1036.6 6.2 add_multiply_fusion
  1042.8 57.6 %all-reduce.4.cloned.1.call-done = (f32[16,9,512]{2,0,1:T(8,128)}, f32[64,512]{1,0:T(8,128)}, f32[16,2048]{1,0:T(8,128)}) async-done(((f32[16,9,512]{2,0,1:T(8,128)}, f32[64,512]{1,0:T(8,128)}, f32[16,2048]{1,0:T(8,128)}), (f32[16,9,512]{2,0,1:T(8,128)}, f32[64,512]{1,0:T(8,128)}, f32[16,2048]{1,0:T(8,128)})) %all-reduce.4.cloned.1.call-update) | async-done | bytes 557072 | tf_op jit(solution)/shard_map/psum | solution.py:146
  (109 shorter events, 68.5 us)
Async XLA Ops:
  7.2 138.2 %all-gather.8.cloned.1.call-start = ((), (), s32[]{:S(2)}) async-start(), calls=%async_computation.7 | async-start | bytes 2162688 | tf_op jit(solution)/shard_map/all_gather | solution.py:131
  7.9 292.6 %all-gather.6.cloned.1.call-start = ((), (), s32[]{:S(2)}) async-start(), calls=%async_computation.6 | async-start | bytes 2162688 | tf_op jit(solution)/shard_map/all_gather | solution.py:130
  8.6 455.1 %all-gather.4.cloned.1.call-start = ((), (), s32[]{:S(2)}) async-start(), calls=%async_computation.5 | async-start | bytes 4866048 | tf_op jit(solution)/shard_map/all_gather | solution.py:129
  11.7 11.2 %all-to-all-start.1 = ((s32[4,2,1]{1,2,0:T(1,128)}), s32[4,2,1]{1,2,0:T(1,128)S(1)}, u32[]{:S(2)}, u32[]{:S(2)}) async-start(s32[4,2,1]{1,2,0:T(1,128)} %bitcast.2), calls=%async_computation.1 | async-start | bytes 4096 | tf_op jit(solution)/shard_map/all_to_all | solution.py:139
  20.9 8.1 copy-start.21
  20.9 8.1 copy-start.22
  23.0 36.0 %all-to-all-start = ((bf16[8,16,16,512]{3,2,1,0:T(8,128)(2,1)}), bf16[8,16,16,512]{3,2,1,0:T(8,128)(2,1)S(1)}, u32[]{:S(2)}, u32[]{:S(2)}) async-start(bf16[8,16,16,512]{3,2,1,0:T(8,128)(2,1)} %copy.29), calls=%async_computation | async-start | bytes 4194304 | tf_op jit(solution)/shard_map/all_to_all | solution.py:138
  27.8 660.4 %reduce-scatter.6.cloned.1.call-start = ((), (), s32[]{:S(2)}) async-start(), calls=%async_computation.9 | async-start | bytes 4325376 | tf_op jit(solution)/shard_map/reduce_scatter | solution.py:149
  315.6 5.1 copy-start.19
  315.6 5.1 copy-start.20
  322.4 1.3 copy-start
  463.8 3.1 copy-start.10
  463.8 3.8 copy-start.17
  467.5 3.3 copy-start.9
  470.8 3.3 copy-start.8
  474.1 3.2 copy-start.7
  477.3 3.2 copy-start.6
  480.5 3.3 copy-start.5
  483.8 3.3 copy-start.4
  487.1 3.3 copy-start.15
  502.2 2.1 copy-start.3
  524.9 328.7 %reduce-scatter.8.cloned.1.call-start = ((), (), s32[]{:S(2)}) async-start(), calls=%async_computation.10 | async-start | bytes 4325376 | tf_op jit(solution)/shard_map/reduce_scatter | solution.py:150
  524.9 3.6 copy-start.1
  524.9 3.6 copy-start.11
  531.2 1.6 copy-start.13
  531.2 2.2 copy-start.18
  533.4 3.9 copy-start.14
  533.4 3.9 copy-start.16
  540.6 495.9 %reduce-scatter.4.cloned.1.call-start = ((), (), s32[]{:S(2)}) async-start(), calls=%async_computation.8 | async-start | bytes 9732096 | tf_op jit(solution)/shard_map/reduce_scatter | solution.py:148
  540.8 4.6 copy-start.2
  540.8 4.6 copy-start.12
  554.8 545.6 %all-reduce.4.cloned.1.call-start = ((), (), s32[]{:S(2)}) async-start(), calls=%async_computation.11 | async-start | bytes 1114112 | tf_op jit(solution)/shard_map/psum | solution.py:146
Sparse Core Ops, SparseCore 0:
  9.6 135.6 all-gather.7
  147.0 153.4 all-gather.5
  302.2 161.5 all-gather.3
  525.0 163.1 reduce-scatter.5
  690.4 163.1 reduce-scatter.7
  855.8 180.6 reduce-scatter.3
  1039.2 61.1 all-reduce.3
where the time goes:
time: 1120 us; the launch traced here: 1110 us
  waiting for transfers between devices  907 us (81%)
  matrix products  78.9 us (7%)
  local copies, waits for them, and re-layouts  78.6 us (7%)
  other arithmetic  21.6 us (2%)
  between operations  14.6 us (1%)
    reduce_scatter x1, waiting for transfers between devices, per_device(): lax.psum_scatter(summed[0], 'fsdp', scatter_dimension=0, tiled=True)  183 us
    reduce_scatter x1, waiting for transfers between devices, per_device(): lax.psum_scatter(summed[2], 'fsdp', scatter_dimension=0, tiled=True)  165 us
    all_gather x1, waiting for transfers between devices, per_device(): lax.all_gather(w_down, 'fsdp', axis=0, tiled=True)  152 us
    all_gather x1, waiting for transfers between devices, per_device(): lax.all_gather(w_conv, 'fsdp', axis=0, tiled=True)  132 us
    reduce_scatter x1, waiting for transfers between devices, per_device(): lax.psum_scatter(summed[1], 'fsdp', scatter_dimension=0, tiled=True)  118 us
    all_gather x1, waiting for transfers between devices, per_device(): lax.all_gather(w_up, 'fsdp', axis=0, tiled=True)  68.2 us
    psum x1, waiting for transfers between devices, per_device(): summed = lax.psum((gradients[0], gradients[1], gradients[2]), 'dp')  57.6 us
    dot_general x9, matrix products, block_pass(): jnp.dot(windows[tap], w_conv[:, tap, :], preferred_element_type=jnp.float32)  37.7 us
  transfers between devices with their start and end apart: 9, of which 8 were waited for; matrix products, arithmetic and copies ran while one was open for 10% of the time, Pallas kernels for 0%

commit v1 on v0

v1 whole, which is shorter than its diff:
```python
import functools
import math

import jax
import jax.numpy as jnp
from jax import lax
from jax.experimental import pallas as pl
from jax.experimental.pallas import tpu as pltpu
from jax.sharding import PartitionSpec as P

GROUPS = 32
epsilon = 1e-05
BF = jnp.bfloat16
F32 = jnp.float32
I32 = jnp.int32
AXES = ("dp", "fsdp")
VMEM_BYTES = 56 * 1024 * 1024


def moved(fn):
    pairs = []
    for index in range(128):
        dp, fsdp = index // 32, index % 32
        place = (dp // 2, dp % 2, fsdp // 8, fsdp // 4 % 2, fsdp % 4)
        h, c, z, y, x = fn(*place)
        pairs.append((index, (h * 2 + c) * 32 + z * 8 + y * 4 + x))
    return pairs


STEP = {
    "y": moved(lambda h, c, z, y, x: (h, c, z, 1 - y, x)),
    "hy": moved(lambda h, c, z, y, x: (1 - h, c, z, 1 - y, x)),
    "c": moved(lambda h, c, z, y, x: (h, 1 - c, z, y, x)),
    "h": moved(lambda h, c, z, y, x: (1 - h, c, z, y, x)),
    "hc": moved(lambda h, c, z, y, x: (1 - h, 1 - c, z, y, x)),
}
PLANES = [[z * 8 + y * 4 + x for z in range(4) for x in range(4)] for y in range(2)]


def send(value, move):
    return lax.ppermute(value, AXES, STEP[move])


def over_dp(blocks):
    own, beside, across, both = blocks
    return (own, send(beside, "c"), send(across, "h"), send(both, "hc"))


def over_column(parts, y):
    kept = lax.dynamic_index_in_dim(parts, y, axis=0, keepdims=False)
    given = lax.dynamic_index_in_dim(parts, 1 - y, axis=0, keepdims=False)
    sent = given.astype(BF)
    got = (send(sent, "y"), send(kept.astype(BF), "h"), send(sent, "hy"))
    total = kept + got[0].astype(F32) + got[1].astype(F32) + got[2].astype(F32)
    return total, send(total, "c")


def over_plane(blocks):
    return lax.all_to_all(
        blocks, "fsdp", split_axis=0, concat_axis=0, axis_index_groups=PLANES, tiled=True
    )


def dot(left, right, left_dim, right_dim):
    return lax.dot_general(
        left, right, (((left_dim,), (right_dim,)), ((), ())), preferred_element_type=F32
    )


def kernel_call(body, out_shape, flops, moved_bytes, scratch=(), **more):
    return pl.pallas_call(
        body,
        out_shape=out_shape,
        scratch_shapes=list(scratch),
        compiler_params=pltpu.CompilerParams(vmem_limit_bytes=VMEM_BYTES),
        cost_estimate=pl.CostEstimate(
            flops=int(flops), bytes_accessed=int(moved_bytes), transcendentals=0
        ),
        **more,
    )


def laned(extent_rows, extent_columns, lanes):
    block = min(128, lanes)
    return pltpu.VMEM((lanes // block, extent_rows, extent_columns, block), F32)


def put_line(ref, row, first, values):
    block = ref.shape[3]
    for b in range(ref.shape[0]):
        ref[b, row, first : first + values.shape[0], :] = values[:, b * block : (b + 1) * block]


def get_line(ref, row):
    return jnp.concatenate([ref[b, row] for b in range(ref.shape[0])], axis=1)


def every_second(ref, row, first, side):
    places = [
        ref[pl.ds(b, 1), pl.ds(row, 1), pl.ds(first, side, stride=2), :].reshape(side, ref.shape[3])
        for b in range(ref.shape[0])
    ]
    return jnp.concatenate(places, axis=1)


def put_every_second(ref, row, first, values):
    side, block = values.shape[0], ref.shape[3]
    for b in range(ref.shape[0]):
        ref[pl.ds(b, 1), pl.ds(row, 1), pl.ds(first, side, stride=2), :] = values[
            :, b * block : (b + 1) * block
        ].reshape(1, 1, side, block)


WHOLE = pl.BlockSpec(memory_space=pltpu.VMEM)
SCALARS = pl.BlockSpec(memory_space=pltpu.SMEM)


def over_group(sums, width):
    lane = lax.broadcasted_iota(I32, sums.shape, 1)
    step = width // 2
    while step:
        lower = (lane & step) == 0
        lanes = sums.shape[1]
        sums = sums + jnp.where(
            lower, pltpu.roll(sums, lanes - step, 1), pltpu.roll(sums, step, 1)
        )
        step //= 2
    return sums


def norm_kernel(extent, meta, image, gain, shift, windows, residual, padded, raw):
    place = pl.program_id(0)
    channels = image.shape[2]
    half = channels // 2
    height, width = meta[place], meta[8 + place]
    core = meta[24]

    @pl.when(place == 0)
    def _():
        padded[...] = jnp.zeros_like(padded)

    inside = lax.broadcasted_iota(I32, (extent, channels), 0) < width

    def line(row):
        return image[0, row * extent : (row + 1) * extent, :].astype(F32)

    def mask(row):
        return (inside & (row < height)).astype(F32)

    group = channels // GROUPS
    counted = jnp.maximum((height * width * group).astype(F32), 1.0)
    total = jnp.zeros((extent, channels), F32)
    for row in range(extent):
        total = total + line(row) * mask(row)
    total = jnp.broadcast_to(jnp.sum(total, axis=0, keepdims=True), (8, channels))
    mean = (over_group(total, group) / counted)[:1]
    total = jnp.zeros((extent, channels), F32)
    for row in range(extent):
        centred = (line(row) - mean) * mask(row)
        total = total + centred * centred
    total = jnp.broadcast_to(jnp.sum(total, axis=0, keepdims=True), (8, channels))
    variance = (over_group(total, group) / counted)[:1]
    scale = lax.rsqrt(variance + epsilon) * gain[...]
    for row in range(extent):
        normed = (line(row) - mean) * scale + shift[...]
        put_line(padded, row + 1, 8, normed / (1.0 + jnp.exp(-normed)) * mask(row))
        residue = image[
            0, row * extent : (row + 1) * extent, pl.ds(pl.multiple_of(core * half, half), half)
        ]
        put_line(raw, row, 0, residue.astype(F32))
    side = extent // 2
    for p in range(4):
        for q in range(4):
            for i in range(0, side, 2):
                pair = [every_second(padded, 2 * n + p, 7 + q, side) for n in (i, i + 1)]
                windows[p * 4 + q, i * side : (i + 2) * side, :] = jnp.concatenate(pair).astype(BF)
    for k in range(4):
        for i in range(0, side, 2):
            pair = [every_second(raw, 2 * n + k // 2, k % 2, side) for n in (i, i + 1)]
            residual[k, i * side : (i + 2) * side, :] = jnp.concatenate(pair).astype(BF)


def normed_windows(meta, images, gain, shift):
    count, extent, _, channels = images.shape
    pixels, half = extent * extent, channels // 2
    quarter = pixels // 4
    return kernel_call(
        functools.partial(norm_kernel, extent),
        (
            jax.ShapeDtypeStruct((16, count * quarter, channels), BF),
            jax.ShapeDtypeStruct((4, count * quarter, half), BF),
        ),
        flops=40 * images.size,
        moved_bytes=12 * images.size,
        scratch=(
            laned(extent + 2, extent + 16, channels),
            laned(extent, extent, half),
        ),
        grid=(count,),
        in_specs=[
            SCALARS,
            pl.BlockSpec((1, pixels, channels), lambda g: (g, 0, 0)),
            pl.BlockSpec((1, channels), lambda g: (0, 0)),
            pl.BlockSpec((1, channels), lambda g: (0, 0)),
        ],
        out_specs=(
            pl.BlockSpec((16, quarter, channels), lambda g: (0, g, 0)),
            pl.BlockSpec((4, quarter, half), lambda g: (0, g, 0)),
        ),
    )(meta, images.reshape(count, pixels, channels), gain[None, :], shift[None, :])


def gather_up(pieces, up):
    rows = pieces.shape[2]
    for f in range(32):
        z, y, x = f // 8, f // 4 % 2, f % 4
        for k in range(4):
            up[k, f * rows : (f + 1) * rows, :] = pieces[z * 4 + x, y * 4 + k]


def gather_down(pieces, down):
    rows, half = pieces.shape[2:]
    for z in range(4):
        for x in range(4):
            for unit in range(8):
                side, step = unit // 4, unit % 4
                first = (x * 4 + step) * rows
                down[z, first : first + rows, side * half : (side + 1) * half] = pieces[
                    z * 4 + x, 8 + unit
                ]


def swapped_sum(own, got):
    middle = own.shape[0] // 2
    return jnp.concatenate(
        [own[:middle] + got[middle:], own[middle:] + got[:middle]], axis=0
    ).astype(BF)


def glow_kernel(
    extent, loss_scale, meta, cot0, cot1, cot2, cot3, pieces, folded, part, raw, up, cot, sem
):
    side = extent // 2
    quarter = side * side
    half = cot.shape[2]
    slots = cot0.shape[0]
    copies = [
        pltpu.make_async_copy(ref, cot.at[pl.ds(r * slots, slots)], sem.at[r])
        for r, ref in enumerate((cot0, cot1, cot2, cot3))
    ]
    for copy in copies:
        copy.start()
    gather_up(pieces, up)
    for copy in copies:
        copy.wait()
    images = folded.shape[1] // quarter
    inside = lax.broadcasted_iota(I32, (extent, half), 0)

    def one(g, carry):
        height, width, slot = meta[g], meta[8 + g], meta[16 + g]
        for row in range(extent):
            kept = ((inside < width) & (row < height)).astype(F32)
            line = cot[slot, row * extent : (row + 1) * extent, :].astype(F32)
            put_line(raw, row, 0, line * kept)
        for k in range(4):
            for i in range(0, side, 2):
                pair = [every_second(raw, 2 * n + k // 2, k % 2, side) for n in (i, i + 1)]
                first = pl.multiple_of(g * quarter + i * side, 2 * side)
                folded[k, pl.ds(first, 2 * side), :] = jnp.concatenate(pair).astype(BF)
        return carry

    lax.fori_loop(0, images, one, 0)
    total = None
    for k in range(4):
        scaled = (folded[k].astype(F32) * loss_scale).astype(BF)
        term = dot(scaled, up[k], 1, 1)
        total = term if total is None else total + term
    part[...] = total


def grad_conv_kernel(
    loss_scale, mask, own, got, folded, pieces, windows_own, windows_pair, glow, grads, down, turned
):
    half = folded.shape[2]
    rows = grads.shape[2]
    middle = folded.shape[1] // 2
    gather_down(pieces, down)
    glow[...] = swapped_sum(own, got)
    kept = jnp.concatenate([mask[...]] * (half // mask.shape[1]), axis=1)
    for k in range(4):
        grad = folded[k].astype(F32) * loss_scale + dot(glow[...], down[k], 1, 1)
        turned[k] = (grad * kept).T.astype(BF)
    for t in range(9):
        total = None
        for k in range(4):
            v = (k // 2 + t // 3) * 4 + k % 2 + t % 3
            for columns, windows in ((slice(0, middle), windows_own), (slice(middle, None), windows_pair)):
                term = dot(turned[k, :, columns], windows[v], 1, 0)
                total = term if total is None else total + term
        total = total.T.astype(BF)
        for f in range(32):
            z, y, x = f // 8, f // 4 % 2, f % 4
            grads[z * 4 + x, y * 9 + t] = total[f * rows : (f + 1) * rows, :]


def conv_kernel(
    mask,
    conv_pieces,
    pieces,
    windows_own,
    windows_pair,
    residual_own,
    residual_pair,
    wide,
    skip,
    part,
    conv,
    down,
):
    half = wide.shape[2]
    rows = conv_pieces.shape[2]
    middle = wide.shape[1] // 2
    for f in range(32):
        z, y, x = f // 8, f // 4 % 2, f % 4
        for t in range(9):
            conv[t, f * rows : (f + 1) * rows, :] = conv_pieces[z * 4 + x, y * 9 + t]
    gather_down(pieces, down)
    total = None
    for k in range(4):
        for first, windows, residual in (
            (0, windows_own, residual_own),
            (middle, windows_pair, residual_pair),
        ):
            convolved = None
            for t in range(9):
                v = (k // 2 + t // 3) * 4 + k % 2 + t % 3
                term = dot(windows[v], conv[t], 1, 0)
                convolved = term if convolved is None else convolved + term
            kept = mask[first : first + middle, :]
            kept = jnp.concatenate([kept] * (half // mask.shape[1]), axis=1)
            masked = (residual[k].astype(F32) + convolved) * kept
            wide[k, first : first + middle, :] = masked
            skip[k, first : first + middle, :] = masked.astype(BF)
        term = dot(skip[k], down[k], 1, 0)
        total = term if total is None else total + term
    part[...] = total


def output_kernel(
    extent,
    loss_scale,
    meta,
    mask,
    own,
    got,
    wide,
    skip,
    glow,
    folded,
    pieces,
    back0,
    back1,
    back2,
    back3,
    grads,
    low,
    up,
    outputs,
    raw,
    returning,
):
    side = extent // 2
    quarter = side * side
    half = wide.shape[2]
    rows = grads.shape[2]
    images = wide.shape[1] // quarter
    gather_up(pieces, up)
    low[...] = swapped_sum(own, got)
    kept = jnp.concatenate([mask[...]] * (half // mask.shape[1]), axis=1)
    for k in range(4):
        outputs[k] = (wide[k] + dot(low[...], up[k], 1, 0)) * kept
    returning[...] = jnp.zeros_like(returning)

    def one(g, carry):
        slot = meta[16 + g]
        for k in range(4):
            for i in range(side):
                first = pl.multiple_of(g * quarter + i * side, side)
                put_every_second(raw, 2 * i + k // 2, k % 2, outputs[k, pl.ds(first, side), :])
        for row in range(extent):
            returning[slot, row * extent : (row + 1) * extent, :] = get_line(raw, row).astype(BF)
        return carry

    lax.fori_loop(0, images, one, 0)
    slots = back0.shape[0]
    for r, back in enumerate((back0, back1, back2, back3)):
        back[...] = returning[r * slots : (r + 1) * slots]
    turned = low[...].astype(F32).T.astype(BF)
    for k in range(4):
        scaled = (folded[k].astype(F32) * loss_scale).astype(BF)
        grad = dot(turned, scaled, 1, 0).astype(BF)
        for f in range(32):
            z, y, x = f // 8, f // 4 % 2, f % 4
            grads[z * 4 + x, y * 4 + k] = grad[f * rows : (f + 1) * rows, :]
        grad = dot(skip[k].astype(F32).T.astype(BF), glow[...], 1, 0).astype(BF)
        for x in range(4):
            for unit in range(8):
                side_of, step = unit // 4, unit % 4
                first = (x * 4 + step) * rows
                grads[k * 4 + x, 8 + unit] = grad[
                    first : first + rows, side_of * half : (side_of + 1) * half
                ]


def replicas(number, half):
    for r in range(4):
        chip, core = number // 2, number % 2
        chip = 1 - chip if r // 2 else chip
        core = 1 - core if r % 2 else core
        yield r, chip, pl.ds(pl.multiple_of(core * half, half), half)


def split_kernel(number, cot, out0, out1, out2, out3):
    outs = (out0, out1, out2, out3)
    slots, _, half = out0.shape
    for r, chip, lanes in replicas(number[0], half):
        outs[r][...] = cot[pl.ds(chip * slots, slots), :, lanes]


def join_kernel(number, back0, back1, back2, back3, out, wide, sem):
    backs = (back0, back1, back2, back3)
    slots, _, half = back0.shape
    copies = []
    for r, chip, lanes in replicas(number[0], half):
        wide[r] = backs[r][...].astype(F32)
        target = out.at[pl.ds(chip * slots, slots), :, lanes]
        copies.append(pltpu.make_async_copy(wide.at[r], target, sem.at[r]))
        copies[-1].start()
    for copy in copies:
        copy.wait()


def per_device(
    images, routes, bucket, heights, widths, w_conv, w_down, w_up, norm_gain, norm_shift, cotangent
):
    count, extent, _, channels = images.shape
    half = channels // 2
    pixels = extent * extent
    quarter = pixels // 4
    most = cotangent.shape[0] // 4
    rows = w_conv.shape[0]
    low_rows = 2 * count * quarter
    loss_scale = 1.0 / math.sqrt(count * 128 * pixels)
    dp, fsdp = lax.axis_index("dp"), lax.axis_index("fsdp")
    core, y = dp % 2, fsdp // 4 % 2

    conv_own = lax.dynamic_slice_in_dim(w_conv, core * half, half, axis=2).transpose(1, 0, 2)
    up_own = lax.dynamic_slice_in_dim(
        w_up.reshape(rows, 4, channels), core * half, half, axis=2
    ).transpose(1, 0, 2)
    down_own = w_down.reshape(4 * rows, 2, half).transpose(1, 0, 2).reshape(8, rows, half)
    packed = jnp.concatenate([up_own, down_own, conv_own])
    other = send(packed, "y")

    block = jax.ShapeDtypeStruct((2 * most, pixels, half), BF)
    number = dp.astype(I32).reshape(1)
    outgoing = kernel_call(
        split_kernel,
        (block,) * 4,
        flops=0,
        moved_bytes=4 * cotangent.size,
        in_specs=[SCALARS, WHOLE],
        out_specs=(WHOLE,) * 4,
    )(number, cotangent.reshape(4 * most, pixels, channels))
    outgoing, other = lax.optimization_barrier((outgoing, other))
    arrived = over_dp(outgoing)
    first = jnp.where(y == 0, packed, other)
    second = jnp.where(y == 0, other, packed)
    down_kept = jnp.where(core == 0, first[4:12], second[4:12])
    up_down = jnp.concatenate([first[:4], second[:4], down_kept])
    conv_two = jnp.concatenate([first[12:], second[12:]])
    up_down = over_plane(jnp.broadcast_to(up_down, (16, *up_down.shape)))
    conv_two = lax.all_gather(conv_two, "fsdp", axis_index_groups=PLANES)

    images_pair = send(images, "c")
    ids = jnp.concatenate([routes, bucket[:, None]], axis=1)
    ids_pair = send(ids, "c")

    def described(table, side):
        target = table[:, 0]
        position = jnp.arange(count, dtype=I32)
        earlier = position[None, :] < position[:, None]
        same_owner = target[:, None] == target[None, :]
        order_in = jnp.sum((same_owner & earlier).astype(I32), axis=1)
        slot = (target ^ dp) * 2 * most + side * most + order_in
        chosen = table[:, 1][:, None] == jnp.arange(heights.shape[0], dtype=I32)[None, :]
        height = jnp.sum(jnp.where(chosen, heights[None, :], 0), axis=1)
        width = jnp.sum(jnp.where(chosen, widths[None, :], 0), axis=1)
        return jnp.stack([height, width, slot])

    def numbers(first, second):
        parts = jnp.concatenate([first, second], axis=1).reshape(-1)
        return jnp.concatenate([parts, jnp.broadcast_to(core, (8,)).astype(I32)])

    own_facts, pair_facts = described(ids, core), described(ids_pair, 1 - core)
    own_meta = numbers(own_facts, own_facts)
    pair_meta = numbers(pair_facts, pair_facts)
    meta = numbers(own_facts, pair_facts)
    height, width = meta[:8], meta[8:16]
    place = jnp.arange(extent // 2, dtype=I32) * 2
    mask = (place[None, :, None] < height[:, None, None]) & (
        place[None, None, :] < width[:, None, None]
    )
    mask = jnp.broadcast_to(mask.astype(F32).reshape(low_rows, 1), (low_rows, min(128, half)))

    windows_own, residual_own = normed_windows(own_meta, images, norm_gain, norm_shift)
    windows_pair, residual_pair = normed_windows(pair_meta, images_pair, norm_gain, norm_shift)

    ready, windows_own, windows_pair = lax.optimization_barrier((meta, windows_own, windows_pair))
    folded, glow_part = kernel_call(
        functools.partial(glow_kernel, extent, loss_scale),
        (
            jax.ShapeDtypeStruct((4, low_rows, half), BF),
            jax.ShapeDtypeStruct((low_rows, channels), F32),
        ),
        flops=8 * low_rows * channels * half,
        moved_bytes=5 << 20,
        scratch=(
            laned(extent, extent, half),
            pltpu.VMEM((4, channels, half), BF),
            pltpu.VMEM((8 * most, pixels, half), BF),
            pltpu.SemaphoreType.DMA((4,)),
        ),
        in_specs=[SCALARS] + [pl.BlockSpec(memory_space=pl.ANY)] * 4 + [WHOLE],
        out_specs=(WHOLE, WHOLE),
    )(ready, *arrived, up_down)
    glow_got = send(glow_part, "c")

    glow, conv_grads = kernel_call(
        functools.partial(grad_conv_kernel, loss_scale),
        (
            jax.ShapeDtypeStruct((low_rows, channels), BF),
            jax.ShapeDtypeStruct((16, 18, rows, half), BF),
        ),
        flops=80 * low_rows * channels * half,
        moved_bytes=15 << 20,
        scratch=(pltpu.VMEM((4, half, channels), BF), pltpu.VMEM((4, half, low_rows), BF)),
        in_specs=[WHOLE] * 7,
        out_specs=(WHOLE, WHOLE),
    )(mask, glow_part, glow_got, folded, up_down, windows_own, windows_pair)
    conv_grads = over_plane(conv_grads)
    glow, windows_own, windows_pair = lax.optimization_barrier((glow, windows_own, windows_pair))

    wide, skip, low_part = kernel_call(
        conv_kernel,
        (
            jax.ShapeDtypeStruct((4, low_rows, half), F32),
            jax.ShapeDtypeStruct((4, low_rows, half), BF),
            jax.ShapeDtypeStruct((low_rows, channels), F32),
        ),
        flops=80 * low_rows * channels * half,
        moved_bytes=18 << 20,
        scratch=(pltpu.VMEM((9, channels, half), BF), pltpu.VMEM((4, half, channels), BF)),
        in_specs=[WHOLE] * 7,
        out_specs=(WHOLE,) * 3,
    )(mask, conv_two, up_down, windows_own, windows_pair, residual_own, residual_pair)
    low_got = send(low_part, "c")

    *returning, grads = kernel_call(
        functools.partial(output_kernel, extent, loss_scale),
        (
            *(block,) * 4,
            jax.ShapeDtypeStruct((16, 16, rows, half), BF),
        ),
        flops=24 * low_rows * channels * half,
        moved_bytes=14 << 20,
        scratch=(
            pltpu.VMEM((low_rows, channels), BF),
            pltpu.VMEM((4, channels, half), BF),
            pltpu.VMEM((4, low_rows, half), F32),
            laned(extent, extent, half),
            pltpu.VMEM((8 * most, pixels, half), BF),
        ),
        in_specs=[SCALARS] + [WHOLE] * 8,
        out_specs=(WHOLE,) * 5,
    )(meta, mask, low_part, low_got, wide, skip, glow, folded, up_down)
    returned = over_dp(returning)
    grads = over_plane(grads)

    conv_sum = jnp.sum(conv_grads.astype(F32), axis=0).reshape(2, 9, rows, half)
    conv_sum, returned = lax.optimization_barrier((conv_sum, returned))

    def by_core(own, pair):
        return jnp.where(core == 0, jnp.stack([own, pair]), jnp.stack([pair, own]))

    out_conv = by_core(*over_column(conv_sum, y)).transpose(2, 1, 0, 3)
    out_conv = out_conv.reshape(rows, 9, channels)
    grads_sum = jnp.sum(grads.astype(F32), axis=0)
    up_sum, down_sum = grads_sum[:8].reshape(2, 4, rows, half), grads_sum[8:]
    shares = jnp.concatenate([up_sum, jnp.broadcast_to(down_sum, (2, *down_sum.shape))], axis=1)
    shares, out_conv = lax.optimization_barrier((shares, out_conv))
    own, pair = over_column(shares, y)
    out_up = by_core(own[:4], pair[:4]).transpose(2, 1, 0, 3).reshape(rows, 4 * channels)
    out_down = jnp.where(y == core, own[4:], pair[4:])
    out_down = out_down.reshape(2, 4 * rows, half).transpose(1, 0, 2).reshape(4 * rows, channels)

    block_out = kernel_call(
        join_kernel,
        jax.ShapeDtypeStruct((4 * most, pixels, channels), F32),
        flops=0,
        moved_bytes=6 * cotangent.size,
        scratch=(pltpu.VMEM((4, 2 * most, pixels, half), F32), pltpu.SemaphoreType.DMA((4,))),
        in_specs=[SCALARS] + [WHOLE] * 4,
        out_specs=pl.BlockSpec(memory_space=pl.ANY),
    )(number, *returned)
    return (block_out.reshape(cotangent.shape), out_conv, out_down, out_up)


def solution(mesh):
    return jax.shard_map(
        per_device,
        mesh=mesh,
        in_specs=(
            P(("dp", "fsdp"), None, None, None),
            P(("dp", "fsdp"), None),
            P(("dp", "fsdp")),
            P(),
            P(),
            P("fsdp", None, None),
            P("fsdp", None),
            P("fsdp", None),
            P(),
            P(),
            P(("dp", "fsdp"), None, None, None),
        ),
        out_specs=(
            P(("dp", "fsdp"), None, None, None),
            P("fsdp", None, None),
            P("fsdp", None),
            P("fsdp", None),
        ),
        check_vma=False,
    )
```

time: 1120 us -> 189 us (0.17)
  waiting for transfers between devices: 907 us -> 56.4 us
  matrix products: 78.9 us -> 0 us
  local copies, waits for them, and re-layouts: 78.6 us -> 11.6 us
  Pallas kernels: 0 us -> 58 us
  starting transfers between devices: 11.2 us -> 43.6 us
  other arithmetic: 21.6 us -> 4.4 us
    reduce_scatter x3 -> x0, waiting for transfers between devices: 467 us -> none  [the longest x1 183 us: per_device(): lax.psum_scatter(summed[0], 'fsdp', scatter_dimension=0, tiled=True)]
    all_gather x3 -> x1, waiting for transfers between devices: 352 us -> 0.02 us  [per_device(): conv_two = lax.all_gather(conv_two, 'fsdp', axis_index_groups=PLANES)]
    dot_general x25 -> x0, matrix products: 78.9 us -> none  [the longest x9 37.7 us: block_pass(): jnp.dot(windows[tap], w_conv[:, tap, :], preferred_element_type=jnp.float32)]
    pallas_call x0 -> x8, Pallas kernels: none -> 58 us  [the longest x2 13.1 us: normed_windows(): kernel_call(functools.partial(norm_kernel, extent), (jax.ShapeDtypeStruct...]
    psum x1 -> x0, waiting for transfers between devices: 57.6 us -> none  [per_device(): summed = lax.psum((gradients[0], gradients[1], gradients[2]), 'dp')]
    ppermute x0 -> x19, waiting for transfers between devices: none -> 43.8 us  [send(): return lax.ppermute(value, AXES, STEP[move])]
    reshape x9 -> x8, local copies, waits for them, and re-layouts: 32.7 us -> 4.34 us  [the longest x1 0.95 us: per_device(): out_conv = out_conv.reshape(rows, 9, channels)]
    ppermute x0 -> x19, starting transfers between devices: none -> 27.2 us  [send(): return lax.ppermute(value, AXES, STEP[move])]
  transfers between devices with their start and end apart: 9 -> 23, of which waited for: 8 -> 14; matrix products, arithmetic and copies ran while one was open for 10% -> 4% of each run, Pallas kernels for 0% -> 31%
where the time goes in v1:
time: 189 us; the launch traced here: 188 us
  Pallas kernels  58 us (31%)
  waiting for transfers between devices  56.4 us (30%)
  starting transfers between devices  43.6 us (23%)
  between operations  14.4 us (8%)
  local copies, waits for them, and re-layouts  11.6 us (6%)
  other arithmetic  4.4 us (2%)
    ppermute x19, waiting for transfers between devices, send(): return lax.ppermute(value, AXES, STEP[move])  43.8 us
    ppermute x19, starting transfers between devices, send(): return lax.ppermute(value, AXES, STEP[move])  27.2 us
    all_to_all x3, starting transfers between devices, over_plane(): lax.all_to_all(blocks, 'fsdp', split_axis=0, concat_axis=0, axis_index_gr...  16.3 us
    pallas_call x2, Pallas kernels, normed_windows(): kernel_call(functools.partial(norm_kernel, extent), (jax.ShapeDtypeStruct...  13.1 us
    all_to_all x3, waiting for transfers between devices, over_plane(): lax.all_to_all(blocks, 'fsdp', split_axis=0, concat_axis=0, axis_index_gr...  12.6 us
    pallas_call x1, Pallas kernels, per_device(): kernel_call(conv_kernel, (jax.ShapeDtypeStruct((4, low_rows, half), F32),...  12.6 us
    pallas_call x1, Pallas kernels, per_device(): kernel_call(functools.partial(grad_conv_kernel, loss_scale), (jax.ShapeDt...  12.4 us
    pallas_call x1, Pallas kernels, per_device(): kernel_call(functools.partial(output_kernel, extent, loss_scale), (*(bloc...  8.12 us
  transfers between devices with their start and end apart: 23, of which 14 were waited for; matrix products, arithmetic and copies ran while one was open for 4% of the time, Pallas kernels for 31%

profile of v1, /device:TPU:1, one launch (start us, length us, event | category | flops | bytes accessed | tf_op | source)
XLA Modules:
  0.0 188.4 jit_solution(10737363350250115612)
XLA Ops:
  9.1 2.2 %collective-permute-start.2 = (bf16[21,16,256]{2,1,0:T(8,128)(2,1)S(1)}, bf16[21,16,256]{2,1,0:T(8,128)(2,1)S(1)}, u32[]{:S(2)}, u32[]{:S(2)}) collective-permute-start(bf16[21,16,256]{2,1,0:T(8,128)(2,1)S(1)} %pad_maximum_fusion.1), channel_id=1, source_target_pairs={{0,4},{1,5},{2,6},{3,7},{4,0},{5,1},{6,2},{7,3},{8,12},{9,13},{10,... | collective-permute-start | bytes 516104 | tf_op jit(solution)/shard_map/ppermute | solution.py:41
  11.3 3.1 %shard_map.140 = (bf16[4,256,256]{2,1,0:T(8,128)(2,1)}, bf16[4,256,256]{2,1,0:T(8,128)(2,1)}, bf16[4,256,256]{2,1,0:T(8,128)(2,1)}, bf16[4,256,256]{2,1,0:T(8,128)(2,1)}) custom-call(s32[1]{0:T(128)} %bitcast.number, bf16[8,256,512]{2,1,0:T(8,128)(2,1)} %bitcast.77), custom_call_target="tpu_custom_call" | custom-call | bytes 4194304 | tf_op jit(solution)/shard_map/pallas_call | solution.py:467
  15.8 1.6 broadcast_in_dim.72
  17.4 8.0 %all-to-all-start = ((bf16[16,16,16,256]{3,2,1,0:T(8,128)(2,1)}), bf16[16,16,16,256]{3,2,1,0:T(8,128)(2,1)S(1)}, u32[]{:S(2)}, u32[]{:S(2)}) async-start(bf16[16,16,16,256]{3,2,1,0:T(8,128)(2,1)} %broadcast_in_dim.72), calls=%async_computation | async-start | bytes 4194304 | tf_op jit(solution)/shard_map/all_to_all | solution.py:59
  25.5 1.9 %collective-permute-start = (s32[4,2]{0,1:T(2,128)S(1)}, s32[4,2]{0,1:T(2,128)S(1)}, u32[]{:S(2)}, u32[]{:S(2)}) collective-permute-start(s32[4,2]{0,1:T(2,128)S(1)} %pad_add_fusion.2), channel_id=1, source_target_pairs={{0,32},{1,33},{2,34},{3,35},{4,36},{5,37},{6,38},{7,39},{8,40},{9,... | collective-permute-start | bytes 104 | tf_op jit(solution)/shard_map/ppermute | solution.py:41
  28.5 2.9 %collective-permute-start.4 = (bf16[4,256,256]{2,1,0:T(8,128)(2,1)}, bf16[4,256,256]{2,1,0:T(8,128)(2,1)}, u32[]{:S(2)}, u32[]{:S(2)}) collective-permute-start(bf16[4,256,256]{2,1,0:T(8,128)(2,1)} %get-tuple-element.51), channel_id=1, source_target_pairs={{0,64},{1,65},{2,66},{3,67},{4,68},{5,69},{6,70},{7,71},{8,72},{9,... | collective-permute-start | bytes 1572872 | tf_op jit(solution)/shard_map/ppermute | solution.py:41
  34.2 6.5 %shard_map.138 = (bf16[16,256,512]{2,1,0:T(8,128)(2,1)}, bf16[4,256,256]{2,1,0:T(8,128)(2,1)}) custom-call(s32[32]{0:T(128)} %concatenate.37.meta, bf16[4,256,512]{2,1,0:T(8,128)(2,1)} %bitcast.80, f32[1,512]{1,0:T(1,128)} %bitcast.87, f32[1,512]{1,0:T(1,128)} %bitcast.89), custom_call_target="tpu_custom_call" | custom-call | flops 20971520 | bytes 6291456 | tf_op jit(solution)/shard_map/pallas_call | solution.py:187
  40.7 6.6 %shard_map.139 = (bf16[16,256,512]{2,1,0:T(8,128)(2,1)}, bf16[4,256,256]{2,1,0:T(8,128)(2,1)}) custom-call(s32[32]{0:T(128)} %concatenate.39.meta, bf16[4,256,512]{2,1,0:T(8,128)(2,1)} %bitcast.18.image, f32[1,512]{1,0:T(1,128)} %bitcast.88, f32[1,512]{1,0:T(1,128)} %bitcast.90), custom_call_target="tpu_custom_call" | custom-call | flops 20971520 | bytes 6291456 | tf_op jit(solution)/shard_map/pallas_call | solution.py:187
  47.3 7.9 %collective-permute-done.5.cot3 = bf16[4,256,256]{2,1,0:T(8,128)(2,1)} collective-permute-done((bf16[4,256,256]{2,1,0:T(8,128)(2,1)}, bf16[4,256,256]{2,1,0:T(8,128)(2,1)}, u32[]{:S(2)}, u32[]{:S(2)}) %collective-permute-start.5) | collective-permute-done | bytes 524320 | tf_op jit(solution)/shard_map/ppermute | solution.py:41
  55.7 1.3 copy-done.1
  57.0 5.2 %shard_map.141 = (bf16[4,512,256]{2,1,0:T(8,128)(2,1)}, f32[512,512]{1,0:T(8,128)}) custom-call(s32[32]{0:T(128)} %concatenate.35.meta, bf16[4,256,256]{2,1,0:T(8,128)(2,1)} %get-tuple-element.49.cot0, bf16[4,256,256]{2,1,0:T(8,128)(2,1)} %collective-permute-done.3.cot1, bf16[4,256,256]{2,1,0:T(8,128)(2,1)} %collective-permute-done.4.cot2, ...), custom_call_target="tpu_custom_call" | custom-call | flops 536870912 | bytes 5242880 | tf_op jit(solution)/shard_map/pallas_call | solution.py:520
  62.2 3.8 %collective-permute-start.6 = (f32[512,512]{1,0:T(8,128)}, f32[512,512]{1,0:T(8,128)S(1)}, u32[]{:S(2)}, u32[]{:S(2)}) collective-permute-start(f32[512,512]{1,0:T(8,128)} %get-tuple-element.54.own), channel_id=1, source_target_pairs={{0,32},{1,33},{2,34},{3,35},{4,36},{5,37},{6,38},{7,39},{8,40},{9,... | collective-permute-start | bytes 3145736 | tf_op jit(solution)/shard_map/ppermute | solution.py:41
  66.3 2.2 %collective-permute-done.6.got = f32[512,512]{1,0:T(8,128)S(1)} collective-permute-done((f32[512,512]{1,0:T(8,128)}, f32[512,512]{1,0:T(8,128)S(1)}, u32[]{:S(2)}, u32[]{:S(2)}) %collective-permute-start.6) | collective-permute-done | bytes 1048608 | tf_op jit(solution)/shard_map/ppermute | solution.py:41
  69.7 12.4 %shard_map.142 = (bf16[512,512]{1,0:T(8,128)(2,1)}, bf16[16,18,16,256]{3,2,1,0:T(8,128)(2,1)}) custom-call(f32[512,128]{1,0:T(8,128)} %broadcast_in_dim.69.mask, f32[512,512]{1,0:T(8,128)} %get-tuple-element.54.own, f32[512,512]{1,0:T(8,128)} %copy-done.10, bf16[4,512,256]{2,1,0:T(8,128)(2,1)} %get-tuple-element.55.folded, ...), custom_call_target="tpu_custom_call" | custom-call | flops 5368709120 | bytes 15728640 | tf_op jit(solution)/shard_map/pallas_call | solution.py:539
  82.1 3.9 %all-to-all-start.1 = ((bf16[16,18,16,256]{3,2,1,0:T(8,128)(2,1)}), bf16[16,18,16,256]{3,2,1,0:T(8,128)(2,1)S(1)}, u32[]{:S(2)}, u32[]{:S(2)}) async-start(bf16[16,18,16,256]{3,2,1,0:T(8,128)(2,1)} %get-tuple-element.58), calls=%async_computation.1 | async-start | bytes 4718592 | tf_op jit(solution)/shard_map/all_to_all | solution.py:59
  86.0 12.6 %shard_map.143 = (f32[4,512,256]{2,1,0:T(8,128)}, bf16[4,512,256]{2,1,0:T(8,128)(2,1)}, f32[512,512]{1,0:T(8,128)}) custom-call(f32[512,128]{1,0:T(8,128)} %broadcast_in_dim.69.mask, bf16[16,18,16,256]{3,2,1,0:T(8,128)(2,1)} %bitcast.97, bf16[16,16,16,256]{3,2,1,0:T(8,128)(2,1)} %copy-done.1, bf16[16,256,512]{2,1,0:T(8,128)(2,1)} %get-tuple-element.60.windows_own, ...), custom_call_target="tpu_custom_call" | custom-call | flops 5368709120 | bytes 18874368 | tf_op jit(solution)/shard_map/pallas_call | solution.py:554
  98.9 2.5 %collective-permute-done.7.got = f32[512,512]{1,0:T(8,128)S(1)} collective-permute-done((f32[512,512]{1,0:T(8,128)}, f32[512,512]{1,0:T(8,128)S(1)}, u32[]{:S(2)}, u32[]{:S(2)}) %collective-permute-start.7) | collective-permute-done | bytes 1048608 | tf_op jit(solution)/shard_map/ppermute | solution.py:41
  102.4 8.1 %shard_map.144 = (bf16[4,256,256]{2,1,0:T(8,128)(2,1)}, bf16[4,256,256]{2,1,0:T(8,128)(2,1)}, bf16[4,256,256]{2,1,0:T(8,128)(2,1)}, bf16[4,256,256]{2,1,0:T(8,128)(2,1)}, bf16[16,16,16,256]{3,2,1,0:T(8,128)(2,1)}) custom-call(s32[32]{0:T(128)} %concatenate.35.meta, f32[512,128]{1,0:T(8,128)} %broadcast_in_dim.69.mask, f32[512,512]{1,0:T(8,128)} %get-tuple-element.64.own, ...), custom_call_target="tpu_custom_call" | custom-call | flops 1610612736 | bytes 14680064 | tf_op jit(solution)/shard_map/pallas_call | solution.py:569
  110.5 12.1 %all-to-all-done.1 = bf16[16,18,16,256]{3,2,1,0:T(8,128)(2,1)S(1)} async-done(((bf16[16,18,16,256]{3,2,1,0:T(8,128)(2,1)}), bf16[16,18,16,256]{3,2,1,0:T(8,128)(2,1)S(1)}, u32[]{:S(2)}, u32[]{:S(2)}) %all-to-all-start.1) | async-done | bytes 2359328 | tf_op jit(solution)/shard_map/all_to_all | solution.py:59
  122.7 4.4 %all-to-all-start.2 = ((bf16[16,16,16,256]{3,2,1,0:T(8,128)(2,1)}), bf16[16,16,16,256]{3,2,1,0:T(8,128)(2,1)}, u32[]{:S(2)}, u32[]{:S(2)}) async-start(bf16[16,16,16,256]{3,2,1,0:T(8,128)(2,1)} %get-tuple-element.76), calls=%async_computation.2 | async-start | bytes 4194304 | tf_op jit(solution)/shard_map/all_to_all | solution.py:59
  127.1 1.2 collective-permute-start.8
  128.4 2.9 %collective-permute-start.9 = (bf16[4,256,256]{2,1,0:T(8,128)(2,1)}, bf16[4,256,256]{2,1,0:T(8,128)(2,1)S(1)}, u32[]{:S(2)}, u32[]{:S(2)}) collective-permute-start(bf16[4,256,256]{2,1,0:T(8,128)(2,1)} %get-tuple-element.70), channel_id=1, source_target_pairs={{0,64},{1,65},{2,66},{3,67},{4,68},{5,69},{6,70},{7,71},{8,72},{9,... | collective-permute-start | bytes 1572872 | tf_op jit(solution)/shard_map/ppermute | solution.py:41
  131.9 11.7 %collective-permute-done.9.back2 = bf16[4,256,256]{2,1,0:T(8,128)(2,1)S(1)} collective-permute-done((bf16[4,256,256]{2,1,0:T(8,128)(2,1)}, bf16[4,256,256]{2,1,0:T(8,128)(2,1)S(1)}, u32[]{:S(2)}, u32[]{:S(2)}) %collective-permute-start.9) | collective-permute-done | bytes 524320 | tf_op jit(solution)/shard_map/ppermute | solution.py:41
  143.7 11.4 %collective-permute-done.10.back3 = bf16[4,256,256]{2,1,0:T(8,128)(2,1)} collective-permute-done((bf16[4,256,256]{2,1,0:T(8,128)(2,1)}, bf16[4,256,256]{2,1,0:T(8,128)(2,1)}, u32[]{:S(2)}, u32[]{:S(2)}) %collective-permute-start.10) | collective-permute-done | bytes 524320 | tf_op jit(solution)/shard_map/ppermute | solution.py:41
  155.1 2.8 %collective-permute-start.13 = (bf16[9,16,256]{2,1,0:T(8,128)(2,1)S(1)}, bf16[9,16,256]{2,1,0:T(8,128)(2,1)S(1)}, u32[]{:S(2)}, u32[]{:S(2)}) collective-permute-start(bf16[9,16,256]{2,1,0:T(8,128)(2,1)S(1)} %get-tuple-element.89), channel_id=1, source_target_pairs={{0,68},{1,69},{2,70},{3,71},{4,64},{5,65},{6,66},{7,67},{8,76},{9,... | collective-permute-start | bytes 221192 | tf_op jit(solution)/shard_map/ppermute | solution.py:41
  158.6 2.3 %collective-permute-done.13 = bf16[9,16,256]{2,1,0:T(8,128)(2,1)S(1)} collective-permute-done((bf16[9,16,256]{2,1,0:T(8,128)(2,1)S(1)}, bf16[9,16,256]{2,1,0:T(8,128)(2,1)S(1)}, u32[]{:S(2)}, u32[]{:S(2)}) %collective-permute-start.13) | collective-permute-done | bytes 73760 | tf_op jit(solution)/shard_map/ppermute | solution.py:41
  160.9 1.7 collective-permute-done.12
  162.6 2.3 %collective-permute-start.14 = (f32[9,16,256]{2,1,0:T(8,128)S(1)}, f32[9,16,256]{2,1,0:T(8,128)S(1)}, u32[]{:S(2)}, u32[]{:S(2)}) collective-permute-start(f32[9,16,256]{2,1,0:T(8,128)S(1)} %fusion.4), channel_id=1, source_target_pairs={{0,32},{1,33},{2,34},{3,35},{4,36},{5,37},{6,38},{7,39},{8,40},{9,... | collective-permute-start | bytes 442376 | tf_op jit(solution)/shard_map/ppermute | solution.py:41
  167.5 1.9 %convert_reduce_fusion.1 = f32[16,16,256]{2,1,0:T(8,128)S(1)} fusion(bf16[16,16,16,256]{3,2,1,0:T(8,128)(2,1)} %all-to-all-done.2), kind=kLoop, calls=%fused_computation.1 | loop fusion | flops 2031616 | bytes 2359296 | tf_op jit(solution)/shard_map/reduce_sum | solution.py:598
  171.4 1.5 collective-permute-start.15
  172.9 3.6 %shard_map.145 = f32[8,256,512]{2,1,0:T(8,128)} custom-call(s32[1]{0:T(128)} %bitcast.number, bf16[4,256,256]{2,1,0:T(8,128)(2,1)} %get-tuple-element.72.back0, bf16[4,256,256]{2,1,0:T(8,128)(2,1)} %copy-done.4, bf16[4,256,256]{2,1,0:T(8,128)(2,1)} %copy-done.5, bf16[4,256,256]{2,1,0:T(8,128)(2,1)} %collective-permute-done.10.back3), custom_call_target="tpu_custom_call" | custom-call | bytes 6291456 | tf_op jit(solution)/shard_map/pallas_call | solution.py:607
  177.4 1.5 collective-permute-start.18
  (100 shorter events, 19.6 us)
Async XLA Ops:
  7.2 1.8 copy-start
  7.2 78.8 %all-gather.3.cloned.1.call-start = ((), (), s32[]{:S(2)}) async-start(), calls=%async_computation.3 | async-start | bytes 2506752 | tf_op jit(solution)/shard_map/all_gather | solution.py:483
  9.1 5.9 %collective-permute-start.2 = (bf16[21,16,256]{2,1,0:T(8,128)(2,1)S(1)}, bf16[21,16,256]{2,1,0:T(8,128)(2,1)S(1)}, u32[]{:S(2)}, u32[]{:S(2)}) collective-permute-start(bf16[21,16,256]{2,1,0:T(8,128)(2,1)S(1)} %pad_maximum_fusion.1), channel_id=1, source_target_pairs={{0,4},{1,5},{2,6},{3,7},{4,0},{5,1},{6,2},{7,3},{8,12},{9,13},{10,... | collective-permute-start | bytes 516104 | tf_op jit(solution)/shard_map/ppermute | solution.py:41
  17.4 8.0 %copy-start.6 = (s32[4,1]{0,1:T(1,128)S(1)}, s32[4,1]{0,1:T(1,128)}, u32[]{:S(2)}) copy-start(s32[4,1]{0,1:T(1,128)} %param.12) | copy-start | bytes 52
  17.4 8.0 %copy-start.7 = (s32[4]{0:T(128)S(1)}, s32[4]{0:T(128)}, u32[]{:S(2)}) copy-start(s32[4]{0:T(128)} %param.13) | copy-start | bytes 52
  17.4 10.0 %copy-start.3 = (bf16[4,16,16,512]{3,2,1,0:T(8,128)(2,1)S(1)}, bf16[4,16,16,512]{3,2,1,0:T(8,128)(2,1)}, u32[]{:S(2)}) copy-start(bf16[4,16,16,512]{3,2,1,0:T(8,128)(2,1)} %param.11) | copy-start | bytes 3145732
  17.4 14.6 %copy-start.8 = (s32[8]{0:T(128)S(1)}, s32[8]{0:T(128)}, u32[]{:S(2)}) copy-start(s32[8]{0:T(128)} %param.14) | copy-start | bytes 100
  17.4 14.6 %copy-start.9 = (s32[8]{0:T(128)S(1)}, s32[8]{0:T(128)}, u32[]{:S(2)}) copy-start(s32[8]{0:T(128)} %param.15) | copy-start | bytes 100
  17.4 38.2 %all-to-all-start = ((bf16[16,16,16,256]{3,2,1,0:T(8,128)(2,1)}), bf16[16,16,16,256]{3,2,1,0:T(8,128)(2,1)S(1)}, u32[]{:S(2)}, u32[]{:S(2)}) async-start(bf16[16,16,16,256]{3,2,1,0:T(8,128)(2,1)} %broadcast_in_dim.72), calls=%async_computation | async-start | bytes 4194304 | tf_op jit(solution)/shard_map/all_to_all | solution.py:59
  25.5 2.7 %collective-permute-start = (s32[4,2]{0,1:T(2,128)S(1)}, s32[4,2]{0,1:T(2,128)S(1)}, u32[]{:S(2)}, u32[]{:S(2)}) collective-permute-start(s32[4,2]{0,1:T(2,128)S(1)} %pad_add_fusion.2), channel_id=1, source_target_pairs={{0,32},{1,33},{2,34},{3,35},{4,36},{5,37},{6,38},{7,39},{8,40},{9,... | collective-permute-start | bytes 104 | tf_op jit(solution)/shard_map/ppermute | solution.py:41
  27.4 13.3 %collective-permute-start.1 = (bf16[4,16,16,512]{3,2,1,0:T(8,128)(2,1)S(1)}, bf16[4,16,16,512]{3,2,1,0:T(8,128)(2,1)}, u32[]{:S(2)}, u32[]{:S(2)}) collective-permute-start(bf16[4,16,16,512]{3,2,1,0:T(8,128)(2,1)S(1)} %copy-done.3), channel_id=1, source_target_pairs={{0,32},{1,33},{2,34},{3,35},{4,36},{5,37},{6,38},{7,39},{8,40},{9,... | collective-permute-start | bytes 3145736 | tf_op jit(solution)/shard_map/ppermute | solution.py:41
  28.2 19.1 %collective-permute-start.3 = (bf16[4,256,256]{2,1,0:T(8,128)(2,1)}, bf16[4,256,256]{2,1,0:T(8,128)(2,1)}, u32[]{:S(2)}, u32[]{:S(2)}) collective-permute-start(bf16[4,256,256]{2,1,0:T(8,128)(2,1)} %get-tuple-element.50), channel_id=1, source_target_pairs={{0,32},{1,33},{2,34},{3,35},{4,36},{5,37},{6,38},{7,39},{8,40},{9,... | collective-permute-start | bytes 1572872 | tf_op jit(solution)/shard_map/ppermute | solution.py:41
  28.5 18.8 %collective-permute-start.4 = (bf16[4,256,256]{2,1,0:T(8,128)(2,1)}, bf16[4,256,256]{2,1,0:T(8,128)(2,1)}, u32[]{:S(2)}, u32[]{:S(2)}) collective-permute-start(bf16[4,256,256]{2,1,0:T(8,128)(2,1)} %get-tuple-element.51), channel_id=1, source_target_pairs={{0,64},{1,65},{2,66},{3,67},{4,68},{5,69},{6,70},{7,71},{8,72},{9,... | collective-permute-start | bytes 1572872 | tf_op jit(solution)/shard_map/ppermute | solution.py:41
  31.4 23.8 %collective-permute-start.5 = (bf16[4,256,256]{2,1,0:T(8,128)(2,1)}, bf16[4,256,256]{2,1,0:T(8,128)(2,1)}, u32[]{:S(2)}, u32[]{:S(2)}) collective-permute-start(bf16[4,256,256]{2,1,0:T(8,128)(2,1)} %get-tuple-element.52), channel_id=1, source_target_pairs={{0,96},{1,97},{2,98},{3,99},{4,100},{5,101},{6,102},{7,103},{8,104... | collective-permute-start | bytes 1572872 | tf_op jit(solution)/shard_map/ppermute | solution.py:41
  55.7 1.3 copy-start.1
  62.2 6.3 %collective-permute-start.6 = (f32[512,512]{1,0:T(8,128)}, f32[512,512]{1,0:T(8,128)S(1)}, u32[]{:S(2)}, u32[]{:S(2)}) collective-permute-start(f32[512,512]{1,0:T(8,128)} %get-tuple-element.54.own), channel_id=1, source_target_pairs={{0,32},{1,33},{2,34},{3,35},{4,36},{5,37},{6,38},{7,39},{8,40},{9,... | collective-permute-start | bytes 3145736 | tf_op jit(solution)/shard_map/ppermute | solution.py:41
  82.1 40.6 %all-to-all-start.1 = ((bf16[16,18,16,256]{3,2,1,0:T(8,128)(2,1)}), bf16[16,18,16,256]{3,2,1,0:T(8,128)(2,1)S(1)}, u32[]{:S(2)}, u32[]{:S(2)}) async-start(bf16[16,18,16,256]{3,2,1,0:T(8,128)(2,1)} %get-tuple-element.58), calls=%async_computation.1 | async-start | bytes 4718592 | tf_op jit(solution)/shard_map/all_to_all | solution.py:59
  98.6 2.9 %collective-permute-start.7 = (f32[512,512]{1,0:T(8,128)}, f32[512,512]{1,0:T(8,128)S(1)}, u32[]{:S(2)}, u32[]{:S(2)}) collective-permute-start(f32[512,512]{1,0:T(8,128)} %get-tuple-element.64.own), channel_id=1, source_target_pairs={{0,32},{1,33},{2,34},{3,35},{4,36},{5,37},{6,38},{7,39},{8,40},{9,... | collective-permute-start | bytes 3145736 | tf_op jit(solution)/shard_map/ppermute | solution.py:41
  122.7 44.8 %all-to-all-start.2 = ((bf16[16,16,16,256]{3,2,1,0:T(8,128)(2,1)}), bf16[16,16,16,256]{3,2,1,0:T(8,128)(2,1)}, u32[]{:S(2)}, u32[]{:S(2)}) async-start(bf16[16,16,16,256]{3,2,1,0:T(8,128)(2,1)} %get-tuple-element.76), calls=%async_computation.2 | async-start | bytes 4194304 | tf_op jit(solution)/shard_map/all_to_all | solution.py:59
  127.1 4.8 %collective-permute-start.8 = (bf16[4,256,256]{2,1,0:T(8,128)(2,1)}, bf16[4,256,256]{2,1,0:T(8,128)(2,1)S(1)}, u32[]{:S(2)}, u32[]{:S(2)}) collective-permute-start(bf16[4,256,256]{2,1,0:T(8,128)(2,1)} %get-tuple-element.69), channel_id=1, source_target_pairs={{0,32},{1,33},{2,34},{3,35},{4,36},{5,37},{6,38},{7,39},{8,40},{9,... | collective-permute-start | bytes 1572872 | tf_op jit(solution)/shard_map/ppermute | solution.py:41
  128.4 15.3 %collective-permute-start.9 = (bf16[4,256,256]{2,1,0:T(8,128)(2,1)}, bf16[4,256,256]{2,1,0:T(8,128)(2,1)S(1)}, u32[]{:S(2)}, u32[]{:S(2)}) collective-permute-start(bf16[4,256,256]{2,1,0:T(8,128)(2,1)} %get-tuple-element.70), channel_id=1, source_target_pairs={{0,64},{1,65},{2,66},{3,67},{4,68},{5,69},{6,70},{7,71},{8,72},{9,... | collective-permute-start | bytes 1572872 | tf_op jit(solution)/shard_map/ppermute | solution.py:41
  131.3 23.8 %collective-permute-start.10 = (bf16[4,256,256]{2,1,0:T(8,128)(2,1)}, bf16[4,256,256]{2,1,0:T(8,128)(2,1)}, u32[]{:S(2)}, u32[]{:S(2)}) collective-permute-start(bf16[4,256,256]{2,1,0:T(8,128)(2,1)} %get-tuple-element.71), channel_id=1, source_target_pairs={{0,96},{1,97},{2,98},{3,99},{4,100},{5,101},{6,102},{7,103},{8,104... | collective-permute-start | bytes 1572872 | tf_op jit(solution)/shard_map/ppermute | solution.py:41
  131.9 37.5 %copy-start.4 = (bf16[4,256,256]{2,1,0:T(8,128)(2,1)}, bf16[4,256,256]{2,1,0:T(8,128)(2,1)S(1)}, u32[]{:S(2)}) copy-start(bf16[4,256,256]{2,1,0:T(8,128)(2,1)S(1)} %collective-permute-done.8.back1) | copy-start | bytes 1572868
  143.7 25.8 %copy-start.5 = (bf16[4,256,256]{2,1,0:T(8,128)(2,1)}, bf16[4,256,256]{2,1,0:T(8,128)(2,1)S(1)}, u32[]{:S(2)}) copy-start(bf16[4,256,256]{2,1,0:T(8,128)(2,1)S(1)} %collective-permute-done.9.back2) | copy-start | bytes 1572868
  155.1 5.8 %collective-permute-start.13 = (bf16[9,16,256]{2,1,0:T(8,128)(2,1)S(1)}, bf16[9,16,256]{2,1,0:T(8,128)(2,1)S(1)}, u32[]{:S(2)}, u32[]{:S(2)}) collective-permute-start(bf16[9,16,256]{2,1,0:T(8,128)(2,1)S(1)} %get-tuple-element.89), channel_id=1, source_target_pairs={{0,68},{1,69},{2,70},{3,71},{4,64},{5,65},{6,66},{7,67},{8,76},{9,... | collective-permute-start | bytes 221192 | tf_op jit(solution)/shard_map/ppermute | solution.py:41
  157.9 4.7 %collective-permute-start.12 = (bf16[9,16,256]{2,1,0:T(8,128)(2,1)S(1)}, bf16[9,16,256]{2,1,0:T(8,128)(2,1)S(1)}, u32[]{:S(2)}, u32[]{:S(2)}) collective-permute-start(bf16[9,16,256]{2,1,0:T(8,128)(2,1)S(1)} %get-tuple-element.88), channel_id=1, source_target_pairs={{0,64},{1,65},{2,66},{3,67},{4,68},{5,69},{6,70},{7,71},{8,72},{9,... | collective-permute-start | bytes 221192 | tf_op jit(solution)/shard_map/ppermute | solution.py:41
  158.2 4.4 %collective-permute-start.11 = (bf16[9,16,256]{2,1,0:T(8,128)(2,1)S(1)}, bf16[9,16,256]{2,1,0:T(8,128)(2,1)S(1)}, u32[]{:S(2)}, u32[]{:S(2)}) collective-permute-start(bf16[9,16,256]{2,1,0:T(8,128)(2,1)S(1)} %get-tuple-element.89), channel_id=1, source_target_pairs={{0,4},{1,5},{2,6},{3,7},{4,0},{5,1},{6,2},{7,3},{8,12},{9,13},{10,... | collective-permute-start | bytes 221192 | tf_op jit(solution)/shard_map/ppermute | solution.py:41
  162.6 3.4 %collective-permute-start.14 = (f32[9,16,256]{2,1,0:T(8,128)S(1)}, f32[9,16,256]{2,1,0:T(8,128)S(1)}, u32[]{:S(2)}, u32[]{:S(2)}) collective-permute-start(f32[9,16,256]{2,1,0:T(8,128)S(1)} %fusion.4), channel_id=1, source_target_pairs={{0,32},{1,33},{2,34},{3,35},{4,36},{5,37},{6,38},{7,39},{8,40},{9,... | collective-permute-start | bytes 442376 | tf_op jit(solution)/shard_map/ppermute | solution.py:41
  169.6 7.0 %collective-permute-start.17 = (bf16[12,16,256]{2,1,0:T(8,128)(2,1)S(1)}, bf16[12,16,256]{2,1,0:T(8,128)(2,1)S(1)}, u32[]{:S(2)}, u32[]{:S(2)}) collective-permute-start(bf16[12,16,256]{2,1,0:T(8,128)(2,1)S(1)} %get-tuple-element.85), channel_id=1, source_target_pairs={{0,68},{1,69},{2,70},{3,71},{4,64},{5,65},{6,66},{7,67},{8,76},{9,... | collective-permute-start | bytes 294920 | tf_op jit(solution)/shard_map/ppermute | solution.py:41
  170.7 5.8 %collective-permute-start.16 = (bf16[12,16,256]{2,1,0:T(8,128)(2,1)S(1)}, bf16[12,16,256]{2,1,0:T(8,128)(2,1)S(1)}, u32[]{:S(2)}, u32[]{:S(2)}) collective-permute-start(bf16[12,16,256]{2,1,0:T(8,128)(2,1)S(1)} %get-tuple-element.84), channel_id=1, source_target_pairs={{0,64},{1,65},{2,66},{3,67},{4,68},{5,69},{6,70},{7,71},{8,72},{9,... | collective-permute-start | bytes 294920 | tf_op jit(solution)/shard_map/ppermute | solution.py:41
  171.4 5.9 %collective-permute-start.15 = (bf16[12,16,256]{2,1,0:T(8,128)(2,1)S(1)}, bf16[12,16,256]{2,1,0:T(8,128)(2,1)S(1)}, u32[]{:S(2)}, u32[]{:S(2)}) collective-permute-start(bf16[12,16,256]{2,1,0:T(8,128)(2,1)S(1)} %get-tuple-element.85), channel_id=1, source_target_pairs={{0,4},{1,5},{2,6},{3,7},{4,0},{5,1},{6,2},{7,3},{8,12},{9,13},{10,... | collective-permute-start | bytes 294920 | tf_op jit(solution)/shard_map/ppermute | solution.py:41
  177.4 2.6 %collective-permute-start.18 = (f32[12,16,256]{2,1,0:T(8,128)S(1)}, f32[12,16,256]{2,1,0:T(8,128)S(1)}, u32[]{:S(2)}, u32[]{:S(2)}) collective-permute-start(f32[12,16,256]{2,1,0:T(8,128)S(1)} %fusion.2), channel_id=1, source_target_pairs={{0,32},{1,33},{2,34},{3,35},{4,36},{5,37},{6,38},{7,39},{8,40},{9,... | collective-permute-start | bytes 589832 | tf_op jit(solution)/shard_map/ppermute | solution.py:41
  (2 other events, 2.1 us)
Sparse Core Ops, SparseCore 0:
  15.9 62.1 all-gather.2

commit v2 on v1

--- a/solution.py
+++ b/solution.py
@@ -14,6 +14,7 @@
 F32 = jnp.float32
 I32 = jnp.int32
 AXES = ("dp", "fsdp")
+SENT = 5
 VMEM_BYTES = 56 * 1024 * 1024
 
 
@@ -279,7 +280,19 @@
 
 
 def grad_conv_kernel(
-    loss_scale, mask, own, got, folded, pieces, windows_own, windows_pair, glow, grads, down, turned
+    loss_scale,
+    mask,
+    own,
+    got,
+    folded,
+    pieces,
+    windows_own,
+    windows_pair,
+    glow,
+    grads,
+    rest,
+    down,
+    turned,
 ):
     half = folded.shape[2]
     rows = grads.shape[2]
@@ -297,10 +310,14 @@
             for columns, windows in ((slice(0, middle), windows_own), (slice(middle, None), windows_pair)):
                 term = dot(turned[k, :, columns], windows[v], 1, 0)
                 total = term if total is None else total + term
-        total = total.T.astype(BF)
+        total = total.T
         for f in range(32):
             z, y, x = f // 8, f // 4 % 2, f % 4
-            grads[z * 4 + x, y * 9 + t] = total[f * rows : (f + 1) * rows, :]
+            piece = total[f * rows : (f + 1) * rows, :]
+            if t < SENT:
+                grads[z * 4 + x, y * SENT + t] = piece.astype(BF)
+            else:
+                rest[z * 4 + x, y * (9 - SENT) + t - SENT] = piece
 
 
 def conv_kernel(
@@ -536,19 +553,23 @@
     )(ready, *arrived, up_down)
     glow_got = send(glow_part, "c")
 
-    glow, conv_grads = kernel_call(
+    glow, conv_grads, conv_rest = kernel_call(
         functools.partial(grad_conv_kernel, loss_scale),
         (
             jax.ShapeDtypeStruct((low_rows, channels), BF),
-            jax.ShapeDtypeStruct((16, 18, rows, half), BF),
+            jax.ShapeDtypeStruct((16, 2 * SENT, rows, half), BF),
+            jax.ShapeDtypeStruct((16, 18 - 2 * SENT, rows, half), F32),
         ),
         flops=80 * low_rows * channels * half,
         moved_bytes=15 << 20,
         scratch=(pltpu.VMEM((4, half, channels), BF), pltpu.VMEM((4, half, low_rows), BF)),
         in_specs=[WHOLE] * 7,
-        out_specs=(WHOLE, WHOLE),
+        out_specs=(WHOLE,) * 3,
     )(mask, glow_part, glow_got, folded, up_down, windows_own, windows_pair)
     conv_grads = over_plane(conv_grads)
+    conv_rest = lax.psum_scatter(
+        conv_rest, "fsdp", scatter_dimension=0, axis_index_groups=PLANES, tiled=True
+    )
     glow, windows_own, windows_pair = lax.optimization_barrier((glow, windows_own, windows_pair))
 
     wide, skip, low_part = kernel_call(
@@ -587,21 +608,23 @@
     returned = over_dp(returning)
     grads = over_plane(grads)
 
-    conv_sum = jnp.sum(conv_grads.astype(F32), axis=0).reshape(2, 9, rows, half)
-    conv_sum, returned = lax.optimization_barrier((conv_sum, returned))
-
-    def by_core(own, pair):
-        return jnp.where(core == 0, jnp.stack([own, pair]), jnp.stack([pair, own]))
-
-    out_conv = by_core(*over_column(conv_sum, y)).transpose(2, 1, 0, 3)
-    out_conv = out_conv.reshape(rows, 9, channels)
+    conv_sum = jnp.sum(conv_grads.astype(F32), axis=0).reshape(2, SENT, rows, half)
+    conv_rest = conv_rest.reshape(2, 9 - SENT, rows, half)
     grads_sum = jnp.sum(grads.astype(F32), axis=0)
     up_sum, down_sum = grads_sum[:8].reshape(2, 4, rows, half), grads_sum[8:]
-    shares = jnp.concatenate([up_sum, jnp.broadcast_to(down_sum, (2, *down_sum.shape))], axis=1)
-    shares, out_conv = lax.optimization_barrier((shares, out_conv))
+    down_sum = jnp.broadcast_to(down_sum, (2, *down_sum.shape))
+    shares = jnp.concatenate([conv_sum, conv_rest, up_sum, down_sum], axis=1)
+    shares, returned = lax.optimization_barrier((shares, returned))
     own, pair = over_column(shares, y)
-    out_up = by_core(own[:4], pair[:4]).transpose(2, 1, 0, 3).reshape(rows, 4 * channels)
-    out_down = jnp.where(y == core, own[4:], pair[4:])
+
+    def by_core(first, last):
+        parts = (own[first:last], pair[first:last])
+        both = jnp.where(core == 0, jnp.stack(parts), jnp.stack(parts[::-1]))
+        return both.transpose(2, 1, 0, 3)
+
+    out_conv = by_core(0, 9).reshape(rows, 9, channels)
+    out_up = by_core(9, 13).reshape(rows, 4 * channels)
+    out_down = jnp.where(y == core, own[13:], pair[13:])
     out_down = out_down.reshape(2, 4 * rows, half).transpose(1, 0, 2).reshape(4 * rows, channels)
 
     block_out = kernel_call(

time: 189 us -> 206 us (1.090)
  waiting for transfers between devices: 56.4 us -> 75 us
    ppermute x19 -> x15, waiting for transfers between devices: 43.8 us -> 17.9 us  [send(): return lax.ppermute(value, AXES, STEP[move])]
    unnamed x1 -> x3, waiting for transfers between devices: 0.02 us -> 25.9 us
    all_to_all x3, waiting for transfers between devices: 12.6 us -> 31.1 us  [over_plane(): lax.all_to_all(blocks, 'fsdp', split_axis=0, concat_axis=0, axis_index_gr...]
    ppermute x19 -> x15, starting transfers between devices: 27.2 us -> 24 us  [send(): return lax.ppermute(value, AXES, STEP[move])]
    all_to_all x3, starting transfers between devices: 16.3 us -> 18.6 us  [over_plane(): lax.all_to_all(blocks, 'fsdp', split_axis=0, concat_axis=0, axis_index_gr...]
  transfers between devices with their start and end apart: 23 -> 20, of which waited for: 14 -> 11; matrix products, arithmetic and copies ran while one was open for 4% -> 4% of each run, Pallas kernels for 31% -> 28%
where the time goes in v2:
time: 206 us; the launch traced here: 205 us
  waiting for transfers between devices  75 us (36%)
  Pallas kernels  58 us (28%)
  starting transfers between devices  42.6 us (21%)
  between operations  14.4 us (7%)
  local copies, waits for them, and re-layouts  11.3 us (5%)
  other arithmetic  3.84 us (2%)
    all_to_all x3, waiting for transfers between devices, over_plane(): lax.all_to_all(blocks, 'fsdp', split_axis=0, concat_axis=0, axis_index_gr...  31.1 us
    unnamed x3, waiting for transfers between devices  25.9 us
    ppermute x15, starting transfers between devices, send(): return lax.ppermute(value, AXES, STEP[move])  24 us
    all_to_all x3, starting transfers between devices, over_plane(): lax.all_to_all(blocks, 'fsdp', split_axis=0, concat_axis=0, axis_index_gr...  18.6 us
    ppermute x15, waiting for transfers between devices, send(): return lax.ppermute(value, AXES, STEP[move])  17.9 us
    pallas_call x2, Pallas kernels, normed_windows(): kernel_call(functools.partial(norm_kernel, extent), (jax.ShapeDtypeStruct...  13 us
    pallas_call x1, Pallas kernels, per_device(): kernel_call(conv_kernel, (jax.ShapeDtypeStruct((4, low_rows, half), F32),...  12.6 us
    pallas_call x1, Pallas kernels, per_device(): kernel_call(functools.partial(grad_conv_kernel, loss_scale), (jax.ShapeDt...  12.4 us
  transfers between devices with their start and end apart: 20, of which 11 were waited for; matrix products, arithmetic and copies ran while one was open for 4% of the time, Pallas kernels for 28%

profile of v2, /device:TPU:1, one launch (start us, length us, event | category | flops | bytes accessed | tf_op | source)
XLA Modules:
  0.0 205.2 jit_solution(15329019214792356192)
XLA Ops:
  9.1 2.2 %collective-permute-start.2 = (bf16[21,16,256]{2,1,0:T(8,128)(2,1)S(1)}, bf16[21,16,256]{2,1,0:T(8,128)(2,1)S(1)}, u32[]{:S(2)}, u32[]{:S(2)}) collective-permute-start(bf16[21,16,256]{2,1,0:T(8,128)(2,1)S(1)} %pad_maximum_fusion.1), channel_id=1, source_target_pairs={{0,4},{1,5},{2,6},{3,7},{4,0},{5,1},{6,2},{7,3},{8,12},{9,13},{10,... | collective-permute-start | bytes 516104 | tf_op jit(solution)/shard_map/ppermute | solution.py:42
  11.3 3.0 %shard_map.140 = (bf16[4,256,256]{2,1,0:T(8,128)(2,1)}, bf16[4,256,256]{2,1,0:T(8,128)(2,1)}, bf16[4,256,256]{2,1,0:T(8,128)(2,1)}, bf16[4,256,256]{2,1,0:T(8,128)(2,1)}) custom-call(s32[1]{0:T(128)} %bitcast.number, bf16[8,256,512]{2,1,0:T(8,128)(2,1)} %bitcast.74), custom_call_target="tpu_custom_call" | custom-call | bytes 4194304 | tf_op jit(solution)/shard_map/pallas_call | solution.py:484
  15.8 1.6 broadcast_in_dim.72
  17.4 8.0 %all-to-all-start = ((bf16[16,16,16,256]{3,2,1,0:T(8,128)(2,1)}), bf16[16,16,16,256]{3,2,1,0:T(8,128)(2,1)S(1)}, u32[]{:S(2)}, u32[]{:S(2)}) async-start(bf16[16,16,16,256]{3,2,1,0:T(8,128)(2,1)} %broadcast_in_dim.72), calls=%async_computation | async-start | bytes 4194304 | tf_op jit(solution)/shard_map/all_to_all | solution.py:60
  25.5 1.9 collective-permute-start
  28.6 2.9 %collective-permute-start.4 = (bf16[4,256,256]{2,1,0:T(8,128)(2,1)}, bf16[4,256,256]{2,1,0:T(8,128)(2,1)}, u32[]{:S(2)}, u32[]{:S(2)}) collective-permute-start(bf16[4,256,256]{2,1,0:T(8,128)(2,1)} %get-tuple-element.50), channel_id=1, source_target_pairs={{0,64},{1,65},{2,66},{3,67},{4,68},{5,69},{6,70},{7,71},{8,72},{9,... | collective-permute-start | bytes 1572872 | tf_op jit(solution)/shard_map/ppermute | solution.py:42
  34.3 6.5 %shard_map.138 = (bf16[16,256,512]{2,1,0:T(8,128)(2,1)}, bf16[4,256,256]{2,1,0:T(8,128)(2,1)}) custom-call(s32[32]{0:T(128)} %concatenate.37.meta, bf16[4,256,512]{2,1,0:T(8,128)(2,1)} %bitcast.75, f32[1,512]{1,0:T(1,128)} %bitcast.85, f32[1,512]{1,0:T(1,128)} %bitcast.87), custom_call_target="tpu_custom_call" | custom-call | flops 20971520 | bytes 6291456 | tf_op jit(solution)/shard_map/pallas_call | solution.py:188
  40.8 6.5 %shard_map.139 = (bf16[16,256,512]{2,1,0:T(8,128)(2,1)}, bf16[4,256,256]{2,1,0:T(8,128)(2,1)}) custom-call(s32[32]{0:T(128)} %concatenate.39.meta, bf16[4,256,512]{2,1,0:T(8,128)(2,1)} %bitcast.18.image, f32[1,512]{1,0:T(1,128)} %bitcast.86, f32[1,512]{1,0:T(1,128)} %bitcast.88), custom_call_target="tpu_custom_call" | custom-call | flops 20971520 | bytes 6291456 | tf_op jit(solution)/shard_map/pallas_call | solution.py:188
  47.3 8.0 %collective-permute-done.5.cot3 = bf16[4,256,256]{2,1,0:T(8,128)(2,1)} collective-permute-done((bf16[4,256,256]{2,1,0:T(8,128)(2,1)}, bf16[4,256,256]{2,1,0:T(8,128)(2,1)}, u32[]{:S(2)}, u32[]{:S(2)}) %collective-permute-start.5) | collective-permute-done | bytes 524320 | tf_op jit(solution)/shard_map/ppermute | solution.py:42
  55.7 1.4 copy-done.1
  57.0 5.2 %shard_map.141 = (bf16[4,512,256]{2,1,0:T(8,128)(2,1)}, f32[512,512]{1,0:T(8,128)}) custom-call(s32[32]{0:T(128)} %concatenate.35.meta, bf16[4,256,256]{2,1,0:T(8,128)(2,1)} %get-tuple-element.48.cot0, bf16[4,256,256]{2,1,0:T(8,128)(2,1)} %collective-permute-done.3.cot1, bf16[4,256,256]{2,1,0:T(8,128)(2,1)} %collective-permute-done.4.cot2, ...), custom_call_target="tpu_custom_call" | custom-call | flops 536870912 | bytes 5242880 | tf_op jit(solution)/shard_map/pallas_call | solution.py:537
  62.3 3.8 %collective-permute-start.6 = (f32[512,512]{1,0:T(8,128)}, f32[512,512]{1,0:T(8,128)S(1)}, u32[]{:S(2)}, u32[]{:S(2)}) collective-permute-start(f32[512,512]{1,0:T(8,128)} %get-tuple-element.53.own), channel_id=1, source_target_pairs={{0,32},{1,33},{2,34},{3,35},{4,36},{5,37},{6,38},{7,39},{8,40},{9,... | collective-permute-start | bytes 3145736 | tf_op jit(solution)/shard_map/ppermute | solution.py:42
  66.4 2.2 %collective-permute-done.6.got = f32[512,512]{1,0:T(8,128)S(1)} collective-permute-done((f32[512,512]{1,0:T(8,128)}, f32[512,512]{1,0:T(8,128)S(1)}, u32[]{:S(2)}, u32[]{:S(2)}) %collective-permute-start.6) | collective-permute-done | bytes 1048608 | tf_op jit(solution)/shard_map/ppermute | solution.py:42
  68.6 1.0 broadcast_in_dim.69.mask
  69.8 12.4 %shard_map.142 = (bf16[512,512]{1,0:T(8,128)(2,1)}, bf16[16,10,16,256]{3,2,1,0:T(8,128)(2,1)}, f32[16,8,16,256]{3,2,1,0:T(8,128)}) custom-call(f32[512,128]{1,0:T(8,128)} %broadcast_in_dim.69.mask, f32[512,512]{1,0:T(8,128)} %get-tuple-element.53.own, f32[512,512]{1,0:T(8,128)} %copy-done.9, bf16[4,512,256]{2,1,0:T(8,128)(2,1)} %get-tuple-element.54.folded, ...), custom_call_target="tpu_custom_call" | custom-call | flops 5368709120 | bytes 15728640 | tf_op jit(solution)/shard_map/pallas_call | solution.py:556
  82.2 3.9 %all-to-all-start.1 = ((bf16[16,10,16,256]{3,2,1,0:T(8,128)(2,1)}), bf16[16,10,16,256]{3,2,1,0:T(8,128)(2,1)S(1)}, u32[]{:S(2)}, u32[]{:S(2)}) async-start(bf16[16,10,16,256]{3,2,1,0:T(8,128)(2,1)} %get-tuple-element.57), calls=%async_computation.1 | async-start | bytes 2621440 | tf_op jit(solution)/shard_map/all_to_all | solution.py:60
  86.1 12.6 %shard_map.143 = (f32[4,512,256]{2,1,0:T(8,128)}, bf16[4,512,256]{2,1,0:T(8,128)(2,1)}, f32[512,512]{1,0:T(8,128)}) custom-call(f32[512,128]{1,0:T(8,128)} %broadcast_in_dim.69.mask, bf16[16,18,16,256]{3,2,1,0:T(8,128)(2,1)} %bitcast.95, bf16[16,16,16,256]{3,2,1,0:T(8,128)(2,1)} %copy-done.1, bf16[16,256,512]{2,1,0:T(8,128)(2,1)} %get-tuple-element.60.windows_own, ...), custom_call_target="tpu_custom_call" | custom-call | flops 5368709120 | bytes 18874368 | tf_op jit(solution)/shard_map/pallas_call | solution.py:575
  99.1 2.5 %collective-permute-done.7.got = f32[512,512]{1,0:T(8,128)S(1)} collective-permute-done((f32[512,512]{1,0:T(8,128)}, f32[512,512]{1,0:T(8,128)S(1)}, u32[]{:S(2)}, u32[]{:S(2)}) %collective-permute-start.7) | collective-permute-done | bytes 1048608 | tf_op jit(solution)/shard_map/ppermute | solution.py:42
  101.6 1.0 copy-done.2
  102.6 8.1 %shard_map.144 = (bf16[4,256,256]{2,1,0:T(8,128)(2,1)}, bf16[4,256,256]{2,1,0:T(8,128)(2,1)}, bf16[4,256,256]{2,1,0:T(8,128)(2,1)}, bf16[4,256,256]{2,1,0:T(8,128)(2,1)}, bf16[16,16,16,256]{3,2,1,0:T(8,128)(2,1)}) custom-call(s32[32]{0:T(128)} %concatenate.35.meta, f32[512,128]{1,0:T(8,128)} %broadcast_in_dim.69.mask, f32[512,512]{1,0:T(8,128)} %get-tuple-element.64.own, ...), custom_call_target="tpu_custom_call" | custom-call | flops 1610612736 | bytes 14680064 | tf_op jit(solution)/shard_map/pallas_call | solution.py:590
  110.7 6.7 %all-to-all-start.2 = ((bf16[16,16,16,256]{3,2,1,0:T(8,128)(2,1)}), bf16[16,16,16,256]{3,2,1,0:T(8,128)(2,1)S(1)}, u32[]{:S(2)}, u32[]{:S(2)}) async-start(bf16[16,16,16,256]{3,2,1,0:T(8,128)(2,1)} %get-tuple-element.68), calls=%async_computation.2 | async-start | bytes 4194304 | tf_op jit(solution)/shard_map/all_to_all | solution.py:60
  118.3 3.4 %collective-permute-start.10 = (bf16[4,256,256]{2,1,0:T(8,128)(2,1)}, bf16[4,256,256]{2,1,0:T(8,128)(2,1)}, u32[]{:S(2)}, u32[]{:S(2)}) collective-permute-start(bf16[4,256,256]{2,1,0:T(8,128)(2,1)} %get-tuple-element.72), channel_id=1, source_target_pairs={{0,96},{1,97},{2,98},{3,99},{4,100},{5,101},{6,102},{7,103},{8,104... | collective-permute-start | bytes 1572872 | tf_op jit(solution)/shard_map/ppermute | solution.py:42
  121.9 30.8 %all-to-all-done.2 = bf16[16,16,16,256]{3,2,1,0:T(8,128)(2,1)S(1)} async-done(((bf16[16,16,16,256]{3,2,1,0:T(8,128)(2,1)}), bf16[16,16,16,256]{3,2,1,0:T(8,128)(2,1)S(1)}, u32[]{:S(2)}, u32[]{:S(2)}) %all-to-all-start.2) | async-done | bytes 2097184 | tf_op jit(solution)/shard_map/all_to_all | solution.py:60
  152.9 25.9 %reduce-scatter.4.cloned.1.call-done = f32[1,8,16,256]{3,2,1,0:T(8,128)} async-done(((f32[16,8,16,256]{3,2,1,0:T(8,128)}), f32[1,8,16,256]{3,2,1,0:T(8,128)}) %reduce-scatter.4.cloned.1.call-update) | async-done | bytes 131088
  178.9 1.0 pad_maximum_fusion
  179.9 1.3 collective-permute-start.11
  181.2 2.4 %collective-permute-start.12 = (bf16[21,16,256]{2,1,0:T(8,128)(2,1)S(1)}, bf16[21,16,256]{2,1,0:T(8,128)(2,1)S(1)}, u32[]{:S(2)}, u32[]{:S(2)}) collective-permute-start(bf16[21,16,256]{2,1,0:T(8,128)(2,1)S(1)} %get-tuple-element.82), channel_id=1, source_target_pairs={{0,64},{1,65},{2,66},{3,67},{4,68},{5,69},{6,70},{7,71},{8,72},{9,... | collective-permute-start | bytes 516104 | tf_op jit(solution)/shard_map/ppermute | solution.py:42
  183.9 3.6 %shard_map.145 = f32[8,256,512]{2,1,0:T(8,128)} custom-call(s32[1]{0:T(128)} %bitcast.number, bf16[4,256,256]{2,1,0:T(8,128)(2,1)} %get-tuple-element.73.back0, bf16[4,256,256]{2,1,0:T(8,128)(2,1)} %collective-permute-done.8.back1, bf16[4,256,256]{2,1,0:T(8,128)(2,1)} %collective-permute-done.9.back2, bf16[4,256,256]{2,1,0:T(8,128)(2,1)} %collective-permute-done.10.back3), custom_call_target="tpu_custom_call" | custom-call | bytes 6291456 | tf_op jit(solution)/shard_map/pallas_call | solution.py:630
  187.5 1.6 collective-permute-done.12
  189.2 1.0 collective-permute-done.13
  190.3 4.5 %collective-permute-start.14 = (f32[21,16,256]{2,1,0:T(8,128)S(1)}, f32[21,16,256]{2,1,0:T(8,128)S(1)}, u32[]{:S(2)}, u32[]{:S(2)}) collective-permute-start(f32[21,16,256]{2,1,0:T(8,128)S(1)} %fusion.1), channel_id=1, source_target_pairs={{0,32},{1,33},{2,34},{3,35},{4,36},{5,37},{6,38},{7,39},{8,40},{9,... | collective-permute-start | bytes 1032200 | tf_op jit(solution)/shard_map/ppermute | solution.py:42
  194.7 1.3 collective-permute-done.14
  (91 shorter events, 12.4 us)
Async XLA Ops:
  7.2 1.0 copy-start
  7.2 78.9 %all-gather.3.cloned.1.call-start = ((), (), s32[]{:S(2)}) async-start(), calls=%async_computation.4 | async-start | bytes 2506752 | tf_op jit(solution)/shard_map/all_gather | solution.py:500
  9.1 5.9 %collective-permute-start.2 = (bf16[21,16,256]{2,1,0:T(8,128)(2,1)S(1)}, bf16[21,16,256]{2,1,0:T(8,128)(2,1)S(1)}, u32[]{:S(2)}, u32[]{:S(2)}) collective-permute-start(bf16[21,16,256]{2,1,0:T(8,128)(2,1)S(1)} %pad_maximum_fusion.1), channel_id=1, source_target_pairs={{0,4},{1,5},{2,6},{3,7},{4,0},{5,1},{6,2},{7,3},{8,12},{9,13},{10,... | collective-permute-start | bytes 516104 | tf_op jit(solution)/shard_map/ppermute | solution.py:42
  17.4 8.1 %copy-start.5 = (s32[4,1]{0,1:T(1,128)S(1)}, s32[4,1]{0,1:T(1,128)}, u32[]{:S(2)}) copy-start(s32[4,1]{0,1:T(1,128)} %param.12) | copy-start | bytes 52
  17.4 8.1 %copy-start.6 = (s32[4]{0:T(128)S(1)}, s32[4]{0:T(128)}, u32[]{:S(2)}) copy-start(s32[4]{0:T(128)} %param.13) | copy-start | bytes 52
  17.4 10.0 %copy-start.3 = (bf16[4,16,16,512]{3,2,1,0:T(8,128)(2,1)S(1)}, bf16[4,16,16,512]{3,2,1,0:T(8,128)(2,1)}, u32[]{:S(2)}) copy-start(bf16[4,16,16,512]{3,2,1,0:T(8,128)(2,1)} %param.11) | copy-start | bytes 3145732
  17.4 14.7 %copy-start.7 = (s32[8]{0:T(128)S(1)}, s32[8]{0:T(128)}, u32[]{:S(2)}) copy-start(s32[8]{0:T(128)} %param.14) | copy-start | bytes 100
  17.4 14.7 %copy-start.8 = (s32[8]{0:T(128)S(1)}, s32[8]{0:T(128)}, u32[]{:S(2)}) copy-start(s32[8]{0:T(128)} %param.15) | copy-start | bytes 100
  17.4 38.2 %all-to-all-start = ((bf16[16,16,16,256]{3,2,1,0:T(8,128)(2,1)}), bf16[16,16,16,256]{3,2,1,0:T(8,128)(2,1)S(1)}, u32[]{:S(2)}, u32[]{:S(2)}) async-start(bf16[16,16,16,256]{3,2,1,0:T(8,128)(2,1)} %broadcast_in_dim.72), calls=%async_computation | async-start | bytes 4194304 | tf_op jit(solution)/shard_map/all_to_all | solution.py:60
  25.5 153.4 %reduce-scatter.4.cloned.1.call-start = ((), (), s32[]{:S(2)}) async-start(), calls=%async_computation.5 | async-start | bytes 2228224
  25.5 2.7 %collective-permute-start = (s32[4,2]{0,1:T(2,128)S(1)}, s32[4,2]{0,1:T(2,128)S(1)}, u32[]{:S(2)}, u32[]{:S(2)}) collective-permute-start(s32[4,2]{0,1:T(2,128)S(1)} %pad_add_fusion.2), channel_id=1, source_target_pairs={{0,32},{1,33},{2,34},{3,35},{4,36},{5,37},{6,38},{7,39},{8,40},{9,... | collective-permute-start | bytes 104 | tf_op jit(solution)/shard_map/ppermute | solution.py:42
  27.4 13.3 %collective-permute-start.1 = (bf16[4,16,16,512]{3,2,1,0:T(8,128)(2,1)S(1)}, bf16[4,16,16,512]{3,2,1,0:T(8,128)(2,1)}, u32[]{:S(2)}, u32[]{:S(2)}) collective-permute-start(bf16[4,16,16,512]{3,2,1,0:T(8,128)(2,1)S(1)} %copy-done.3), channel_id=1, source_target_pairs={{0,32},{1,33},{2,34},{3,35},{4,36},{5,37},{6,38},{7,39},{8,40},{9,... | collective-permute-start | bytes 3145736 | tf_op jit(solution)/shard_map/ppermute | solution.py:42
  28.3 19.0 %collective-permute-start.3 = (bf16[4,256,256]{2,1,0:T(8,128)(2,1)}, bf16[4,256,256]{2,1,0:T(8,128)(2,1)}, u32[]{:S(2)}, u32[]{:S(2)}) collective-permute-start(bf16[4,256,256]{2,1,0:T(8,128)(2,1)} %get-tuple-element.49), channel_id=1, source_target_pairs={{0,32},{1,33},{2,34},{3,35},{4,36},{5,37},{6,38},{7,39},{8,40},{9,... | collective-permute-start | bytes 1572872 | tf_op jit(solution)/shard_map/ppermute | solution.py:42
  28.6 18.7 %collective-permute-start.4 = (bf16[4,256,256]{2,1,0:T(8,128)(2,1)}, bf16[4,256,256]{2,1,0:T(8,128)(2,1)}, u32[]{:S(2)}, u32[]{:S(2)}) collective-permute-start(bf16[4,256,256]{2,1,0:T(8,128)(2,1)} %get-tuple-element.50), channel_id=1, source_target_pairs={{0,64},{1,65},{2,66},{3,67},{4,68},{5,69},{6,70},{7,71},{8,72},{9,... | collective-permute-start | bytes 1572872 | tf_op jit(solution)/shard_map/ppermute | solution.py:42
  31.5 23.8 %collective-permute-start.5 = (bf16[4,256,256]{2,1,0:T(8,128)(2,1)}, bf16[4,256,256]{2,1,0:T(8,128)(2,1)}, u32[]{:S(2)}, u32[]{:S(2)}) collective-permute-start(bf16[4,256,256]{2,1,0:T(8,128)(2,1)} %get-tuple-element.51), channel_id=1, source_target_pairs={{0,96},{1,97},{2,98},{3,99},{4,100},{5,101},{6,102},{7,103},{8,104... | collective-permute-start | bytes 1572872 | tf_op jit(solution)/shard_map/ppermute | solution.py:42
  55.7 1.4 copy-start.1
  62.3 6.3 %collective-permute-start.6 = (f32[512,512]{1,0:T(8,128)}, f32[512,512]{1,0:T(8,128)S(1)}, u32[]{:S(2)}, u32[]{:S(2)}) collective-permute-start(f32[512,512]{1,0:T(8,128)} %get-tuple-element.53.own), channel_id=1, source_target_pairs={{0,32},{1,33},{2,34},{3,35},{4,36},{5,37},{6,38},{7,39},{8,40},{9,... | collective-permute-start | bytes 3145736 | tf_op jit(solution)/shard_map/ppermute | solution.py:42
  68.6 1.2 copy-start.9
  82.2 28.5 %all-to-all-start.1 = ((bf16[16,10,16,256]{3,2,1,0:T(8,128)(2,1)}), bf16[16,10,16,256]{3,2,1,0:T(8,128)(2,1)S(1)}, u32[]{:S(2)}, u32[]{:S(2)}) async-start(bf16[16,10,16,256]{3,2,1,0:T(8,128)(2,1)} %get-tuple-element.57), calls=%async_computation.1 | async-start | bytes 2621440 | tf_op jit(solution)/shard_map/all_to_all | solution.py:60
  98.7 2.9 %collective-permute-start.7 = (f32[512,512]{1,0:T(8,128)}, f32[512,512]{1,0:T(8,128)S(1)}, u32[]{:S(2)}, u32[]{:S(2)}) collective-permute-start(f32[512,512]{1,0:T(8,128)} %get-tuple-element.64.own), channel_id=1, source_target_pairs={{0,32},{1,33},{2,34},{3,35},{4,36},{5,37},{6,38},{7,39},{8,40},{9,... | collective-permute-start | bytes 3145736 | tf_op jit(solution)/shard_map/ppermute | solution.py:42
  101.6 1.0 copy-start.2
  110.7 41.9 %all-to-all-start.2 = ((bf16[16,16,16,256]{3,2,1,0:T(8,128)(2,1)}), bf16[16,16,16,256]{3,2,1,0:T(8,128)(2,1)S(1)}, u32[]{:S(2)}, u32[]{:S(2)}) async-start(bf16[16,16,16,256]{3,2,1,0:T(8,128)(2,1)} %get-tuple-element.68), calls=%async_computation.2 | async-start | bytes 4194304 | tf_op jit(solution)/shard_map/all_to_all | solution.py:60
  118.3 60.6 %copy-start.4 = (f32[10,16,256]{2,1,0:T(8,128)S(1)}, f32[10,16,256]{2,1,0:T(8,128)}, u32[]{:S(2)}) copy-start(f32[10,16,256]{2,1,0:T(8,128)} %convert_reduce_fusion.1) | copy-start | bytes 491524
  118.3 61.5 %collective-permute-start.10 = (bf16[4,256,256]{2,1,0:T(8,128)(2,1)}, bf16[4,256,256]{2,1,0:T(8,128)(2,1)}, u32[]{:S(2)}, u32[]{:S(2)}) collective-permute-start(bf16[4,256,256]{2,1,0:T(8,128)(2,1)} %get-tuple-element.72), channel_id=1, source_target_pairs={{0,96},{1,97},{2,98},{3,99},{4,100},{5,101},{6,102},{7,103},{8,104... | collective-permute-start | bytes 1572872 | tf_op jit(solution)/shard_map/ppermute | solution.py:42
  121.7 58.1 %collective-permute-start.8 = (bf16[4,256,256]{2,1,0:T(8,128)(2,1)}, bf16[4,256,256]{2,1,0:T(8,128)(2,1)}, u32[]{:S(2)}, u32[]{:S(2)}) collective-permute-start(bf16[4,256,256]{2,1,0:T(8,128)(2,1)} %get-tuple-element.70), channel_id=1, source_target_pairs={{0,32},{1,33},{2,34},{3,35},{4,36},{5,37},{6,38},{7,39},{8,40},{9,... | collective-permute-start | bytes 1572872 | tf_op jit(solution)/shard_map/ppermute | solution.py:42
  121.7 58.1 %collective-permute-start.9 = (bf16[4,256,256]{2,1,0:T(8,128)(2,1)}, bf16[4,256,256]{2,1,0:T(8,128)(2,1)}, u32[]{:S(2)}, u32[]{:S(2)}) collective-permute-start(bf16[4,256,256]{2,1,0:T(8,128)(2,1)} %get-tuple-element.71), channel_id=1, source_target_pairs={{0,64},{1,65},{2,66},{3,67},{4,68},{5,69},{6,70},{7,71},{8,72},{9,... | collective-permute-start | bytes 1572872 | tf_op jit(solution)/shard_map/ppermute | solution.py:42
  179.9 7.6 %collective-permute-start.11 = (bf16[21,16,256]{2,1,0:T(8,128)(2,1)S(1)}, bf16[21,16,256]{2,1,0:T(8,128)(2,1)S(1)}, u32[]{:S(2)}, u32[]{:S(2)}) collective-permute-start(bf16[21,16,256]{2,1,0:T(8,128)(2,1)S(1)} %get-tuple-element.83), channel_id=1, source_target_pairs={{0,4},{1,5},{2,6},{3,7},{4,0},{5,1},{6,2},{7,3},{8,12},{9,13},{10,... | collective-permute-start | bytes 516104 | tf_op jit(solution)/shard_map/ppermute | solution.py:42
  181.2 7.9 %collective-permute-start.12 = (bf16[21,16,256]{2,1,0:T(8,128)(2,1)S(1)}, bf16[21,16,256]{2,1,0:T(8,128)(2,1)S(1)}, u32[]{:S(2)}, u32[]{:S(2)}) collective-permute-start(bf16[21,16,256]{2,1,0:T(8,128)(2,1)S(1)} %get-tuple-element.82), channel_id=1, source_target_pairs={{0,64},{1,65},{2,66},{3,67},{4,68},{5,69},{6,70},{7,71},{8,72},{9,... | collective-permute-start | bytes 516104 | tf_op jit(solution)/shard_map/ppermute | solution.py:42
  183.7 6.5 %collective-permute-start.13 = (bf16[21,16,256]{2,1,0:T(8,128)(2,1)S(1)}, bf16[21,16,256]{2,1,0:T(8,128)(2,1)S(1)}, u32[]{:S(2)}, u32[]{:S(2)}) collective-permute-start(bf16[21,16,256]{2,1,0:T(8,128)(2,1)S(1)} %get-tuple-element.83), channel_id=1, source_target_pairs={{0,68},{1,69},{2,70},{3,71},{4,64},{5,65},{6,66},{7,67},{8,76},{9,... | collective-permute-start | bytes 516104 | tf_op jit(solution)/shard_map/ppermute | solution.py:42
  190.3 5.7 %collective-permute-start.14 = (f32[21,16,256]{2,1,0:T(8,128)S(1)}, f32[21,16,256]{2,1,0:T(8,128)S(1)}, u32[]{:S(2)}, u32[]{:S(2)}) collective-permute-start(f32[21,16,256]{2,1,0:T(8,128)S(1)} %fusion.1), channel_id=1, source_target_pairs={{0,32},{1,33},{2,34},{3,35},{4,36},{5,37},{6,38},{7,39},{8,40},{9,... | collective-permute-start | bytes 1032200 | tf_op jit(solution)/shard_map/ppermute | solution.py:42
Sparse Core Ops, SparseCore 0:
  15.9 62.1 all-gather.2
  82.3 96.4 reduce-scatter.3

commit v3 on v1

--- a/solution.py
+++ b/solution.py
@@ -226,7 +226,7 @@
                 side, step = unit // 4, unit % 4
                 first = (x * 4 + step) * rows
                 down[z, first : first + rows, side * half : (side + 1) * half] = pieces[
-                    z * 4 + x, 8 + unit
+                    z * 4 + x, unit
                 ]
 
 
@@ -279,9 +279,28 @@
 
 
 def grad_conv_kernel(
-    loss_scale, mask, own, got, folded, pieces, windows_own, windows_pair, glow, grads, down, turned
+    loss_scale,
+    mask,
+    own,
+    got,
+    folded,
+    pieces,
+    windows_own,
+    windows_pair,
+    glow,
+    grads,
+    down,
+    turned,
+    windows,
+    sem,
 ):
     half = folded.shape[2]
+    copies = [
+        pltpu.make_async_copy(ref, windows.at[part], sem.at[part])
+        for part, ref in enumerate((windows_own, windows_pair))
+    ]
+    for copy in copies:
+        copy.start()
     rows = grads.shape[2]
     middle = folded.shape[1] // 2
     gather_down(pieces, down)
@@ -290,12 +309,15 @@
     for k in range(4):
         grad = folded[k].astype(F32) * loss_scale + dot(glow[...], down[k], 1, 1)
         turned[k] = (grad * kept).T.astype(BF)
+    for copy in copies:
+        copy.wait()
     for t in range(9):
         total = None
         for k in range(4):
             v = (k // 2 + t // 3) * 4 + k % 2 + t % 3
-            for columns, windows in ((slice(0, middle), windows_own), (slice(middle, None), windows_pair)):
-                term = dot(turned[k, :, columns], windows[v], 1, 0)
+            for part in range(2):
+                columns = slice(part * middle, (part + 1) * middle)
+                term = dot(turned[k, :, columns], windows[part, v], 1, 0)
                 total = term if total is None else total + term
         total = total.T.astype(BF)
         for f in range(32):
@@ -477,9 +499,10 @@
     first = jnp.where(y == 0, packed, other)
     second = jnp.where(y == 0, other, packed)
     down_kept = jnp.where(core == 0, first[4:12], second[4:12])
-    up_down = jnp.concatenate([first[:4], second[:4], down_kept])
+    up_two = jnp.concatenate([first[:4], second[:4]])
     conv_two = jnp.concatenate([first[12:], second[12:]])
-    up_down = over_plane(jnp.broadcast_to(up_down, (16, *up_down.shape)))
+    up_two = over_plane(jnp.broadcast_to(up_two, (16, *up_two.shape)))
+    down_kept = over_plane(jnp.broadcast_to(down_kept, (16, *down_kept.shape)))
     conv_two = lax.all_gather(conv_two, "fsdp", axis_index_groups=PLANES)
 
     images_pair = send(images, "c")
@@ -516,7 +539,9 @@
     windows_own, residual_own = normed_windows(own_meta, images, norm_gain, norm_shift)
     windows_pair, residual_pair = normed_windows(pair_meta, images_pair, norm_gain, norm_shift)
 
-    ready, windows_own, windows_pair = lax.optimization_barrier((meta, windows_own, windows_pair))
+    ready, mask, windows_own, windows_pair = lax.optimization_barrier(
+        (meta, mask, windows_own, windows_pair)
+    )
     folded, glow_part = kernel_call(
         functools.partial(glow_kernel, extent, loss_scale),
         (
@@ -533,7 +558,7 @@
         ),
         in_specs=[SCALARS] + [pl.BlockSpec(memory_space=pl.ANY)] * 4 + [WHOLE],
         out_specs=(WHOLE, WHOLE),
-    )(ready, *arrived, up_down)
+    )(ready, *arrived, up_two)
     glow_got = send(glow_part, "c")
 
     glow, conv_grads = kernel_call(
@@ -544,10 +569,15 @@
         ),
         flops=80 * low_rows * channels * half,
         moved_bytes=15 << 20,
-        scratch=(pltpu.VMEM((4, half, channels), BF), pltpu.VMEM((4, half, low_rows), BF)),
-        in_specs=[WHOLE] * 7,
+        scratch=(
+            pltpu.VMEM((4, half, channels), BF),
+            pltpu.VMEM((4, half, low_rows), BF),
+            pltpu.VMEM((2, *windows_own.shape), BF),
+            pltpu.SemaphoreType.DMA((2,)),
+        ),
+        in_specs=[WHOLE] * 5 + [pl.BlockSpec(memory_space=pl.ANY)] * 2,
         out_specs=(WHOLE, WHOLE),
-    )(mask, glow_part, glow_got, folded, up_down, windows_own, windows_pair)
+    )(mask, glow_part, glow_got, folded, down_kept, windows_own, windows_pair)
     conv_grads = over_plane(conv_grads)
     glow, windows_own, windows_pair = lax.optimization_barrier((glow, windows_own, windows_pair))
 
@@ -563,7 +593,7 @@
         scratch=(pltpu.VMEM((9, channels, half), BF), pltpu.VMEM((4, half, channels), BF)),
         in_specs=[WHOLE] * 7,
         out_specs=(WHOLE,) * 3,
-    )(mask, conv_two, up_down, windows_own, windows_pair, residual_own, residual_pair)
+    )(mask, conv_two, down_kept, windows_own, windows_pair, residual_own, residual_pair)
     low_got = send(low_part, "c")
 
     *returning, grads = kernel_call(
@@ -583,12 +613,13 @@
         ),
         in_specs=[SCALARS] + [WHOLE] * 8,
         out_specs=(WHOLE,) * 5,
-    )(meta, mask, low_part, low_got, wide, skip, glow, folded, up_down)
+    )(meta, mask, low_part, low_got, wide, skip, glow, folded, up_two)
     returned = over_dp(returning)
     grads = over_plane(grads)
 
     conv_sum = jnp.sum(conv_grads.astype(F32), axis=0).reshape(2, 9, rows, half)
-    conv_sum, returned = lax.optimization_barrier((conv_sum, returned))
+    conv_sum, beside = lax.optimization_barrier((conv_sum, returned[1]))
+    returned = (returned[0], beside, *returned[2:])
 
     def by_core(own, pair):
         return jnp.where(core == 0, jnp.stack([own, pair]), jnp.stack([pair, own]))

time: 189 us -> 197 us (1.042)
  blocking collectives: 0 us -> 23.2 us
  waiting for transfers between devices: 56.4 us -> 40.6 us
    all_to_all x0 -> x1, blocking collectives: none -> 23.2 us  [over_plane(): lax.all_to_all(blocks, 'fsdp', split_axis=0, concat_axis=0, axis_index_gr...]
    ppermute x19, waiting for transfers between devices: 43.8 us -> 25.1 us  [send(): return lax.ppermute(value, AXES, STEP[move])]
    all_to_all x3, waiting for transfers between devices: 12.6 us -> 15.5 us  [over_plane(): lax.all_to_all(blocks, 'fsdp', split_axis=0, concat_axis=0, axis_index_gr...]
    unnamed x22 -> x30, local copies, waits for them, and re-layouts: 2.46 us -> 4.8 us
  transfers between devices with their start and end apart: 23 -> 23, of which waited for: 14 -> 11; matrix products, arithmetic and copies ran while one was open for 4% -> 5% of each run, Pallas kernels for 31% -> 29%
where the time goes in v3:
time: 197 us
  Pallas kernels  56.9 us (29%)
  starting transfers between devices  42.8 us (22%)
  waiting for transfers between devices  40.6 us (21%)
  blocking collectives  23.2 us (12%)
  between operations  14.5 us (7%)
  local copies, waits for them, and re-layouts  13.4 us (7%)
  other arithmetic  5.25 us (3%)
    ppermute x19, starting transfers between devices, send(): return lax.ppermute(value, AXES, STEP[move])  25.9 us
    ppermute x19, waiting for transfers between devices, send(): return lax.ppermute(value, AXES, STEP[move])  25.1 us
    all_to_all x1, blocking collectives, over_plane(): lax.all_to_all(blocks, 'fsdp', split_axis=0, concat_axis=0, axis_index_gr...  23.2 us
    all_to_all x3, starting transfers between devices, over_plane(): lax.all_to_all(blocks, 'fsdp', split_axis=0, concat_axis=0, axis_index_gr...  16.9 us
    all_to_all x3, waiting for transfers between devices, over_plane(): lax.all_to_all(blocks, 'fsdp', split_axis=0, concat_axis=0, axis_index_gr...  15.5 us
    pallas_call x2, Pallas kernels, normed_windows(): kernel_call(functools.partial(norm_kernel, extent), (jax.ShapeDtypeStruct...  13 us
    pallas_call x1, Pallas kernels, per_device(): kernel_call(functools.partial(grad_conv_kernel, loss_scale), (jax.ShapeDt...  12.3 us
    pallas_call x1, Pallas kernels, per_device(): kernel_call(conv_kernel, (jax.ShapeDtypeStruct((4, low_rows, half), F32),...  12.2 us
  transfers between devices with their start and end apart: 23, of which 11 were waited for; matrix products, arithmetic and copies ran while one was open for 5% of the time, Pallas kernels for 29%

profile of v3, /device:TPU:1, one launch (start us, length us, event | category | flops | bytes accessed | tf_op | source)
XLA Modules:
  0.0 196.6 jit_solution(9269237448025545499)
XLA Ops:
  9.2 2.2 %collective-permute-start.2 = (bf16[21,16,256]{2,1,0:T(8,128)(2,1)S(1)}, bf16[21,16,256]{2,1,0:T(8,128)(2,1)S(1)}, u32[]{:S(2)}, u32[]{:S(2)}) collective-permute-start(bf16[21,16,256]{2,1,0:T(8,128)(2,1)S(1)} %pad_maximum_fusion.1), channel_id=1, source_target_pairs={{0,4},{1,5},{2,6},{3,7},{4,0},{5,1},{6,2},{7,3},{8,12},{9,13},{10,... | collective-permute-start | bytes 516104 | tf_op jit(solution)/shard_map/ppermute | solution.py:41
  11.4 3.1 %shard_map.140 = (bf16[4,256,256]{2,1,0:T(8,128)(2,1)}, bf16[4,256,256]{2,1,0:T(8,128)(2,1)}, bf16[4,256,256]{2,1,0:T(8,128)(2,1)}, bf16[4,256,256]{2,1,0:T(8,128)(2,1)}) custom-call(s32[1]{0:T(128)} %bitcast.number, bf16[8,256,512]{2,1,0:T(8,128)(2,1)} %bitcast.77), custom_call_target="tpu_custom_call" | custom-call | bytes 4194304 | tf_op jit(solution)/shard_map/pallas_call | solution.py:489
  16.0 1.7 collective-permute-start
  20.0 7.8 %all-to-all-start.1 = ((bf16[16,8,16,256]{3,2,1,0:T(8,128)(2,1)}), bf16[16,8,16,256]{3,2,1,0:T(8,128)(2,1)S(1)}, u32[]{:S(2)}, u32[]{:S(2)}) async-start(bf16[16,8,16,256]{3,2,1,0:T(8,128)(2,1)} %broadcast_in_dim.76), calls=%async_computation.1 | async-start | bytes 2097152 | tf_op jit(solution)/shard_map/all_to_all | solution.py:59
  28.5 2.9 %collective-permute-start.4 = (bf16[4,256,256]{2,1,0:T(8,128)(2,1)}, bf16[4,256,256]{2,1,0:T(8,128)(2,1)}, u32[]{:S(2)}, u32[]{:S(2)}) collective-permute-start(bf16[4,256,256]{2,1,0:T(8,128)(2,1)} %get-tuple-element.51), channel_id=1, source_target_pairs={{0,64},{1,65},{2,66},{3,67},{4,68},{5,69},{6,70},{7,71},{8,72},{9,... | collective-permute-start | bytes 1572872 | tf_op jit(solution)/shard_map/ppermute | solution.py:41
  33.8 6.5 %shard_map.138 = (bf16[16,256,512]{2,1,0:T(8,128)(2,1)}, bf16[4,256,256]{2,1,0:T(8,128)(2,1)}) custom-call(s32[32]{0:T(128)} %concatenate.37.meta, bf16[4,256,512]{2,1,0:T(8,128)(2,1)} %bitcast.80, f32[1,512]{1,0:T(1,128)} %bitcast.88, f32[1,512]{1,0:T(1,128)} %bitcast.90), custom_call_target="tpu_custom_call" | custom-call | flops 20971520 | bytes 6291456 | tf_op jit(solution)/shard_map/pallas_call | solution.py:187
  41.3 6.5 %shard_map.139 = (bf16[16,256,512]{2,1,0:T(8,128)(2,1)}, bf16[4,256,256]{2,1,0:T(8,128)(2,1)}) custom-call(s32[32]{0:T(128)} %concatenate.39.meta, bf16[4,256,512]{2,1,0:T(8,128)(2,1)} %bitcast.81, f32[1,512]{1,0:T(1,128)} %bitcast.89, f32[1,512]{1,0:T(1,128)} %bitcast.91), custom_call_target="tpu_custom_call" | custom-call | flops 20971520 | bytes 6291456 | tf_op jit(solution)/shard_map/pallas_call | solution.py:187
  48.7 6.6 %collective-permute-done.5.cot3 = bf16[4,256,256]{2,1,0:T(8,128)(2,1)} collective-permute-done((bf16[4,256,256]{2,1,0:T(8,128)(2,1)}, bf16[4,256,256]{2,1,0:T(8,128)(2,1)}, u32[]{:S(2)}, u32[]{:S(2)}) %collective-permute-start.5) | collective-permute-done | bytes 524320 | tf_op jit(solution)/shard_map/ppermute | solution.py:41
  56.2 4.9 %shard_map.141 = (bf16[4,512,256]{2,1,0:T(8,128)(2,1)}, f32[512,512]{1,0:T(8,128)}) custom-call(s32[32]{0:T(128)} %concatenate.35.meta, bf16[4,256,256]{2,1,0:T(8,128)(2,1)} %get-tuple-element.49.cot0, bf16[4,256,256]{2,1,0:T(8,128)(2,1)} %collective-permute-done.3.cot1, bf16[4,256,256]{2,1,0:T(8,128)(2,1)} %collective-permute-done.4.cot2, ...), custom_call_target="tpu_custom_call" | custom-call | flops 536870912 | bytes 5242880 | tf_op jit(solution)/shard_map/pallas_call | solution.py:545
  62.5 23.2 %all_to_all.20.pieces = bf16[16,8,16,256]{3,2,1,0:T(8,128)(2,1)} all-to-all(bf16[16,8,16,256]{3,2,1,0:T(8,128)(2,1)S(1)} %broadcast_in_dim.75), channel_id=1, replica_groups={{0,1,2,3,8,9,10,11,16,17,18,19,24,25,26,27},{4,5,6,7,12,13,14,15,20,21,..., dimensions={0} | all-to-all | bytes 2097152 | tf_op jit(solution)/shard_map/all_to_all | solution.py:59
  86.7 12.3 %shard_map.142 = (bf16[512,512]{1,0:T(8,128)(2,1)}, bf16[16,18,16,256]{3,2,1,0:T(8,128)(2,1)}) custom-call(f32[512,128]{1,0:T(8,128)} %broadcast_in_dim.72.mask, f32[512,512]{1,0:T(8,128)} %get-tuple-element.53.own, f32[512,512]{1,0:T(8,128)} %copy-done.13, bf16[4,512,256]{2,1,0:T(8,128)(2,1)} %get-tuple-element.54.folded, ...), custom_call_target="tpu_custom_call" | custom-call | flops 5368709120 | bytes 15728640 | tf_op jit(solution)/shard_map/pallas_call | solution.py:564
  99.1 3.9 %all-to-all-start.2 = ((bf16[16,18,16,256]{3,2,1,0:T(8,128)(2,1)}), bf16[16,18,16,256]{3,2,1,0:T(8,128)(2,1)S(1)}, u32[]{:S(2)}, u32[]{:S(2)}) async-start(bf16[16,18,16,256]{3,2,1,0:T(8,128)(2,1)} %get-tuple-element.67), calls=%async_computation.2 | async-start | bytes 4718592 | tf_op jit(solution)/shard_map/all_to_all | solution.py:59
  103.0 12.2 %shard_map.143 = (f32[4,512,256]{2,1,0:T(8,128)}, bf16[4,512,256]{2,1,0:T(8,128)(2,1)}, f32[512,512]{1,0:T(8,128)}) custom-call(f32[512,128]{1,0:T(8,128)} %broadcast_in_dim.72.mask, bf16[16,18,16,256]{3,2,1,0:T(8,128)(2,1)} %bitcast.98, bf16[16,8,16,256]{3,2,1,0:T(8,128)(2,1)} %all_to_all.20.pieces, bf16[16,256,512]{2,1,0:T(8,128)(2,1)} %get-tuple-element.58.windows_own, ...), custom_call_target="tpu_custom_call" | custom-call | flops 5368709120 | bytes 18874368 | tf_op jit(solution)/shard_map/pallas_call | solution.py:584
  115.2 1.7 collective-permute-start.7
  116.9 2.5 %collective-permute-done.7.got = f32[512,512]{1,0:T(8,128)S(1)} collective-permute-done((f32[512,512]{1,0:T(8,128)}, f32[512,512]{1,0:T(8,128)S(1)}, u32[]{:S(2)}, u32[]{:S(2)}) %collective-permute-start.7) | collective-permute-done | bytes 1048608 | tf_op jit(solution)/shard_map/ppermute | solution.py:41
  120.4 7.7 %shard_map.144 = (bf16[4,256,256]{2,1,0:T(8,128)(2,1)}, bf16[4,256,256]{2,1,0:T(8,128)(2,1)}, bf16[4,256,256]{2,1,0:T(8,128)(2,1)}, bf16[4,256,256]{2,1,0:T(8,128)(2,1)}, bf16[16,16,16,256]{3,2,1,0:T(8,128)(2,1)}) custom-call(s32[32]{0:T(128)} %concatenate.35.meta, f32[512,128]{1,0:T(8,128)} %broadcast_in_dim.72.mask, f32[512,512]{1,0:T(8,128)} %get-tuple-element.62.own, ...), custom_call_target="tpu_custom_call" | custom-call | flops 1610612736 | bytes 14680064 | tf_op jit(solution)/shard_map/pallas_call | solution.py:599
  128.1 7.1 %all-to-all-done.2 = bf16[16,18,16,256]{3,2,1,0:T(8,128)(2,1)S(1)} async-done(((bf16[16,18,16,256]{3,2,1,0:T(8,128)(2,1)}), bf16[16,18,16,256]{3,2,1,0:T(8,128)(2,1)S(1)}, u32[]{:S(2)}, u32[]{:S(2)}) %all-to-all-start.2) | async-done | bytes 2359328 | tf_op jit(solution)/shard_map/all_to_all | solution.py:59
  135.2 5.2 %all-to-all-start.3 = ((bf16[16,16,16,256]{3,2,1,0:T(8,128)(2,1)}), bf16[16,16,16,256]{3,2,1,0:T(8,128)(2,1)}, u32[]{:S(2)}, u32[]{:S(2)}) async-start(bf16[16,16,16,256]{3,2,1,0:T(8,128)(2,1)} %get-tuple-element.72), calls=%async_computation.3 | async-start | bytes 4194304 | tf_op jit(solution)/shard_map/all_to_all | solution.py:59
  140.4 2.1 %collective-permute-start.8 = (bf16[4,256,256]{2,1,0:T(8,128)(2,1)}, bf16[4,256,256]{2,1,0:T(8,128)(2,1)S(1)}, u32[]{:S(2)}, u32[]{:S(2)}) collective-permute-start(bf16[4,256,256]{2,1,0:T(8,128)(2,1)} %get-tuple-element.68), channel_id=1, source_target_pairs={{0,32},{1,33},{2,34},{3,35},{4,36},{5,37},{6,38},{7,39},{8,40},{9,... | collective-permute-start | bytes 1572872 | tf_op jit(solution)/shard_map/ppermute | solution.py:41
  142.9 1.4 collective-permute-done.8.back1
  144.3 1.3 collective-permute-start.11
  145.6 2.4 %collective-permute-start.12 = (bf16[9,16,256]{2,1,0:T(8,128)(2,1)S(1)}, bf16[9,16,256]{2,1,0:T(8,128)(2,1)S(1)}, u32[]{:S(2)}, u32[]{:S(2)}) collective-permute-start(bf16[9,16,256]{2,1,0:T(8,128)(2,1)S(1)} %get-tuple-element.84), channel_id=1, source_target_pairs={{0,64},{1,65},{2,66},{3,67},{4,68},{5,69},{6,70},{7,71},{8,72},{9,... | collective-permute-start | bytes 221192 | tf_op jit(solution)/shard_map/ppermute | solution.py:41
  148.3 3.5 %collective-permute-done.12 = bf16[9,16,256]{2,1,0:T(8,128)(2,1)S(1)} collective-permute-done((bf16[9,16,256]{2,1,0:T(8,128)(2,1)S(1)}, bf16[9,16,256]{2,1,0:T(8,128)(2,1)S(1)}, u32[]{:S(2)}, u32[]{:S(2)}) %collective-permute-start.12) | collective-permute-done | bytes 73760 | tf_op jit(solution)/shard_map/ppermute | solution.py:41
  151.7 1.6 collective-permute-done.13
  155.1 2.5 %collective-permute-start.9 = (bf16[4,256,256]{2,1,0:T(8,128)(2,1)S(1)}, bf16[4,256,256]{2,1,0:T(8,128)(2,1)S(1)}, u32[]{:S(2)}, u32[]{:S(2)}) collective-permute-start(bf16[4,256,256]{2,1,0:T(8,128)(2,1)S(1)} %copy-done.14), channel_id=1, source_target_pairs={{0,64},{1,65},{2,66},{3,67},{4,68},{5,69},{6,70},{7,71},{8,72},{9,... | collective-permute-start | bytes 1572872 | tf_op jit(solution)/shard_map/ppermute | solution.py:41
  159.2 8.4 %all-to-all-done.3 = bf16[16,16,16,256]{3,2,1,0:T(8,128)(2,1)} async-done(((bf16[16,16,16,256]{3,2,1,0:T(8,128)(2,1)}), bf16[16,16,16,256]{3,2,1,0:T(8,128)(2,1)}, u32[]{:S(2)}, u32[]{:S(2)}) %all-to-all-start.3) | async-done | bytes 2097184 | tf_op jit(solution)/shard_map/all_to_all | solution.py:59
  167.6 1.9 convert_reduce_fusion.1
  169.6 1.3 collective-permute-start.15
  171.0 2.7 %collective-permute-start.16 = (bf16[12,16,256]{2,1,0:T(8,128)(2,1)S(1)}, bf16[12,16,256]{2,1,0:T(8,128)(2,1)S(1)}, u32[]{:S(2)}, u32[]{:S(2)}) collective-permute-start(bf16[12,16,256]{2,1,0:T(8,128)(2,1)S(1)} %get-tuple-element.80), channel_id=1, source_target_pairs={{0,64},{1,65},{2,66},{3,67},{4,68},{5,69},{6,70},{7,71},{8,72},{9,... | collective-permute-start | bytes 294920 | tf_op jit(solution)/shard_map/ppermute | solution.py:41
  173.7 7.3 %collective-permute-done.9.back2 = bf16[4,256,256]{2,1,0:T(8,128)(2,1)S(1)} collective-permute-done((bf16[4,256,256]{2,1,0:T(8,128)(2,1)S(1)}, bf16[4,256,256]{2,1,0:T(8,128)(2,1)S(1)}, u32[]{:S(2)}, u32[]{:S(2)}) %collective-permute-start.9) | collective-permute-done | bytes 524320 | tf_op jit(solution)/shard_map/ppermute | solution.py:41
  181.8 3.6 %shard_map.145 = f32[8,256,512]{2,1,0:T(8,128)} custom-call(s32[1]{0:T(128)} %bitcast.number, bf16[4,256,256]{2,1,0:T(8,128)(2,1)} %get-tuple-element.66.back0, bf16[4,256,256]{2,1,0:T(8,128)(2,1)} %copy-done.6, bf16[4,256,256]{2,1,0:T(8,128)(2,1)} %copy-done.8, bf16[4,256,256]{2,1,0:T(8,128)(2,1)} %copy-done.7), custom_call_target="tpu_custom_call" | custom-call | bytes 6291456 | tf_op jit(solution)/shard_map/pallas_call | solution.py:638
  185.5 1.6 collective-permute-start.18
  (110 shorter events, 22.4 us)
Async XLA Ops:
  7.2 8.7 %copy-start.10 = (s32[4]{0:T(128)S(1)}, s32[4]{0:T(128)}, u32[]{:S(2)}) copy-start(s32[4]{0:T(128)} %param.13) | copy-start | bytes 52
  7.2 8.7 %copy-start.9 = (s32[4,1]{0,1:T(1,128)S(1)}, s32[4,1]{0,1:T(1,128)}, u32[]{:S(2)}) copy-start(s32[4,1]{0,1:T(1,128)} %param.12) | copy-start | bytes 52
  7.2 10.5 %copy-start.2 = (bf16[4,16,16,512]{3,2,1,0:T(8,128)(2,1)S(1)}, bf16[4,16,16,512]{3,2,1,0:T(8,128)(2,1)}, u32[]{:S(2)}) copy-start(bf16[4,16,16,512]{3,2,1,0:T(8,128)(2,1)} %param.11) | copy-start | bytes 3145732
  7.2 11.5 %copy-start.11 = (s32[8]{0:T(128)S(1)}, s32[8]{0:T(128)}, u32[]{:S(2)}) copy-start(s32[8]{0:T(128)} %param.14) | copy-start | bytes 100
  7.2 11.5 %copy-start.12 = (s32[8]{0:T(128)S(1)}, s32[8]{0:T(128)}, u32[]{:S(2)}) copy-start(s32[8]{0:T(128)} %param.15) | copy-start | bytes 100
  7.2 95.8 %all-gather.3.cloned.1.call-start = ((), (), s32[]{:S(2)}) async-start(), calls=%async_computation.4 | async-start | bytes 2506752 | tf_op jit(solution)/shard_map/all_gather | solution.py:506
  9.2 5.9 %collective-permute-start.2 = (bf16[21,16,256]{2,1,0:T(8,128)(2,1)S(1)}, bf16[21,16,256]{2,1,0:T(8,128)(2,1)S(1)}, u32[]{:S(2)}, u32[]{:S(2)}) collective-permute-start(bf16[21,16,256]{2,1,0:T(8,128)(2,1)S(1)} %pad_maximum_fusion.1), channel_id=1, source_target_pairs={{0,4},{1,5},{2,6},{3,7},{4,0},{5,1},{6,2},{7,3},{8,12},{9,13},{10,... | collective-permute-start | bytes 516104 | tf_op jit(solution)/shard_map/ppermute | solution.py:41
  15.2 4.9 %copy-start.5 = (bf16[21,16,256]{2,1,0:T(8,128)(2,1)}, bf16[21,16,256]{2,1,0:T(8,128)(2,1)S(1)}, u32[]{:S(2)}) copy-start(bf16[21,16,256]{2,1,0:T(8,128)(2,1)S(1)} %get-tuple-element.83) | copy-start | bytes 516100
  16.0 2.5 %collective-permute-start = (s32[4,2]{0,1:T(2,128)S(1)}, s32[4,2]{0,1:T(2,128)S(1)}, u32[]{:S(2)}, u32[]{:S(2)}) collective-permute-start(s32[4,2]{0,1:T(2,128)S(1)} %pad_add_fusion.2), channel_id=1, source_target_pairs={{0,32},{1,33},{2,34},{3,35},{4,36},{5,37},{6,38},{7,39},{8,40},{9,... | collective-permute-start | bytes 104 | tf_op jit(solution)/shard_map/ppermute | solution.py:41
  17.7 22.6 %collective-permute-start.1 = (bf16[4,16,16,512]{3,2,1,0:T(8,128)(2,1)S(1)}, bf16[4,16,16,512]{3,2,1,0:T(8,128)(2,1)S(1)}, u32[]{:S(2)}, u32[]{:S(2)}) collective-permute-start(bf16[4,16,16,512]{3,2,1,0:T(8,128)(2,1)S(1)} %copy-done.2), channel_id=1, source_target_pairs={{0,32},{1,33},{2,34},{3,35},{4,36},{5,37},{6,38},{7,39},{8,40},{9,... | collective-permute-start | bytes 3145736 | tf_op jit(solution)/shard_map/ppermute | solution.py:41
  20.0 35.2 %all-to-all-start.1 = ((bf16[16,8,16,256]{3,2,1,0:T(8,128)(2,1)}), bf16[16,8,16,256]{3,2,1,0:T(8,128)(2,1)S(1)}, u32[]{:S(2)}, u32[]{:S(2)}) async-start(bf16[16,8,16,256]{3,2,1,0:T(8,128)(2,1)} %broadcast_in_dim.76), calls=%async_computation.1 | async-start | bytes 2097152 | tf_op jit(solution)/shard_map/all_to_all | solution.py:59
  27.9 20.8 %collective-permute-start.3 = (bf16[4,256,256]{2,1,0:T(8,128)(2,1)}, bf16[4,256,256]{2,1,0:T(8,128)(2,1)}, u32[]{:S(2)}, u32[]{:S(2)}) collective-permute-start(bf16[4,256,256]{2,1,0:T(8,128)(2,1)} %get-tuple-element.50), channel_id=1, source_target_pairs={{0,32},{1,33},{2,34},{3,35},{4,36},{5,37},{6,38},{7,39},{8,40},{9,... | collective-permute-start | bytes 1572872 | tf_op jit(solution)/shard_map/ppermute | solution.py:41
  28.5 20.1 %collective-permute-start.4 = (bf16[4,256,256]{2,1,0:T(8,128)(2,1)}, bf16[4,256,256]{2,1,0:T(8,128)(2,1)}, u32[]{:S(2)}, u32[]{:S(2)}) collective-permute-start(bf16[4,256,256]{2,1,0:T(8,128)(2,1)} %get-tuple-element.51), channel_id=1, source_target_pairs={{0,64},{1,65},{2,66},{3,67},{4,68},{5,69},{6,70},{7,71},{8,72},{9,... | collective-permute-start | bytes 1572872 | tf_op jit(solution)/shard_map/ppermute | solution.py:41
  31.5 23.8 %collective-permute-start.5 = (bf16[4,256,256]{2,1,0:T(8,128)(2,1)}, bf16[4,256,256]{2,1,0:T(8,128)(2,1)}, u32[]{:S(2)}, u32[]{:S(2)}) collective-permute-start(bf16[4,256,256]{2,1,0:T(8,128)(2,1)} %get-tuple-element.52), channel_id=1, source_target_pairs={{0,96},{1,97},{2,98},{3,99},{4,100},{5,101},{6,102},{7,103},{8,104... | collective-permute-start | bytes 1572872 | tf_op jit(solution)/shard_map/ppermute | solution.py:41
  61.2 24.6 %collective-permute-start.6 = (f32[512,512]{1,0:T(8,128)}, f32[512,512]{1,0:T(8,128)S(1)}, u32[]{:S(2)}, u32[]{:S(2)}) collective-permute-start(f32[512,512]{1,0:T(8,128)} %get-tuple-element.53.own), channel_id=1, source_target_pairs={{0,32},{1,33},{2,34},{3,35},{4,36},{5,37},{6,38},{7,39},{8,40},{9,... | collective-permute-start | bytes 3145736 | tf_op jit(solution)/shard_map/ppermute | solution.py:41
  99.1 36.1 %all-to-all-start.2 = ((bf16[16,18,16,256]{3,2,1,0:T(8,128)(2,1)}), bf16[16,18,16,256]{3,2,1,0:T(8,128)(2,1)S(1)}, u32[]{:S(2)}, u32[]{:S(2)}) async-start(bf16[16,18,16,256]{3,2,1,0:T(8,128)(2,1)} %get-tuple-element.67), calls=%async_computation.2 | async-start | bytes 4718592 | tf_op jit(solution)/shard_map/all_to_all | solution.py:59
  115.2 4.2 %collective-permute-start.7 = (f32[512,512]{1,0:T(8,128)}, f32[512,512]{1,0:T(8,128)S(1)}, u32[]{:S(2)}, u32[]{:S(2)}) collective-permute-start(f32[512,512]{1,0:T(8,128)} %get-tuple-element.62.own), channel_id=1, source_target_pairs={{0,32},{1,33},{2,34},{3,35},{4,36},{5,37},{6,38},{7,39},{8,40},{9,... | collective-permute-start | bytes 3145736 | tf_op jit(solution)/shard_map/ppermute | solution.py:41
  135.2 32.4 %all-to-all-start.3 = ((bf16[16,16,16,256]{3,2,1,0:T(8,128)(2,1)}), bf16[16,16,16,256]{3,2,1,0:T(8,128)(2,1)}, u32[]{:S(2)}, u32[]{:S(2)}) async-start(bf16[16,16,16,256]{3,2,1,0:T(8,128)(2,1)} %get-tuple-element.72), calls=%async_computation.3 | async-start | bytes 4194304 | tf_op jit(solution)/shard_map/all_to_all | solution.py:59
  140.4 14.7 %copy-start.14 = (bf16[4,256,256]{2,1,0:T(8,128)(2,1)S(1)}, bf16[4,256,256]{2,1,0:T(8,128)(2,1)}, u32[]{:S(2)}) copy-start(bf16[4,256,256]{2,1,0:T(8,128)(2,1)} %get-tuple-element.70) | copy-start | bytes 1572868
  140.4 3.9 %collective-permute-start.8 = (bf16[4,256,256]{2,1,0:T(8,128)(2,1)}, bf16[4,256,256]{2,1,0:T(8,128)(2,1)S(1)}, u32[]{:S(2)}, u32[]{:S(2)}) collective-permute-start(bf16[4,256,256]{2,1,0:T(8,128)(2,1)} %get-tuple-element.68), channel_id=1, source_target_pairs={{0,32},{1,33},{2,34},{3,35},{4,36},{5,37},{6,38},{7,39},{8,40},{9,... | collective-permute-start | bytes 1572872 | tf_op jit(solution)/shard_map/ppermute | solution.py:41
  144.3 25.2 %copy-start.6 = (bf16[4,256,256]{2,1,0:T(8,128)(2,1)}, bf16[4,256,256]{2,1,0:T(8,128)(2,1)S(1)}, u32[]{:S(2)}) copy-start(bf16[4,256,256]{2,1,0:T(8,128)(2,1)S(1)} %collective-permute-done.8.back1) | copy-start | bytes 1572868
  144.3 3.9 %collective-permute-start.11 = (bf16[9,16,256]{2,1,0:T(8,128)(2,1)S(1)}, bf16[9,16,256]{2,1,0:T(8,128)(2,1)S(1)}, u32[]{:S(2)}, u32[]{:S(2)}) collective-permute-start(bf16[9,16,256]{2,1,0:T(8,128)(2,1)S(1)} %get-tuple-element.85), channel_id=1, source_target_pairs={{0,4},{1,5},{2,6},{3,7},{4,0},{5,1},{6,2},{7,3},{8,12},{9,13},{10,... | collective-permute-start | bytes 221192 | tf_op jit(solution)/shard_map/ppermute | solution.py:41
  145.6 6.1 %collective-permute-start.12 = (bf16[9,16,256]{2,1,0:T(8,128)(2,1)S(1)}, bf16[9,16,256]{2,1,0:T(8,128)(2,1)S(1)}, u32[]{:S(2)}, u32[]{:S(2)}) collective-permute-start(bf16[9,16,256]{2,1,0:T(8,128)(2,1)S(1)} %get-tuple-element.84), channel_id=1, source_target_pairs={{0,64},{1,65},{2,66},{3,67},{4,68},{5,69},{6,70},{7,71},{8,72},{9,... | collective-permute-start | bytes 221192 | tf_op jit(solution)/shard_map/ppermute | solution.py:41
  148.0 5.3 %collective-permute-start.13 = (bf16[9,16,256]{2,1,0:T(8,128)(2,1)S(1)}, bf16[9,16,256]{2,1,0:T(8,128)(2,1)S(1)}, u32[]{:S(2)}, u32[]{:S(2)}) collective-permute-start(bf16[9,16,256]{2,1,0:T(8,128)(2,1)S(1)} %get-tuple-element.85), channel_id=1, source_target_pairs={{0,68},{1,69},{2,70},{3,71},{4,64},{5,65},{6,66},{7,67},{8,76},{9,... | collective-permute-start | bytes 221192 | tf_op jit(solution)/shard_map/ppermute | solution.py:41
  153.4 4.3 %collective-permute-start.14 = (f32[9,16,256]{2,1,0:T(8,128)S(1)}, f32[9,16,256]{2,1,0:T(8,128)S(1)}, u32[]{:S(2)}, u32[]{:S(2)}) collective-permute-start(f32[9,16,256]{2,1,0:T(8,128)S(1)} %fusion.4), channel_id=1, source_target_pairs={{0,32},{1,33},{2,34},{3,35},{4,36},{5,37},{6,38},{7,39},{8,40},{9,... | collective-permute-start | bytes 442376 | tf_op jit(solution)/shard_map/ppermute | solution.py:41
  154.6 19.1 %collective-permute-start.10 = (bf16[4,256,256]{2,1,0:T(8,128)(2,1)}, bf16[4,256,256]{2,1,0:T(8,128)(2,1)S(1)}, u32[]{:S(2)}, u32[]{:S(2)}) collective-permute-start(bf16[4,256,256]{2,1,0:T(8,128)(2,1)} %get-tuple-element.71), channel_id=1, source_target_pairs={{0,96},{1,97},{2,98},{3,99},{4,100},{5,101},{6,102},{7,103},{8,104... | collective-permute-start | bytes 1572872 | tf_op jit(solution)/shard_map/ppermute | solution.py:41
  155.1 25.9 %collective-permute-start.9 = (bf16[4,256,256]{2,1,0:T(8,128)(2,1)S(1)}, bf16[4,256,256]{2,1,0:T(8,128)(2,1)S(1)}, u32[]{:S(2)}, u32[]{:S(2)}) collective-permute-start(bf16[4,256,256]{2,1,0:T(8,128)(2,1)S(1)} %copy-done.14), channel_id=1, source_target_pairs={{0,64},{1,65},{2,66},{3,67},{4,68},{5,69},{6,70},{7,71},{8,72},{9,... | collective-permute-start | bytes 1572872 | tf_op jit(solution)/shard_map/ppermute | solution.py:41
  169.6 15.8 %collective-permute-start.15 = (bf16[12,16,256]{2,1,0:T(8,128)(2,1)S(1)}, bf16[12,16,256]{2,1,0:T(8,128)(2,1)S(1)}, u32[]{:S(2)}, u32[]{:S(2)}) collective-permute-start(bf16[12,16,256]{2,1,0:T(8,128)(2,1)S(1)} %get-tuple-element.81), channel_id=1, source_target_pairs={{0,4},{1,5},{2,6},{3,7},{4,0},{5,1},{6,2},{7,3},{8,12},{9,13},{10,... | collective-permute-start | bytes 294920 | tf_op jit(solution)/shard_map/ppermute | solution.py:41
  171.0 14.4 %collective-permute-start.16 = (bf16[12,16,256]{2,1,0:T(8,128)(2,1)S(1)}, bf16[12,16,256]{2,1,0:T(8,128)(2,1)S(1)}, u32[]{:S(2)}, u32[]{:S(2)}) collective-permute-start(bf16[12,16,256]{2,1,0:T(8,128)(2,1)S(1)} %get-tuple-element.80), channel_id=1, source_target_pairs={{0,64},{1,65},{2,66},{3,67},{4,68},{5,69},{6,70},{7,71},{8,72},{9,... | collective-permute-start | bytes 294920 | tf_op jit(solution)/shard_map/ppermute | solution.py:41
  173.7 11.7 %collective-permute-start.17 = (bf16[12,16,256]{2,1,0:T(8,128)(2,1)S(1)}, bf16[12,16,256]{2,1,0:T(8,128)(2,1)S(1)}, u32[]{:S(2)}, u32[]{:S(2)}) collective-permute-start(bf16[12,16,256]{2,1,0:T(8,128)(2,1)S(1)} %get-tuple-element.81), channel_id=1, source_target_pairs={{0,68},{1,69},{2,70},{3,71},{4,64},{5,65},{6,66},{7,67},{8,76},{9,... | collective-permute-start | bytes 294920 | tf_op jit(solution)/shard_map/ppermute | solution.py:41
  173.7 7.3 %copy-start.7 = (bf16[4,256,256]{2,1,0:T(8,128)(2,1)}, bf16[4,256,256]{2,1,0:T(8,128)(2,1)S(1)}, u32[]{:S(2)}) copy-start(bf16[4,256,256]{2,1,0:T(8,128)(2,1)S(1)} %collective-permute-done.10.back3) | copy-start | bytes 1572868
  185.5 2.7 %collective-permute-start.18 = (f32[12,16,256]{2,1,0:T(8,128)S(1)}, f32[12,16,256]{2,1,0:T(8,128)S(1)}, u32[]{:S(2)}, u32[]{:S(2)}) collective-permute-start(f32[12,16,256]{2,1,0:T(8,128)S(1)} %fusion.2), channel_id=1, source_target_pairs={{0,32},{1,33},{2,34},{3,35},{4,36},{5,37},{6,38},{7,39},{8,40},{9,... | collective-permute-start | bytes 589832 | tf_op jit(solution)/shard_map/ppermute | solution.py:41
  (6 other events, 5.9 us)
Sparse Core Ops, SparseCore 0:
  16.0 55.0 all-gather.2

commit v4 on v3

--- a/solution.py
+++ b/solution.py
@@ -226,7 +226,7 @@
                 side, step = unit // 4, unit % 4
                 first = (x * 4 + step) * rows
                 down[z, first : first + rows, side * half : (side + 1) * half] = pieces[
-                    z * 4 + x, unit
+                    z * 4 + x, 8 + unit
                 ]
 
 
@@ -237,9 +237,7 @@
     ).astype(BF)
 
 
-def glow_kernel(
-    extent, loss_scale, meta, cot0, cot1, cot2, cot3, pieces, folded, part, raw, up, cot, sem
-):
+def fold_kernel(extent, meta, cot0, cot1, cot2, cot3, folded, raw, cot, sem):
     side = extent // 2
     quarter = side * side
     half = cot.shape[2]
@@ -250,7 +248,6 @@
     ]
     for copy in copies:
         copy.start()
-    gather_up(pieces, up)
     for copy in copies:
         copy.wait()
     images = folded.shape[1] // quarter
@@ -270,6 +267,13 @@
         return carry
 
     lax.fori_loop(0, images, one, 0)
+
+
+def glow_kernel(loss_scale, folded, pieces, part, up, held, sem):
+    copy = pltpu.make_async_copy(pieces.at[:, pl.ds(0, 8)], held, sem)
+    copy.start()
+    copy.wait()
+    gather_up(held, up)
     total = None
     for k in range(4):
         scaled = (folded[k].astype(F32) * loss_scale).astype(BF)
@@ -291,6 +295,7 @@
     grads,
     down,
     turned,
+    sums,
     windows,
     sem,
 ):
@@ -311,15 +316,23 @@
         turned[k] = (grad * kept).T.astype(BF)
     for copy in copies:
         copy.wait()
+    seen = set()
+    for v in range(16):
+        p, q = v // 4, v % 4
+        users = [k for k in range(4) if 0 <= p - k // 2 < 3 and 0 <= q - k % 2 < 3]
+        term = None
+        for part in range(2):
+            columns = slice(part * middle, (part + 1) * middle)
+            left = jnp.concatenate([turned[k, :, columns] for k in users])
+            piece = dot(left, windows[part, v], 1, 0)
+            term = piece if term is None else term + piece
+        for place, k in enumerate(users):
+            t = (p - k // 2) * 3 + q - k % 2
+            piece = term[place * half : (place + 1) * half]
+            sums[t] = sums[t] + piece if t in seen else piece
+            seen.add(t)
     for t in range(9):
-        total = None
-        for k in range(4):
-            v = (k // 2 + t // 3) * 4 + k % 2 + t % 3
-            for part in range(2):
-                columns = slice(part * middle, (part + 1) * middle)
-                term = dot(turned[k, :, columns], windows[part, v], 1, 0)
-                total = term if total is None else total + term
-        total = total.T.astype(BF)
+        total = sums[t].T.astype(BF)
         for f in range(32):
             z, y, x = f // 8, f // 4 % 2, f % 4
             grads[z * 4 + x, y * 9 + t] = total[f * rows : (f + 1) * rows, :]
@@ -499,10 +512,9 @@
     first = jnp.where(y == 0, packed, other)
     second = jnp.where(y == 0, other, packed)
     down_kept = jnp.where(core == 0, first[4:12], second[4:12])
-    up_two = jnp.concatenate([first[:4], second[:4]])
+    up_down = jnp.concatenate([first[:4], second[:4], down_kept])
     conv_two = jnp.concatenate([first[12:], second[12:]])
-    up_two = over_plane(jnp.broadcast_to(up_two, (16, *up_two.shape)))
-    down_kept = over_plane(jnp.broadcast_to(down_kept, (16, *down_kept.shape)))
+    up_down = over_plane(jnp.broadcast_to(up_down, (16, *up_down.shape)))
     conv_two = lax.all_gather(conv_two, "fsdp", axis_index_groups=PLANES)
 
     images_pair = send(images, "c")
@@ -542,23 +554,32 @@
     ready, mask, windows_own, windows_pair = lax.optimization_barrier(
         (meta, mask, windows_own, windows_pair)
     )
-    folded, glow_part = kernel_call(
-        functools.partial(glow_kernel, extent, loss_scale),
-        (
-            jax.ShapeDtypeStruct((4, low_rows, half), BF),
-            jax.ShapeDtypeStruct((low_rows, channels), F32),
-        ),
-        flops=8 * low_rows * channels * half,
-        moved_bytes=5 << 20,
+    folded = kernel_call(
+        functools.partial(fold_kernel, extent),
+        jax.ShapeDtypeStruct((4, low_rows, half), BF),
+        flops=0,
+        moved_bytes=3 << 20,
         scratch=(
             laned(extent, extent, half),
-            pltpu.VMEM((4, channels, half), BF),
             pltpu.VMEM((8 * most, pixels, half), BF),
             pltpu.SemaphoreType.DMA((4,)),
         ),
-        in_specs=[SCALARS] + [pl.BlockSpec(memory_space=pl.ANY)] * 4 + [WHOLE],
-        out_specs=(WHOLE, WHOLE),
-    )(ready, *arrived, up_two)
+        in_specs=[SCALARS] + [pl.BlockSpec(memory_space=pl.ANY)] * 4,
+        out_specs=WHOLE,
+    )(ready, *arrived)
+    glow_part = kernel_call(
+        functools.partial(glow_kernel, loss_scale),
+        jax.ShapeDtypeStruct((low_rows, channels), F32),
+        flops=8 * low_rows * channels * half,
+        moved_bytes=3 << 20,
+        scratch=(
+            pltpu.VMEM((4, channels, half), BF),
+            pltpu.VMEM((16, 8, rows, half), BF),
+            pltpu.SemaphoreType.DMA,
+        ),
+        in_specs=[WHOLE, pl.BlockSpec(memory_space=pl.ANY)],
+        out_specs=WHOLE,
+    )(folded, up_down)
     glow_got = send(glow_part, "c")
 
     glow, conv_grads = kernel_call(
@@ -572,12 +593,13 @@
         scratch=(
             pltpu.VMEM((4, half, channels), BF),
             pltpu.VMEM((4, half, low_rows), BF),
+            pltpu.VMEM((9, half, channels), F32),
             pltpu.VMEM((2, *windows_own.shape), BF),
             pltpu.SemaphoreType.DMA((2,)),
         ),
         in_specs=[WHOLE] * 5 + [pl.BlockSpec(memory_space=pl.ANY)] * 2,
         out_specs=(WHOLE, WHOLE),
-    )(mask, glow_part, glow_got, folded, down_kept, windows_own, windows_pair)
+    )(mask, glow_part, glow_got, folded, up_down, windows_own, windows_pair)
     conv_grads = over_plane(conv_grads)
     glow, windows_own, windows_pair = lax.optimization_barrier((glow, windows_own, windows_pair))
 
@@ -593,7 +615,7 @@
         scratch=(pltpu.VMEM((9, channels, half), BF), pltpu.VMEM((4, half, channels), BF)),
         in_specs=[WHOLE] * 7,
         out_specs=(WHOLE,) * 3,
-    )(mask, conv_two, down_kept, windows_own, windows_pair, residual_own, residual_pair)
+    )(mask, conv_two, up_down, windows_own, windows_pair, residual_own, residual_pair)
     low_got = send(low_part, "c")
 
     *returning, grads = kernel_call(
@@ -613,26 +635,26 @@
         ),
         in_specs=[SCALARS] + [WHOLE] * 8,
         out_specs=(WHOLE,) * 5,
-    )(meta, mask, low_part, low_got, wide, skip, glow, folded, up_two)
+    )(meta, mask, low_part, low_got, wide, skip, glow, folded, up_down)
     returned = over_dp(returning)
     grads = over_plane(grads)
 
     conv_sum = jnp.sum(conv_grads.astype(F32), axis=0).reshape(2, 9, rows, half)
-    conv_sum, beside = lax.optimization_barrier((conv_sum, returned[1]))
-    returned = (returned[0], beside, *returned[2:])
-
-    def by_core(own, pair):
-        return jnp.where(core == 0, jnp.stack([own, pair]), jnp.stack([pair, own]))
-
-    out_conv = by_core(*over_column(conv_sum, y)).transpose(2, 1, 0, 3)
-    out_conv = out_conv.reshape(rows, 9, channels)
     grads_sum = jnp.sum(grads.astype(F32), axis=0)
     up_sum, down_sum = grads_sum[:8].reshape(2, 4, rows, half), grads_sum[8:]
-    shares = jnp.concatenate([up_sum, jnp.broadcast_to(down_sum, (2, *down_sum.shape))], axis=1)
-    shares, out_conv = lax.optimization_barrier((shares, out_conv))
+    down_sum = jnp.broadcast_to(down_sum, (2, *down_sum.shape))
+    shares = jnp.concatenate([conv_sum, up_sum, down_sum], axis=1)
+    shares, returned = lax.optimization_barrier((shares, returned))
     own, pair = over_column(shares, y)
-    out_up = by_core(own[:4], pair[:4]).transpose(2, 1, 0, 3).reshape(rows, 4 * channels)
-    out_down = jnp.where(y == core, own[4:], pair[4:])
+
+    def by_core(first, last):
+        parts = (own[first:last], pair[first:last])
+        both = jnp.where(core == 0, jnp.stack(parts), jnp.stack(parts[::-1]))
+        return both.transpose(2, 1, 0, 3)
+
+    out_conv = by_core(0, 9).reshape(rows, 9, channels)
+    out_up = by_core(9, 13).reshape(rows, 4 * channels)
+    out_down = jnp.where(y == core, own[13:], pair[13:])
     out_down = out_down.reshape(2, 4 * rows, half).transpose(1, 0, 2).reshape(4 * rows, channels)
 
     block_out = kernel_call(

time: 197 us -> 187 us (0.949)
  blocking collectives: 23.2 us -> 0 us
  waiting for transfers between devices: 40.6 us -> 54.4 us
  Pallas kernels: 56.9 us -> 61 us
  starting transfers between devices: 42.8 us -> 40.8 us
    all_to_all x1 -> x0, blocking collectives: 23.2 us -> none  [over_plane(): lax.all_to_all(blocks, 'fsdp', split_axis=0, concat_axis=0, axis_index_gr...]
    all_to_all x3, waiting for transfers between devices: 15.5 us -> 36.5 us  [over_plane(): lax.all_to_all(blocks, 'fsdp', split_axis=0, concat_axis=0, axis_index_gr...]
    ppermute x19 -> x15, waiting for transfers between devices: 25.1 us -> 17.9 us  [send(): return lax.ppermute(value, AXES, STEP[move])]
    ppermute x19 -> x15, starting transfers between devices: 25.9 us -> 21.4 us  [send(): return lax.ppermute(value, AXES, STEP[move])]
    pallas_call x1 -> x2, Pallas kernels: 4.93 us -> 7.73 us  [the longest x1 4.15 us: per_device(): kernel_call(functools.partial(glow_kernel, loss_scale), jax.ShapeDtypeStr...]
    all_to_all x3, starting transfers between devices: 16.9 us -> 19.3 us  [over_plane(): lax.all_to_all(blocks, 'fsdp', split_axis=0, concat_axis=0, axis_index_gr...]
    unnamed x30 -> x24, local copies, waits for them, and re-layouts: 4.8 us -> 3.41 us
  transfers between devices with their start and end apart: 23 -> 19, of which waited for: 11 -> 10; matrix products, arithmetic and copies ran while one was open for 5% -> 4% of each run, Pallas kernels for 29% -> 33%
where the time goes in v4:
time: 187 us
  Pallas kernels  61 us (33%)
  waiting for transfers between devices  54.4 us (29%)
  starting transfers between devices  40.8 us (22%)
  between operations  14.5 us (8%)
  local copies, waits for them, and re-layouts  12 us (6%)
  other arithmetic  4.02 us (2%)
    all_to_all x3, waiting for transfers between devices, over_plane(): lax.all_to_all(blocks, 'fsdp', split_axis=0, concat_axis=0, axis_index_gr...  36.5 us
    ppermute x15, starting transfers between devices, send(): return lax.ppermute(value, AXES, STEP[move])  21.4 us
    all_to_all x3, starting transfers between devices, over_plane(): lax.all_to_all(blocks, 'fsdp', split_axis=0, concat_axis=0, axis_index_gr...  19.3 us
    ppermute x15, waiting for transfers between devices, send(): return lax.ppermute(value, AXES, STEP[move])  17.9 us
    pallas_call x2, Pallas kernels, normed_windows(): kernel_call(functools.partial(norm_kernel, extent), (jax.ShapeDtypeStruct...  13 us
    pallas_call x1, Pallas kernels, per_device(): kernel_call(functools.partial(grad_conv_kernel, loss_scale), (jax.ShapeDt...  12.9 us
    pallas_call x1, Pallas kernels, per_device(): kernel_call(conv_kernel, (jax.ShapeDtypeStruct((4, low_rows, half), F32),...  12.6 us
    pallas_call x1, Pallas kernels, per_device(): kernel_call(functools.partial(output_kernel, extent, loss_scale), (*(bloc...  8.11 us
  transfers between devices with their start and end apart: 19, of which 10 were waited for; matrix products, arithmetic and copies ran while one was open for 4% of the time, Pallas kernels for 33%

profile of v4, /device:TPU:1, one launch (start us, length us, event | category | flops | bytes accessed | tf_op | source)
XLA Modules:
  0.0 186.7 jit_solution(17048487682638088136)
XLA Ops:
  9.1 2.2 %collective-permute-start.2 = (bf16[21,16,256]{2,1,0:T(8,128)(2,1)S(1)}, bf16[21,16,256]{2,1,0:T(8,128)(2,1)S(1)}, u32[]{:S(2)}, u32[]{:S(2)}) collective-permute-start(bf16[21,16,256]{2,1,0:T(8,128)(2,1)S(1)} %pad_maximum_fusion.1), channel_id=1, source_target_pairs={{0,4},{1,5},{2,6},{3,7},{4,0},{5,1},{6,2},{7,3},{8,12},{9,13},{10,... | collective-permute-start | bytes 516104 | tf_op jit(solution)/shard_map/ppermute | solution.py:41
  11.3 3.1 %shard_map.140 = (bf16[4,256,256]{2,1,0:T(8,128)(2,1)}, bf16[4,256,256]{2,1,0:T(8,128)(2,1)}, bf16[4,256,256]{2,1,0:T(8,128)(2,1)}, bf16[4,256,256]{2,1,0:T(8,128)(2,1)}) custom-call(s32[1]{0:T(128)} %bitcast.number, bf16[8,256,512]{2,1,0:T(8,128)(2,1)} %bitcast.72), custom_call_target="tpu_custom_call" | custom-call | bytes 4194304 | tf_op jit(solution)/shard_map/pallas_call | solution.py:502
  15.8 1.6 broadcast_in_dim.72
  17.4 8.0 %all-to-all-start = ((bf16[16,16,16,256]{3,2,1,0:T(8,128)(2,1)}), bf16[16,16,16,256]{3,2,1,0:T(8,128)(2,1)S(1)}, u32[]{:S(2)}, u32[]{:S(2)}) async-start(bf16[16,16,16,256]{3,2,1,0:T(8,128)(2,1)} %broadcast_in_dim.72), calls=%async_computation | async-start | bytes 4194304 | tf_op jit(solution)/shard_map/all_to_all | solution.py:59
  25.5 1.9 %collective-permute-start = (s32[4,2]{0,1:T(2,128)S(1)}, s32[4,2]{0,1:T(2,128)S(1)}, u32[]{:S(2)}, u32[]{:S(2)}) collective-permute-start(s32[4,2]{0,1:T(2,128)S(1)} %pad_add_fusion.2), channel_id=1, source_target_pairs={{0,32},{1,33},{2,34},{3,35},{4,36},{5,37},{6,38},{7,39},{8,40},{9,... | collective-permute-start | bytes 104 | tf_op jit(solution)/shard_map/ppermute | solution.py:41
  29.0 2.9 %collective-permute-start.4 = (bf16[4,256,256]{2,1,0:T(8,128)(2,1)}, bf16[4,256,256]{2,1,0:T(8,128)(2,1)}, u32[]{:S(2)}, u32[]{:S(2)}) collective-permute-start(bf16[4,256,256]{2,1,0:T(8,128)(2,1)} %get-tuple-element.49), channel_id=1, source_target_pairs={{0,64},{1,65},{2,66},{3,67},{4,68},{5,69},{6,70},{7,71},{8,72},{9,... | collective-permute-start | bytes 1572872 | tf_op jit(solution)/shard_map/ppermute | solution.py:41
  34.5 6.5 %shard_map.138 = (bf16[16,256,512]{2,1,0:T(8,128)(2,1)}, bf16[4,256,256]{2,1,0:T(8,128)(2,1)}) custom-call(s32[32]{0:T(128)} %concatenate.37.meta, bf16[4,256,512]{2,1,0:T(8,128)(2,1)} %bitcast.74, f32[1,512]{1,0:T(1,128)} %bitcast.82, f32[1,512]{1,0:T(1,128)} %bitcast.84), custom_call_target="tpu_custom_call" | custom-call | flops 20971520 | bytes 6291456 | tf_op jit(solution)/shard_map/pallas_call | solution.py:187
  41.0 6.5 %shard_map.139 = (bf16[16,256,512]{2,1,0:T(8,128)(2,1)}, bf16[4,256,256]{2,1,0:T(8,128)(2,1)}) custom-call(s32[32]{0:T(128)} %concatenate.39.meta, bf16[4,256,512]{2,1,0:T(8,128)(2,1)} %bitcast.18.image, f32[1,512]{1,0:T(1,128)} %bitcast.83, f32[1,512]{1,0:T(1,128)} %bitcast.85), custom_call_target="tpu_custom_call" | custom-call | flops 20971520 | bytes 6291456 | tf_op jit(solution)/shard_map/pallas_call | solution.py:187
  48.3 7.4 %collective-permute-done.5.cot3 = bf16[4,256,256]{2,1,0:T(8,128)(2,1)} collective-permute-done((bf16[4,256,256]{2,1,0:T(8,128)(2,1)}, bf16[4,256,256]{2,1,0:T(8,128)(2,1)}, u32[]{:S(2)}, u32[]{:S(2)}) %collective-permute-start.5) | collective-permute-done | bytes 524320 | tf_op jit(solution)/shard_map/ppermute | solution.py:41
  55.8 3.6 %shard_map.141.folded = bf16[4,512,256]{2,1,0:T(8,128)(2,1)} custom-call(s32[32]{0:T(128)} %concatenate.35.meta, bf16[4,256,256]{2,1,0:T(8,128)(2,1)} %get-tuple-element.47.cot0, bf16[4,256,256]{2,1,0:T(8,128)(2,1)} %collective-permute-done.3.cot1, bf16[4,256,256]{2,1,0:T(8,128)(2,1)} %collective-permute-done.4.cot2, ...), custom_call_target="tpu_custom_call" | custom-call | bytes 3145728 | tf_op jit(solution)/shard_map/pallas_call | solution.py:557
  59.4 1.3 copy-done.1
  60.7 4.2 %shard_map.142.own = f32[512,512]{1,0:T(8,128)} custom-call(bf16[4,512,256]{2,1,0:T(8,128)(2,1)} %shard_map.141.folded, bf16[16,16,16,256]{3,2,1,0:T(8,128)(2,1)} %copy-done.1), custom_call_target="tpu_custom_call" | custom-call | flops 536870912 | bytes 3145728 | tf_op jit(solution)/shard_map/pallas_call | solution.py:570
  65.0 2.8 %collective-permute-done.6.got = f32[512,512]{1,0:T(8,128)S(1)} collective-permute-done((f32[512,512]{1,0:T(8,128)}, f32[512,512]{1,0:T(8,128)S(1)}, u32[]{:S(2)}, u32[]{:S(2)}) %collective-permute-start.6) | collective-permute-done | bytes 1048608 | tf_op jit(solution)/shard_map/ppermute | solution.py:41
  67.8 1.0 copy-done.11
  68.8 12.9 %shard_map.143 = (bf16[512,512]{1,0:T(8,128)(2,1)}, bf16[16,18,16,256]{3,2,1,0:T(8,128)(2,1)}) custom-call(f32[512,128]{1,0:T(8,128)} %broadcast_in_dim.69.mask, f32[512,512]{1,0:T(8,128)} %shard_map.142.own, f32[512,512]{1,0:T(8,128)} %copy-done.11, bf16[4,512,256]{2,1,0:T(8,128)(2,1)} %shard_map.141.folded, bf16[16,16,16,256]{3,2,1,0:T(8,128)(2,1)} %copy-done.1, ...), custom_call_target="tpu_custom_call" | custom-call | flops 5368709120 | bytes 15728640 | tf_op jit(solution)/shard_map/pallas_call | solution.py:585
  81.7 6.9 %all-to-all-start.1 = ((bf16[16,18,16,256]{3,2,1,0:T(8,128)(2,1)}), bf16[16,18,16,256]{3,2,1,0:T(8,128)(2,1)S(1)}, u32[]{:S(2)}, u32[]{:S(2)}) async-start(bf16[16,18,16,256]{3,2,1,0:T(8,128)(2,1)} %get-tuple-element.54), calls=%async_computation.1 | async-start | bytes 4718592 | tf_op jit(solution)/shard_map/all_to_all | solution.py:59
  88.6 12.6 %shard_map.144 = (f32[4,512,256]{2,1,0:T(8,128)}, bf16[4,512,256]{2,1,0:T(8,128)(2,1)}, f32[512,512]{1,0:T(8,128)}) custom-call(f32[512,128]{1,0:T(8,128)} %broadcast_in_dim.69.mask, bf16[16,18,16,256]{3,2,1,0:T(8,128)(2,1)} %bitcast.92, bf16[16,16,16,256]{3,2,1,0:T(8,128)(2,1)} %copy-done.1, bf16[16,256,512]{2,1,0:T(8,128)(2,1)} %get-tuple-element.56.windows_own, ...), custom_call_target="tpu_custom_call" | custom-call | flops 5368709120 | bytes 18874368 | tf_op jit(solution)/shard_map/pallas_call | solution.py:606
  101.6 2.5 %collective-permute-done.7.got = f32[512,512]{1,0:T(8,128)S(1)} collective-permute-done((f32[512,512]{1,0:T(8,128)}, f32[512,512]{1,0:T(8,128)S(1)}, u32[]{:S(2)}, u32[]{:S(2)}) %collective-permute-start.7) | collective-permute-done | bytes 1048608 | tf_op jit(solution)/shard_map/ppermute | solution.py:41
  104.1 1.0 copy-done.2
  105.1 8.1 %shard_map.145 = (bf16[4,256,256]{2,1,0:T(8,128)(2,1)}, bf16[4,256,256]{2,1,0:T(8,128)(2,1)}, bf16[4,256,256]{2,1,0:T(8,128)(2,1)}, bf16[4,256,256]{2,1,0:T(8,128)(2,1)}, bf16[16,16,16,256]{3,2,1,0:T(8,128)(2,1)}) custom-call(s32[32]{0:T(128)} %concatenate.35.meta, f32[512,128]{1,0:T(8,128)} %broadcast_in_dim.69.mask, f32[512,512]{1,0:T(8,128)} %get-tuple-element.60.own, ...), custom_call_target="tpu_custom_call" | custom-call | flops 1610612736 | bytes 14680064 | tf_op jit(solution)/shard_map/pallas_call | solution.py:621
  113.3 11.8 %all-to-all-done.1 = bf16[16,18,16,256]{3,2,1,0:T(8,128)(2,1)S(1)} async-done(((bf16[16,18,16,256]{3,2,1,0:T(8,128)(2,1)}), bf16[16,18,16,256]{3,2,1,0:T(8,128)(2,1)S(1)}, u32[]{:S(2)}, u32[]{:S(2)}) %all-to-all-start.1) | async-done | bytes 2359328 | tf_op jit(solution)/shard_map/all_to_all | solution.py:59
  125.0 4.4 %all-to-all-start.2 = ((bf16[16,16,16,256]{3,2,1,0:T(8,128)(2,1)}), bf16[16,16,16,256]{3,2,1,0:T(8,128)(2,1)}, u32[]{:S(2)}, u32[]{:S(2)}) async-start(bf16[16,16,16,256]{3,2,1,0:T(8,128)(2,1)} %get-tuple-element.64), calls=%async_computation.2 | async-start | bytes 4194304 | tf_op jit(solution)/shard_map/all_to_all | solution.py:59
  129.8 4.2 %collective-permute-start.10 = (bf16[4,256,256]{2,1,0:T(8,128)(2,1)}, bf16[4,256,256]{2,1,0:T(8,128)(2,1)S(1)}, u32[]{:S(2)}, u32[]{:S(2)}) collective-permute-start(bf16[4,256,256]{2,1,0:T(8,128)(2,1)} %get-tuple-element.68), channel_id=1, source_target_pairs={{0,96},{1,97},{2,98},{3,99},{4,100},{5,101},{6,102},{7,103},{8,104... | collective-permute-start | bytes 1572872 | tf_op jit(solution)/shard_map/ppermute | solution.py:41
  134.3 24.7 %all-to-all-done.2 = bf16[16,16,16,256]{3,2,1,0:T(8,128)(2,1)} async-done(((bf16[16,16,16,256]{3,2,1,0:T(8,128)(2,1)}), bf16[16,16,16,256]{3,2,1,0:T(8,128)(2,1)}, u32[]{:S(2)}, u32[]{:S(2)}) %all-to-all-start.2) | async-done | bytes 2097184 | tf_op jit(solution)/shard_map/all_to_all | solution.py:59
  159.0 1.9 %convert_reduce_fusion.1 = f32[16,16,256]{2,1,0:T(8,128)S(1)} fusion(bf16[16,16,16,256]{3,2,1,0:T(8,128)(2,1)} %all-to-all-done.2), kind=kLoop, calls=%fused_computation.1 | loop fusion | flops 2031616 | bytes 2359296 | tf_op jit(solution)/shard_map/reduce_sum | solution.py:643
  161.1 1.4 collective-permute-start.11
  162.5 2.6 %collective-permute-start.12 = (bf16[21,16,256]{2,1,0:T(8,128)(2,1)S(1)}, bf16[21,16,256]{2,1,0:T(8,128)(2,1)S(1)}, u32[]{:S(2)}, u32[]{:S(2)}) collective-permute-start(bf16[21,16,256]{2,1,0:T(8,128)(2,1)S(1)} %get-tuple-element.78), channel_id=1, source_target_pairs={{0,64},{1,65},{2,66},{3,67},{4,68},{5,69},{6,70},{7,71},{8,72},{9,... | collective-permute-start | bytes 516104 | tf_op jit(solution)/shard_map/ppermute | solution.py:41
  165.2 3.6 %shard_map.146 = f32[8,256,512]{2,1,0:T(8,128)} custom-call(s32[1]{0:T(128)} %bitcast.number, bf16[4,256,256]{2,1,0:T(8,128)(2,1)} %get-tuple-element.69.back0, bf16[4,256,256]{2,1,0:T(8,128)(2,1)} %copy-done.5, bf16[4,256,256]{2,1,0:T(8,128)(2,1)} %copy-done.6, bf16[4,256,256]{2,1,0:T(8,128)(2,1)} %copy-done.4), custom_call_target="tpu_custom_call" | custom-call | bytes 6291456 | tf_op jit(solution)/shard_map/pallas_call | solution.py:660
  168.8 1.6 collective-permute-done.12
  170.5 1.2 collective-permute-done.13
  171.7 4.5 %collective-permute-start.14 = (f32[21,16,256]{2,1,0:T(8,128)S(1)}, f32[21,16,256]{2,1,0:T(8,128)S(1)}, u32[]{:S(2)}, u32[]{:S(2)}) collective-permute-start(f32[21,16,256]{2,1,0:T(8,128)S(1)} %fusion.1), channel_id=1, source_target_pairs={{0,32},{1,33},{2,34},{3,35},{4,36},{5,37},{6,38},{7,39},{8,40},{9,... | collective-permute-start | bytes 1032200 | tf_op jit(solution)/shard_map/ppermute | solution.py:41
  176.2 1.3 collective-permute-done.14
  (93 shorter events, 12.0 us)
Async XLA Ops:
  7.2 1.0 copy-start
  7.2 81.4 %all-gather.3.cloned.1.call-start = ((), (), s32[]{:S(2)}) async-start(), calls=%async_computation.3 | async-start | bytes 2506752 | tf_op jit(solution)/shard_map/all_gather | solution.py:518
  9.1 5.9 %collective-permute-start.2 = (bf16[21,16,256]{2,1,0:T(8,128)(2,1)S(1)}, bf16[21,16,256]{2,1,0:T(8,128)(2,1)S(1)}, u32[]{:S(2)}, u32[]{:S(2)}) collective-permute-start(bf16[21,16,256]{2,1,0:T(8,128)(2,1)S(1)} %pad_maximum_fusion.1), channel_id=1, source_target_pairs={{0,4},{1,5},{2,6},{3,7},{4,0},{5,1},{6,2},{7,3},{8,12},{9,13},{10,... | collective-permute-start | bytes 516104 | tf_op jit(solution)/shard_map/ppermute | solution.py:41
  17.4 8.0 %copy-start.7 = (s32[4,1]{0,1:T(1,128)S(1)}, s32[4,1]{0,1:T(1,128)}, u32[]{:S(2)}) copy-start(s32[4,1]{0,1:T(1,128)} %param.12) | copy-start | bytes 52
  17.4 8.0 %copy-start.8 = (s32[4]{0:T(128)S(1)}, s32[4]{0:T(128)}, u32[]{:S(2)}) copy-start(s32[4]{0:T(128)} %param.13) | copy-start | bytes 52
  17.4 10.0 %copy-start.3 = (bf16[4,16,16,512]{3,2,1,0:T(8,128)(2,1)S(1)}, bf16[4,16,16,512]{3,2,1,0:T(8,128)(2,1)}, u32[]{:S(2)}) copy-start(bf16[4,16,16,512]{3,2,1,0:T(8,128)(2,1)} %param.11) | copy-start | bytes 3145732
  17.4 10.8 %copy-start.9 = (s32[8]{0:T(128)S(1)}, s32[8]{0:T(128)}, u32[]{:S(2)}) copy-start(s32[8]{0:T(128)} %param.14) | copy-start | bytes 100
  17.4 10.8 %copy-start.10 = (s32[8]{0:T(128)S(1)}, s32[8]{0:T(128)}, u32[]{:S(2)}) copy-start(s32[8]{0:T(128)} %param.15) | copy-start | bytes 100
  17.4 41.9 %all-to-all-start = ((bf16[16,16,16,256]{3,2,1,0:T(8,128)(2,1)}), bf16[16,16,16,256]{3,2,1,0:T(8,128)(2,1)S(1)}, u32[]{:S(2)}, u32[]{:S(2)}) async-start(bf16[16,16,16,256]{3,2,1,0:T(8,128)(2,1)} %broadcast_in_dim.72), calls=%async_computation | async-start | bytes 4194304 | tf_op jit(solution)/shard_map/all_to_all | solution.py:59
  25.5 2.7 %collective-permute-start = (s32[4,2]{0,1:T(2,128)S(1)}, s32[4,2]{0,1:T(2,128)S(1)}, u32[]{:S(2)}, u32[]{:S(2)}) collective-permute-start(s32[4,2]{0,1:T(2,128)S(1)} %pad_add_fusion.2), channel_id=1, source_target_pairs={{0,32},{1,33},{2,34},{3,35},{4,36},{5,37},{6,38},{7,39},{8,40},{9,... | collective-permute-start | bytes 104 | tf_op jit(solution)/shard_map/ppermute | solution.py:41
  27.4 13.6 %collective-permute-start.1 = (bf16[4,16,16,512]{3,2,1,0:T(8,128)(2,1)S(1)}, bf16[4,16,16,512]{3,2,1,0:T(8,128)(2,1)}, u32[]{:S(2)}, u32[]{:S(2)}) collective-permute-start(bf16[4,16,16,512]{3,2,1,0:T(8,128)(2,1)S(1)} %copy-done.3), channel_id=1, source_target_pairs={{0,32},{1,33},{2,34},{3,35},{4,36},{5,37},{6,38},{7,39},{8,40},{9,... | collective-permute-start | bytes 3145736 | tf_op jit(solution)/shard_map/ppermute | solution.py:41
  28.7 19.6 %collective-permute-start.3 = (bf16[4,256,256]{2,1,0:T(8,128)(2,1)}, bf16[4,256,256]{2,1,0:T(8,128)(2,1)}, u32[]{:S(2)}, u32[]{:S(2)}) collective-permute-start(bf16[4,256,256]{2,1,0:T(8,128)(2,1)} %get-tuple-element.48), channel_id=1, source_target_pairs={{0,32},{1,33},{2,34},{3,35},{4,36},{5,37},{6,38},{7,39},{8,40},{9,... | collective-permute-start | bytes 1572872 | tf_op jit(solution)/shard_map/ppermute | solution.py:41
  29.0 19.3 %collective-permute-start.4 = (bf16[4,256,256]{2,1,0:T(8,128)(2,1)}, bf16[4,256,256]{2,1,0:T(8,128)(2,1)}, u32[]{:S(2)}, u32[]{:S(2)}) collective-permute-start(bf16[4,256,256]{2,1,0:T(8,128)(2,1)} %get-tuple-element.49), channel_id=1, source_target_pairs={{0,64},{1,65},{2,66},{3,67},{4,68},{5,69},{6,70},{7,71},{8,72},{9,... | collective-permute-start | bytes 1572872 | tf_op jit(solution)/shard_map/ppermute | solution.py:41
  32.0 23.8 %collective-permute-start.5 = (bf16[4,256,256]{2,1,0:T(8,128)(2,1)}, bf16[4,256,256]{2,1,0:T(8,128)(2,1)}, u32[]{:S(2)}, u32[]{:S(2)}) collective-permute-start(bf16[4,256,256]{2,1,0:T(8,128)(2,1)} %get-tuple-element.50), channel_id=1, source_target_pairs={{0,96},{1,97},{2,98},{3,99},{4,100},{5,101},{6,102},{7,103},{8,104... | collective-permute-start | bytes 1572872 | tf_op jit(solution)/shard_map/ppermute | solution.py:41
  59.3 1.3 copy-start.1
  64.8 3.0 %collective-permute-start.6 = (f32[512,512]{1,0:T(8,128)}, f32[512,512]{1,0:T(8,128)S(1)}, u32[]{:S(2)}, u32[]{:S(2)}) collective-permute-start(f32[512,512]{1,0:T(8,128)} %shard_map.142.own), channel_id=1, source_target_pairs={{0,32},{1,33},{2,34},{3,35},{4,36},{5,37},{6,38},{7,39},{8,40},{9,... | collective-permute-start | bytes 3145736 | tf_op jit(solution)/shard_map/ppermute | solution.py:41
  67.8 1.0 copy-start.11
  81.7 43.3 %all-to-all-start.1 = ((bf16[16,18,16,256]{3,2,1,0:T(8,128)(2,1)}), bf16[16,18,16,256]{3,2,1,0:T(8,128)(2,1)S(1)}, u32[]{:S(2)}, u32[]{:S(2)}) async-start(bf16[16,18,16,256]{3,2,1,0:T(8,128)(2,1)} %get-tuple-element.54), calls=%async_computation.1 | async-start | bytes 4718592 | tf_op jit(solution)/shard_map/all_to_all | solution.py:59
  101.2 3.0 %collective-permute-start.7 = (f32[512,512]{1,0:T(8,128)}, f32[512,512]{1,0:T(8,128)S(1)}, u32[]{:S(2)}, u32[]{:S(2)}) collective-permute-start(f32[512,512]{1,0:T(8,128)} %get-tuple-element.60.own), channel_id=1, source_target_pairs={{0,32},{1,33},{2,34},{3,35},{4,36},{5,37},{6,38},{7,39},{8,40},{9,... | collective-permute-start | bytes 3145736 | tf_op jit(solution)/shard_map/ppermute | solution.py:41
  104.1 1.0 copy-start.2
  125.0 33.9 %all-to-all-start.2 = ((bf16[16,16,16,256]{3,2,1,0:T(8,128)(2,1)}), bf16[16,16,16,256]{3,2,1,0:T(8,128)(2,1)}, u32[]{:S(2)}, u32[]{:S(2)}) async-start(bf16[16,16,16,256]{3,2,1,0:T(8,128)(2,1)} %get-tuple-element.64), calls=%async_computation.2 | async-start | bytes 4194304 | tf_op jit(solution)/shard_map/all_to_all | solution.py:59
  129.8 31.1 %collective-permute-start.10 = (bf16[4,256,256]{2,1,0:T(8,128)(2,1)}, bf16[4,256,256]{2,1,0:T(8,128)(2,1)S(1)}, u32[]{:S(2)}, u32[]{:S(2)}) collective-permute-start(bf16[4,256,256]{2,1,0:T(8,128)(2,1)} %get-tuple-element.68), channel_id=1, source_target_pairs={{0,96},{1,97},{2,98},{3,99},{4,100},{5,101},{6,102},{7,103},{8,104... | collective-permute-start | bytes 1572872 | tf_op jit(solution)/shard_map/ppermute | solution.py:41
  134.1 27.0 %collective-permute-start.8 = (bf16[4,256,256]{2,1,0:T(8,128)(2,1)}, bf16[4,256,256]{2,1,0:T(8,128)(2,1)S(1)}, u32[]{:S(2)}, u32[]{:S(2)}) collective-permute-start(bf16[4,256,256]{2,1,0:T(8,128)(2,1)} %get-tuple-element.66), channel_id=1, source_target_pairs={{0,32},{1,33},{2,34},{3,35},{4,36},{5,37},{6,38},{7,39},{8,40},{9,... | collective-permute-start | bytes 1572872 | tf_op jit(solution)/shard_map/ppermute | solution.py:41
  134.1 27.0 %collective-permute-start.9 = (bf16[4,256,256]{2,1,0:T(8,128)(2,1)}, bf16[4,256,256]{2,1,0:T(8,128)(2,1)S(1)}, u32[]{:S(2)}, u32[]{:S(2)}) collective-permute-start(bf16[4,256,256]{2,1,0:T(8,128)(2,1)} %get-tuple-element.67), channel_id=1, source_target_pairs={{0,64},{1,65},{2,66},{3,67},{4,68},{5,69},{6,70},{7,71},{8,72},{9,... | collective-permute-start | bytes 1572872 | tf_op jit(solution)/shard_map/ppermute | solution.py:41
  161.0 4.2 %copy-start.4 = (bf16[4,256,256]{2,1,0:T(8,128)(2,1)}, bf16[4,256,256]{2,1,0:T(8,128)(2,1)S(1)}, u32[]{:S(2)}) copy-start(bf16[4,256,256]{2,1,0:T(8,128)(2,1)S(1)} %collective-permute-done.10.back3) | copy-start | bytes 1572868
  161.0 4.2 %copy-start.5 = (bf16[4,256,256]{2,1,0:T(8,128)(2,1)}, bf16[4,256,256]{2,1,0:T(8,128)(2,1)S(1)}, u32[]{:S(2)}) copy-start(bf16[4,256,256]{2,1,0:T(8,128)(2,1)S(1)} %collective-permute-done.8.back1) | copy-start | bytes 1572868
  161.0 4.1 %copy-start.6 = (bf16[4,256,256]{2,1,0:T(8,128)(2,1)}, bf16[4,256,256]{2,1,0:T(8,128)(2,1)S(1)}, u32[]{:S(2)}) copy-start(bf16[4,256,256]{2,1,0:T(8,128)(2,1)S(1)} %collective-permute-done.9.back2) | copy-start | bytes 1572868
  161.1 7.7 %collective-permute-start.11 = (bf16[21,16,256]{2,1,0:T(8,128)(2,1)S(1)}, bf16[21,16,256]{2,1,0:T(8,128)(2,1)S(1)}, u32[]{:S(2)}, u32[]{:S(2)}) collective-permute-start(bf16[21,16,256]{2,1,0:T(8,128)(2,1)S(1)} %get-tuple-element.79), channel_id=1, source_target_pairs={{0,4},{1,5},{2,6},{3,7},{4,0},{5,1},{6,2},{7,3},{8,12},{9,13},{10,... | collective-permute-start | bytes 516104 | tf_op jit(solution)/shard_map/ppermute | solution.py:41
  162.5 7.9 %collective-permute-start.12 = (bf16[21,16,256]{2,1,0:T(8,128)(2,1)S(1)}, bf16[21,16,256]{2,1,0:T(8,128)(2,1)S(1)}, u32[]{:S(2)}, u32[]{:S(2)}) collective-permute-start(bf16[21,16,256]{2,1,0:T(8,128)(2,1)S(1)} %get-tuple-element.78), channel_id=1, source_target_pairs={{0,64},{1,65},{2,66},{3,67},{4,68},{5,69},{6,70},{7,71},{8,72},{9,... | collective-permute-start | bytes 516104 | tf_op jit(solution)/shard_map/ppermute | solution.py:41
  165.2 6.5 %collective-permute-start.13 = (bf16[21,16,256]{2,1,0:T(8,128)(2,1)S(1)}, bf16[21,16,256]{2,1,0:T(8,128)(2,1)S(1)}, u32[]{:S(2)}, u32[]{:S(2)}) collective-permute-start(bf16[21,16,256]{2,1,0:T(8,128)(2,1)S(1)} %get-tuple-element.79), channel_id=1, source_target_pairs={{0,68},{1,69},{2,70},{3,71},{4,64},{5,65},{6,66},{7,67},{8,76},{9,... | collective-permute-start | bytes 516104 | tf_op jit(solution)/shard_map/ppermute | solution.py:41
  171.7 5.7 %collective-permute-start.14 = (f32[21,16,256]{2,1,0:T(8,128)S(1)}, f32[21,16,256]{2,1,0:T(8,128)S(1)}, u32[]{:S(2)}, u32[]{:S(2)}) collective-permute-start(f32[21,16,256]{2,1,0:T(8,128)S(1)} %fusion.1), channel_id=1, source_target_pairs={{0,32},{1,33},{2,34},{3,35},{4,36},{5,37},{6,38},{7,39},{8,40},{9,... | collective-permute-start | bytes 1032200 | tf_op jit(solution)/shard_map/ppermute | solution.py:41
Sparse Core Ops, SparseCore 0:
  15.9 62.0 all-gather.2

commit v5 on v4

--- a/solution.py
+++ b/solution.py
@@ -14,6 +14,7 @@
 F32 = jnp.float32
 I32 = jnp.int32
 AXES = ("dp", "fsdp")
+FIRST = 3
 VMEM_BYTES = 56 * 1024 * 1024
 
 
@@ -53,6 +54,11 @@
     got = (send(sent, "y"), send(kept.astype(BF), "h"), send(sent, "hy"))
     total = kept + got[0].astype(F32) + got[1].astype(F32) + got[2].astype(F32)
     return total, send(total, "c")
+
+
+def over_dp_by_chip(blocks):
+    own, beside, across, both = blocks
+    return (own, send(beside, "c"), send(across, "h"), send(send(both, "h"), "c"))
 
 
 def over_plane(blocks):
@@ -226,7 +232,7 @@
                 side, step = unit // 4, unit % 4
                 first = (x * 4 + step) * rows
                 down[z, first : first + rows, side * half : (side + 1) * half] = pieces[
-                    z * 4 + x, 8 + unit
+                    z * 4 + x, unit
                 ]
 
 
@@ -282,33 +288,75 @@
     part[...] = total
 
 
-def grad_conv_kernel(
+def tap_grads(taps, turned, windows, sums, grads):
+    half = turned.shape[1]
+    middle = turned.shape[2] // 2
+    rows = grads.shape[2]
+    seen = set()
+    for p in range(4):
+        for q in range(4):
+            users = []
+            for k in range(4):
+                dy, dx = p - k // 2, q - k % 2
+                if 0 <= dy < 3 and 0 <= dx < 3 and dy * 3 + dx in taps:
+                    users.append((k, taps.index(dy * 3 + dx)))
+            if not users:
+                continue
+            term = None
+            for part in range(2):
+                columns = slice(part * middle, (part + 1) * middle)
+                left = jnp.concatenate([turned[k, :, columns] for k, _ in users])
+                piece = dot(left, windows[part, p * 4 + q], 1, 0)
+                term = piece if term is None else term + piece
+            for place, (_, t) in enumerate(users):
+                piece = term[place * half : (place + 1) * half]
+                sums[t] = sums[t] + piece if t in seen else piece
+                seen.add(t)
+    for t in range(len(taps)):
+        total = sums[t].T.astype(BF)
+        for f in range(32):
+            z, y, x = f // 8, f // 4 % 2, f % 4
+            grads[z * 4 + x, y * len(taps) + t] = total[f * rows : (f + 1) * rows, :]
+
+
+def window_copies(first, last, windows_own, windows_pair, windows, sem):
+    part_of = pl.ds(first, last - first)
+    return [
+        pltpu.make_async_copy(ref.at[part_of], windows.at[part, part_of], sem.at[part])
+        for part, ref in enumerate((windows_own, windows_pair))
+    ]
+
+
+def first_taps_kernel(
     loss_scale,
     mask,
     own,
-    got,
+    got_far,
     folded,
     pieces,
     windows_own,
     windows_pair,
     glow,
+    turned,
     grads,
     down,
-    turned,
+    got,
+    held,
     sums,
     windows,
     sem,
 ):
     half = folded.shape[2]
-    copies = [
-        pltpu.make_async_copy(ref, windows.at[part], sem.at[part])
-        for part, ref in enumerate((windows_own, windows_pair))
+    fetched = [
+        pltpu.make_async_copy(got_far, got, sem.at[2]),
+        pltpu.make_async_copy(pieces.at[:, pl.ds(8, 8)], held, sem.at[3]),
     ]
-    for copy in copies:
+    copies = window_copies(0, 8, windows_own, windows_pair, windows, sem)
+    for copy in fetched + copies:
         copy.start()
-    rows = grads.shape[2]
-    middle = folded.shape[1] // 2
-    gather_down(pieces, down)
+    for copy in fetched:
+        copy.wait()
+    gather_down(held, down)
     glow[...] = swapped_sum(own, got)
     kept = jnp.concatenate([mask[...]] * (half // mask.shape[1]), axis=1)
     for k in range(4):
@@ -316,26 +364,16 @@
         turned[k] = (grad * kept).T.astype(BF)
     for copy in copies:
         copy.wait()
-    seen = set()
-    for v in range(16):
-        p, q = v // 4, v % 4
-        users = [k for k in range(4) if 0 <= p - k // 2 < 3 and 0 <= q - k % 2 < 3]
-        term = None
-        for part in range(2):
-            columns = slice(part * middle, (part + 1) * middle)
-            left = jnp.concatenate([turned[k, :, columns] for k in users])
-            piece = dot(left, windows[part, v], 1, 0)
-            term = piece if term is None else term + piece
-        for place, k in enumerate(users):
-            t = (p - k // 2) * 3 + q - k % 2
-            piece = term[place * half : (place + 1) * half]
-            sums[t] = sums[t] + piece if t in seen else piece
-            seen.add(t)
-    for t in range(9):
-        total = sums[t].T.astype(BF)
-        for f in range(32):
-            z, y, x = f // 8, f // 4 % 2, f % 4
-            grads[z * 4 + x, y * 9 + t] = total[f * rows : (f + 1) * rows, :]
+    tap_grads(list(range(FIRST)), turned, windows, sums, grads)
+
+
+def other_taps_kernel(turned, windows_own, windows_pair, grads, sums, windows, sem):
+    copies = window_copies(4, 16, windows_own, windows_pair, windows, sem)
+    for copy in copies:
+        copy.start()
+    for copy in copies:
+        copy.wait()
+    tap_grads(list(range(FIRST, 9)), turned, windows, sums, grads)
 
 
 def conv_kernel(
@@ -351,15 +389,20 @@
     part,
     conv,
     down,
+    held,
+    sem,
 ):
     half = wide.shape[2]
     rows = conv_pieces.shape[2]
     middle = wide.shape[1] // 2
+    copy = pltpu.make_async_copy(pieces.at[:, pl.ds(8, 8)], held, sem)
+    copy.start()
     for f in range(32):
         z, y, x = f // 8, f // 4 % 2, f % 4
         for t in range(9):
             conv[t, f * rows : (f + 1) * rows, :] = conv_pieces[z * 4 + x, y * 9 + t]
-    gather_down(pieces, down)
+    copy.wait()
+    gather_down(held, down)
     total = None
     for k in range(4):
         for first, windows, residual in (
@@ -387,7 +430,7 @@
     meta,
     mask,
     own,
-    got,
+    got_far,
     wide,
     skip,
     glow,
@@ -403,13 +446,24 @@
     outputs,
     raw,
     returning,
+    got,
+    held,
+    sem,
 ):
     side = extent // 2
     quarter = side * side
     half = wide.shape[2]
     rows = grads.shape[2]
     images = wide.shape[1] // quarter
-    gather_up(pieces, up)
+    copies = [
+        pltpu.make_async_copy(got_far, got, sem.at[0]),
+        pltpu.make_async_copy(pieces.at[:, pl.ds(0, 8)], held, sem.at[1]),
+    ]
+    for copy in copies:
+        copy.start()
+    for copy in copies:
+        copy.wait()
+    gather_up(held, up)
     low[...] = swapped_sum(own, got)
     kept = jnp.concatenate([mask[...]] * (half // mask.shape[1]), axis=1)
     for k in range(4):
@@ -582,26 +636,48 @@
     )(folded, up_down)
     glow_got = send(glow_part, "c")
 
-    glow, conv_grads = kernel_call(
-        functools.partial(grad_conv_kernel, loss_scale),
+    held = pltpu.VMEM((16, 8, rows, half), BF)
+    far = pl.BlockSpec(memory_space=pl.ANY)
+    both_windows = pltpu.VMEM((2, *windows_own.shape), BF)
+    glow, turned, first_grads = kernel_call(
+        functools.partial(first_taps_kernel, loss_scale),
         (
             jax.ShapeDtypeStruct((low_rows, channels), BF),
-            jax.ShapeDtypeStruct((16, 18, rows, half), BF),
-        ),
-        flops=80 * low_rows * channels * half,
-        moved_bytes=15 << 20,
+            jax.ShapeDtypeStruct((4, half, low_rows), BF),
+            jax.ShapeDtypeStruct((16, 2 * FIRST, rows, half), BF),
+        ),
+        flops=32 * low_rows * channels * half,
+        moved_bytes=10 << 20,
         scratch=(
             pltpu.VMEM((4, half, channels), BF),
-            pltpu.VMEM((4, half, low_rows), BF),
-            pltpu.VMEM((9, half, channels), F32),
-            pltpu.VMEM((2, *windows_own.shape), BF),
+            pltpu.VMEM((low_rows, channels), F32),
+            held,
+            pltpu.VMEM((FIRST, half, channels), F32),
+            both_windows,
+            pltpu.SemaphoreType.DMA((4,)),
+        ),
+        in_specs=[WHOLE, WHOLE, far, WHOLE, far, far, far],
+        out_specs=(WHOLE,) * 3,
+    )(mask, glow_part, glow_got, folded, up_down, windows_own, windows_pair)
+    first_grads = over_plane(first_grads)
+    other_grads = kernel_call(
+        other_taps_kernel,
+        jax.ShapeDtypeStruct((16, 18 - 2 * FIRST, rows, half), BF),
+        flops=48 * low_rows * channels * half,
+        moved_bytes=10 << 20,
+        scratch=(
+            pltpu.VMEM((9 - FIRST, half, channels), F32),
+            both_windows,
             pltpu.SemaphoreType.DMA((2,)),
         ),
-        in_specs=[WHOLE] * 5 + [pl.BlockSpec(memory_space=pl.ANY)] * 2,
-        out_specs=(WHOLE, WHOLE),
-    )(mask, glow_part, glow_got, folded, up_down, windows_own, windows_pair)
-    conv_grads = over_plane(conv_grads)
-    glow, windows_own, windows_pair = lax.optimization_barrier((glow, windows_own, windows_pair))
+        in_specs=[WHOLE, far, far],
+        out_specs=WHOLE,
+    )(turned, windows_own, windows_pair)
+    other_grads, windows_own, windows_pair = lax.optimization_barrier(
+        (other_grads, windows_own, windows_pair)
+    )
+    other_grads, first_grads = lax.optimization_barrier((other_grads, first_grads))
+    other_grads = over_plane(other_grads)
 
     wide, skip, low_part = kernel_call(
         conv_kernel,
@@ -612,8 +688,13 @@
         ),
         flops=80 * low_rows * channels * half,
         moved_bytes=18 << 20,
-        scratch=(pltpu.VMEM((9, channels, half), BF), pltpu.VMEM((4, half, channels), BF)),
-        in_specs=[WHOLE] * 7,
+        scratch=(
+            pltpu.VMEM((9, channels, half), BF),
+            pltpu.VMEM((4, half, channels), BF),
+            held,
+            pltpu.SemaphoreType.DMA,
+        ),
+        in_specs=[WHOLE, WHOLE, far] + [WHOLE] * 4,
         out_specs=(WHOLE,) * 3,
     )(mask, conv_two, up_down, windows_own, windows_pair, residual_own, residual_pair)
     low_got = send(low_part, "c")
@@ -632,29 +713,37 @@
             pltpu.VMEM((4, low_rows, half), F32),
             laned(extent, extent, half),
             pltpu.VMEM((8 * most, pixels, half), BF),
-        ),
-        in_specs=[SCALARS] + [WHOLE] * 8,
+            pltpu.VMEM((low_rows, channels), F32),
+            held,
+            pltpu.SemaphoreType.DMA((2,)),
+        ),
+        in_specs=[SCALARS, WHOLE, WHOLE, far] + [WHOLE] * 4 + [far],
         out_specs=(WHOLE,) * 5,
     )(meta, mask, low_part, low_got, wide, skip, glow, folded, up_down)
-    returned = over_dp(returning)
+    returned = over_dp_by_chip(returning)
     grads = over_plane(grads)
 
-    conv_sum = jnp.sum(conv_grads.astype(F32), axis=0).reshape(2, 9, rows, half)
+    conv_sum = jnp.concatenate(
+        [
+            jnp.sum(part.astype(F32), axis=0).reshape(2, -1, rows, half)
+            for part in (first_grads, other_grads)
+        ],
+        axis=1,
+    )
+    conv_sum, returned = lax.optimization_barrier((conv_sum, returned))
+
+    def by_core(own, pair):
+        both = jnp.where(core == 0, jnp.stack([own, pair]), jnp.stack([pair, own]))
+        return both.transpose(2, 1, 0, 3)
+
+    out_conv = by_core(*over_column(conv_sum, y)).reshape(rows, 9, channels)
     grads_sum = jnp.sum(grads.astype(F32), axis=0)
     up_sum, down_sum = grads_sum[:8].reshape(2, 4, rows, half), grads_sum[8:]
-    down_sum = jnp.broadcast_to(down_sum, (2, *down_sum.shape))
-    shares = jnp.concatenate([conv_sum, up_sum, down_sum], axis=1)
-    shares, returned = lax.optimization_barrier((shares, returned))
+    shares = jnp.concatenate([up_sum, jnp.broadcast_to(down_sum, (2, *down_sum.shape))], axis=1)
+    shares, out_conv = lax.optimization_barrier((shares, out_conv))
     own, pair = over_column(shares, y)
-
-    def by_core(first, last):
-        parts = (own[first:last], pair[first:last])
-        both = jnp.where(core == 0, jnp.stack(parts), jnp.stack(parts[::-1]))
-        return both.transpose(2, 1, 0, 3)
-
-    out_conv = by_core(0, 9).reshape(rows, 9, channels)
-    out_up = by_core(9, 13).reshape(rows, 4 * channels)
-    out_down = jnp.where(y == core, own[13:], pair[13:])
+    out_up = by_core(own[:4], pair[:4]).reshape(rows, 4 * channels)
+    out_down = jnp.where(y == core, own[4:], pair[4:])
     out_down = out_down.reshape(2, 4 * rows, half).transpose(1, 0, 2).reshape(4 * rows, channels)
 
     block_out = kernel_call(

time: 187 us -> 195 us (1.043)
  starting transfers between devices: 40.8 us -> 53.3 us
  waiting for transfers between devices: 54.4 us -> 43.1 us
  Pallas kernels: 61 us -> 65.6 us
    all_to_all x3 -> x4, waiting for transfers between devices: 36.5 us -> 4.97 us  [over_plane(): lax.all_to_all(blocks, 'fsdp', split_axis=0, concat_axis=0, axis_index_gr...]
    ppermute x15 -> x20, waiting for transfers between devices: 17.9 us -> 38.1 us  [send(): return lax.ppermute(value, AXES, STEP[move])]
    ppermute x15 -> x20, starting transfers between devices: 21.4 us -> 27.7 us  [send(): return lax.ppermute(value, AXES, STEP[move])]
    all_to_all x3 -> x4, starting transfers between devices: 19.3 us -> 25.5 us  [over_plane(): lax.all_to_all(blocks, 'fsdp', split_axis=0, concat_axis=0, axis_index_gr...]
    pallas_call x1 -> x2, Pallas kernels: 12.9 us -> 16.1 us  [the longest x1 8.74 us: per_device(): kernel_call(other_taps_kernel, jax.ShapeDtypeStruct((16, 18 - 2 * FIRST,...]
    unnamed x24 -> x22, local copies, waits for them, and re-layouts: 3.41 us -> 4.57 us
  transfers between devices with their start and end apart: 19 -> 25, of which waited for: 10 -> 13; matrix products, arithmetic and copies ran while one was open for 4% -> 4% of each run, Pallas kernels for 33% -> 34%
where the time goes in v5:
time: 195 us; the launch traced here: 194 us
  Pallas kernels  65.6 us (34%)
  starting transfers between devices  53.3 us (27%)
  waiting for transfers between devices  43.1 us (22%)
  between operations  14.5 us (7%)
  local copies, waits for them, and re-layouts  13.5 us (7%)
  other arithmetic  4.23 us (2%)
    ppermute x20, waiting for transfers between devices, send(): return lax.ppermute(value, AXES, STEP[move])  38.1 us
    ppermute x20, starting transfers between devices, send(): return lax.ppermute(value, AXES, STEP[move])  27.7 us
    all_to_all x4, starting transfers between devices, over_plane(): lax.all_to_all(blocks, 'fsdp', split_axis=0, concat_axis=0, axis_index_gr...  25.5 us
    pallas_call x1, Pallas kernels, per_device(): kernel_call(conv_kernel, (jax.ShapeDtypeStruct((4, low_rows, half), F32),...  13.2 us
    pallas_call x2, Pallas kernels, normed_windows(): kernel_call(functools.partial(norm_kernel, extent), (jax.ShapeDtypeStruct...  13.1 us
    pallas_call x1, Pallas kernels, per_device(): kernel_call(other_taps_kernel, jax.ShapeDtypeStruct((16, 18 - 2 * FIRST,...  8.74 us
    pallas_call x1, Pallas kernels, per_device(): kernel_call(functools.partial(output_kernel, extent, loss_scale), (*(bloc...  8.68 us
    pallas_call x1, Pallas kernels, per_device(): kernel_call(functools.partial(first_taps_kernel, loss_scale), (jax.ShapeD...  7.4 us
  transfers between devices with their start and end apart: 25, of which 13 were waited for; matrix products, arithmetic and copies ran while one was open for 4% of the time, Pallas kernels for 34%

profile of v5, /device:TPU:1, one launch (start us, length us, event | category | flops | bytes accessed | tf_op | source)
XLA Modules:
  0.0 194.1 jit_solution(13995641101670556664)
XLA Ops:
  9.1 2.2 %collective-permute-start.2 = (bf16[21,16,256]{2,1,0:T(8,128)(2,1)S(1)}, bf16[21,16,256]{2,1,0:T(8,128)(2,1)S(1)}, u32[]{:S(2)}, u32[]{:S(2)}) collective-permute-start(bf16[21,16,256]{2,1,0:T(8,128)(2,1)S(1)} %pad_maximum_fusion.2), channel_id=1, source_target_pairs={{0,4},{1,5},{2,6},{3,7},{4,0},{5,1},{6,2},{7,3},{8,12},{9,13},{10,... | collective-permute-start | bytes 516104 | tf_op jit(solution)/shard_map/ppermute | solution.py:42
  11.3 3.0 %shard_map.140 = (bf16[4,256,256]{2,1,0:T(8,128)(2,1)}, bf16[4,256,256]{2,1,0:T(8,128)(2,1)}, bf16[4,256,256]{2,1,0:T(8,128)(2,1)}, bf16[4,256,256]{2,1,0:T(8,128)(2,1)}) custom-call(s32[1]{0:T(128)} %bitcast.number, bf16[8,256,512]{2,1,0:T(8,128)(2,1)} %bitcast.78), custom_call_target="tpu_custom_call" | custom-call | bytes 4194304 | tf_op jit(solution)/shard_map/pallas_call | solution.py:556
  15.8 1.6 broadcast_in_dim.72
  17.4 8.0 %all-to-all-start = ((bf16[16,16,16,256]{3,2,1,0:T(8,128)(2,1)}), bf16[16,16,16,256]{3,2,1,0:T(8,128)(2,1)S(1)}, u32[]{:S(2)}, u32[]{:S(2)}) async-start(bf16[16,16,16,256]{3,2,1,0:T(8,128)(2,1)} %broadcast_in_dim.72), calls=%async_computation | async-start | bytes 4194304 | tf_op jit(solution)/shard_map/all_to_all | solution.py:65
  25.5 1.9 collective-permute-start
  29.0 2.9 %collective-permute-start.4 = (bf16[4,256,256]{2,1,0:T(8,128)(2,1)}, bf16[4,256,256]{2,1,0:T(8,128)(2,1)}, u32[]{:S(2)}, u32[]{:S(2)}) collective-permute-start(bf16[4,256,256]{2,1,0:T(8,128)(2,1)} %get-tuple-element.54), channel_id=1, source_target_pairs={{0,64},{1,65},{2,66},{3,67},{4,68},{5,69},{6,70},{7,71},{8,72},{9,... | collective-permute-start | bytes 1572872 | tf_op jit(solution)/shard_map/ppermute | solution.py:42
  34.4 6.5 %shard_map.138 = (bf16[16,256,512]{2,1,0:T(8,128)(2,1)}, bf16[4,256,256]{2,1,0:T(8,128)(2,1)}) custom-call(s32[32]{0:T(128)} %concatenate.40.meta, bf16[4,256,512]{2,1,0:T(8,128)(2,1)} %bitcast.79, f32[1,512]{1,0:T(1,128)} %bitcast.88, f32[1,512]{1,0:T(1,128)} %bitcast.90), custom_call_target="tpu_custom_call" | custom-call | flops 20971520 | bytes 6291456 | tf_op jit(solution)/shard_map/pallas_call | solution.py:193
  40.9 6.6 %shard_map.139 = (bf16[16,256,512]{2,1,0:T(8,128)(2,1)}, bf16[4,256,256]{2,1,0:T(8,128)(2,1)}) custom-call(s32[32]{0:T(128)} %concatenate.42.meta, bf16[4,256,512]{2,1,0:T(8,128)(2,1)} %bitcast.18.image, f32[1,512]{1,0:T(1,128)} %bitcast.89, f32[1,512]{1,0:T(1,128)} %bitcast.91), custom_call_target="tpu_custom_call" | custom-call | flops 20971520 | bytes 6291456 | tf_op jit(solution)/shard_map/pallas_call | solution.py:193
  48.4 7.4 %collective-permute-done.5.cot3 = bf16[4,256,256]{2,1,0:T(8,128)(2,1)} collective-permute-done((bf16[4,256,256]{2,1,0:T(8,128)(2,1)}, bf16[4,256,256]{2,1,0:T(8,128)(2,1)}, u32[]{:S(2)}, u32[]{:S(2)}) %collective-permute-start.5) | collective-permute-done | bytes 524320 | tf_op jit(solution)/shard_map/ppermute | solution.py:42
  55.7 3.6 %shard_map.141.folded = bf16[4,512,256]{2,1,0:T(8,128)(2,1)} custom-call(s32[32]{0:T(128)} %concatenate.38.meta, bf16[4,256,256]{2,1,0:T(8,128)(2,1)} %get-tuple-element.52.cot0, bf16[4,256,256]{2,1,0:T(8,128)(2,1)} %collective-permute-done.3.cot1, bf16[4,256,256]{2,1,0:T(8,128)(2,1)} %collective-permute-done.4.cot2, ...), custom_call_target="tpu_custom_call" | custom-call | bytes 3145728 | tf_op jit(solution)/shard_map/pallas_call | solution.py:611
  60.8 4.2 %shard_map.142.own = f32[512,512]{1,0:T(8,128)} custom-call(bf16[4,512,256]{2,1,0:T(8,128)(2,1)} %shard_map.141.folded, bf16[16,16,16,256]{3,2,1,0:T(8,128)(2,1)} %copy-done.1), custom_call_target="tpu_custom_call" | custom-call | flops 536870912 | bytes 3145728 | tf_op jit(solution)/shard_map/pallas_call | solution.py:624
  65.1 2.8 %collective-permute-done.6.got_far = f32[512,512]{1,0:T(8,128)S(1)} collective-permute-done((f32[512,512]{1,0:T(8,128)}, f32[512,512]{1,0:T(8,128)S(1)}, u32[]{:S(2)}, u32[]{:S(2)}) %collective-permute-start.6) | collective-permute-done | bytes 1048608 | tf_op jit(solution)/shard_map/ppermute | solution.py:42
  68.9 7.4 %shard_map.143 = (bf16[512,512]{1,0:T(8,128)(2,1)}, bf16[4,256,512]{2,1,0:T(8,128)(2,1)}, bf16[16,6,16,256]{3,2,1,0:T(8,128)(2,1)}) custom-call(f32[512,128]{1,0:T(8,128)} %broadcast_in_dim.69.mask, f32[512,512]{1,0:T(8,128)} %shard_map.142.own, f32[512,512]{1,0:T(8,128)} %copy-done.5, bf16[4,512,256]{2,1,0:T(8,128)(2,1)} %shard_map.141.folded, ...), custom_call_target="tpu_custom_call" | custom-call | flops 2147483648 | bytes 10485760 | tf_op jit(solution)/shard_map/pallas_call | solution.py:642
  76.3 7.0 %all-to-all-start.1 = ((bf16[16,6,16,256]{3,2,1,0:T(8,128)(2,1)}), bf16[16,6,16,256]{3,2,1,0:T(8,128)(2,1)S(1)}, u32[]{:S(2)}, u32[]{:S(2)}) async-start(bf16[16,6,16,256]{3,2,1,0:T(8,128)(2,1)} %get-tuple-element.61), calls=%async_computation.1 | async-start | bytes 1572864 | tf_op jit(solution)/shard_map/all_to_all | solution.py:65
  83.3 8.7 %shard_map.144 = bf16[16,12,16,256]{3,2,1,0:T(8,128)(2,1)} custom-call(bf16[4,256,512]{2,1,0:T(8,128)(2,1)} %get-tuple-element.59.turned, bf16[16,256,512]{2,1,0:T(8,128)(2,1)} %get-tuple-element.64.windows_own, bf16[16,256,512]{2,1,0:T(8,128)(2,1)} %get-tuple-element.65.windows_pair), custom_call_target="tpu_custom_call" | custom-call | flops 3221225472 | bytes 10485760 | tf_op jit(solution)/shard_map/pallas_call | solution.py:663
  92.0 5.0 %all-to-all-done.1 = bf16[16,6,16,256]{3,2,1,0:T(8,128)(2,1)S(1)} async-done(((bf16[16,6,16,256]{3,2,1,0:T(8,128)(2,1)}), bf16[16,6,16,256]{3,2,1,0:T(8,128)(2,1)S(1)}, u32[]{:S(2)}, u32[]{:S(2)}) %all-to-all-start.1) | async-done | bytes 786464 | tf_op jit(solution)/shard_map/all_to_all | solution.py:65
  97.0 3.9 %all-to-all-start.2 = ((bf16[16,12,16,256]{3,2,1,0:T(8,128)(2,1)}), bf16[16,12,16,256]{3,2,1,0:T(8,128)(2,1)S(1)}, u32[]{:S(2)}, u32[]{:S(2)}) async-start(bf16[16,12,16,256]{3,2,1,0:T(8,128)(2,1)} %shard_map.144), calls=%async_computation.2 | async-start | bytes 3145728 | tf_op jit(solution)/shard_map/all_to_all | solution.py:65
  100.9 13.2 %shard_map.145 = (f32[4,512,256]{2,1,0:T(8,128)}, bf16[4,512,256]{2,1,0:T(8,128)(2,1)}, f32[512,512]{1,0:T(8,128)}) custom-call(f32[512,128]{1,0:T(8,128)} %broadcast_in_dim.69.mask, bf16[16,18,16,256]{3,2,1,0:T(8,128)(2,1)} %bitcast.98, bf16[16,16,16,256]{3,2,1,0:T(8,128)(2,1)} %copy-done.1, bf16[16,256,512]{2,1,0:T(8,128)(2,1)} %get-tuple-element.64.windows_own, ...), custom_call_target="tpu_custom_call" | custom-call | flops 5368709120 | bytes 18874368 | tf_op jit(solution)/shard_map/pallas_call | solution.py:682
  114.1 1.7 collective-permute-start.7
  115.7 2.5 %collective-permute-done.7.got_far = f32[512,512]{1,0:T(8,128)S(1)} collective-permute-done((f32[512,512]{1,0:T(8,128)}, f32[512,512]{1,0:T(8,128)S(1)}, u32[]{:S(2)}, u32[]{:S(2)}) %collective-permute-start.7) | collective-permute-done | bytes 1048608 | tf_op jit(solution)/shard_map/ppermute | solution.py:42
  119.2 8.7 %shard_map.146 = (bf16[4,256,256]{2,1,0:T(8,128)(2,1)}, bf16[4,256,256]{2,1,0:T(8,128)(2,1)}, bf16[4,256,256]{2,1,0:T(8,128)(2,1)}, bf16[4,256,256]{2,1,0:T(8,128)(2,1)}, bf16[16,16,16,256]{3,2,1,0:T(8,128)(2,1)}) custom-call(s32[32]{0:T(128)} %concatenate.38.meta, f32[512,128]{1,0:T(8,128)} %broadcast_in_dim.69.mask, f32[512,512]{1,0:T(8,128)} %get-tuple-element.68.own, ...), custom_call_target="tpu_custom_call" | custom-call | flops 1610612736 | bytes 14680064 | tf_op jit(solution)/shard_map/pallas_call | solution.py:702
  129.1 6.7 %all-to-all-start.3 = ((bf16[16,16,16,256]{3,2,1,0:T(8,128)(2,1)}), bf16[16,16,16,256]{3,2,1,0:T(8,128)(2,1)S(1)}, u32[]{:S(2)}, u32[]{:S(2)}) async-start(bf16[16,16,16,256]{3,2,1,0:T(8,128)(2,1)} %get-tuple-element.80), calls=%async_computation.3 | async-start | bytes 4194304 | tf_op jit(solution)/shard_map/all_to_all | solution.py:65
  135.8 3.0 %collective-permute-start.10 = (bf16[4,256,256]{2,1,0:T(8,128)(2,1)}, bf16[4,256,256]{2,1,0:T(8,128)(2,1)}, u32[]{:S(2)}, u32[]{:S(2)}) collective-permute-start(bf16[4,256,256]{2,1,0:T(8,128)(2,1)} %get-tuple-element.75), channel_id=1, source_target_pairs={{0,64},{1,65},{2,66},{3,67},{4,68},{5,69},{6,70},{7,71},{8,72},{9,... | collective-permute-start | bytes 1572872 | tf_op jit(solution)/shard_map/ppermute | solution.py:42
  139.8 10.7 %collective-permute-done.10 = bf16[4,256,256]{2,1,0:T(8,128)(2,1)} collective-permute-done((bf16[4,256,256]{2,1,0:T(8,128)(2,1)}, bf16[4,256,256]{2,1,0:T(8,128)(2,1)}, u32[]{:S(2)}, u32[]{:S(2)}) %collective-permute-start.10) | collective-permute-done | bytes 524320 | tf_op jit(solution)/shard_map/ppermute | solution.py:42
  150.5 2.7 %collective-permute-start.11 = (bf16[4,256,256]{2,1,0:T(8,128)(2,1)}, bf16[4,256,256]{2,1,0:T(8,128)(2,1)}, u32[]{:S(2)}, u32[]{:S(2)}) collective-permute-start(bf16[4,256,256]{2,1,0:T(8,128)(2,1)} %collective-permute-done.10), channel_id=1, source_target_pairs={{0,32},{1,33},{2,34},{3,35},{4,36},{5,37},{6,38},{7,39},{8,40},{9,... | collective-permute-start | bytes 1572872 | tf_op jit(solution)/shard_map/ppermute | solution.py:42
  153.3 1.6 convert_reduce_fusion.1
  155.0 6.8 %collective-permute-done.9.back2 = bf16[4,256,256]{2,1,0:T(8,128)(2,1)} collective-permute-done((bf16[4,256,256]{2,1,0:T(8,128)(2,1)}, bf16[4,256,256]{2,1,0:T(8,128)(2,1)}, u32[]{:S(2)}, u32[]{:S(2)}) %collective-permute-start.9) | collective-permute-done | bytes 524320 | tf_op jit(solution)/shard_map/ppermute | solution.py:42
  161.8 2.8 %collective-permute-start.14 = (bf16[9,16,256]{2,1,0:T(8,128)(2,1)S(1)}, bf16[9,16,256]{2,1,0:T(8,128)(2,1)S(1)}, u32[]{:S(2)}, u32[]{:S(2)}) collective-permute-start(bf16[9,16,256]{2,1,0:T(8,128)(2,1)S(1)} %get-tuple-element.93), channel_id=1, source_target_pairs={{0,68},{1,69},{2,70},{3,71},{4,64},{5,65},{6,66},{7,67},{8,76},{9,... | collective-permute-start | bytes 221192 | tf_op jit(solution)/shard_map/ppermute | solution.py:42
  166.6 2.6 %collective-permute-done.13 = bf16[9,16,256]{2,1,0:T(8,128)(2,1)S(1)} collective-permute-done((bf16[9,16,256]{2,1,0:T(8,128)(2,1)S(1)}, bf16[9,16,256]{2,1,0:T(8,128)(2,1)S(1)}, u32[]{:S(2)}, u32[]{:S(2)}) %collective-permute-start.13) | collective-permute-done | bytes 73760 | tf_op jit(solution)/shard_map/ppermute | solution.py:42
  169.3 3.0 %collective-permute-start.15 = (f32[9,16,256]{2,1,0:T(8,128)S(1)}, f32[9,16,256]{2,1,0:T(8,128)S(1)}, u32[]{:S(2)}, u32[]{:S(2)}) collective-permute-start(f32[9,16,256]{2,1,0:T(8,128)S(1)} %fusion.4), channel_id=1, source_target_pairs={{0,32},{1,33},{2,34},{3,35},{4,36},{5,37},{6,38},{7,39},{8,40},{9,... | collective-permute-start | bytes 442376 | tf_op jit(solution)/shard_map/ppermute | solution.py:42
  178.6 3.6 %shard_map.147 = f32[8,256,512]{2,1,0:T(8,128)} custom-call(s32[1]{0:T(128)} %bitcast.number, bf16[4,256,256]{2,1,0:T(8,128)(2,1)} %get-tuple-element.76.back0, bf16[4,256,256]{2,1,0:T(8,128)(2,1)} %copy-done.6, bf16[4,256,256]{2,1,0:T(8,128)(2,1)} %collective-permute-done.9.back2, bf16[4,256,256]{2,1,0:T(8,128)(2,1)} %collective-permute-done.11.back3), custom_call_target="tpu_custom_call" | custom-call | bytes 6291456 | tf_op jit(solution)/shard_map/pallas_call | solution.py:749
  183.1 1.5 collective-permute-start.19
  (108 shorter events, 25.9 us)
Async XLA Ops:
  7.2 1.8 copy-start
  7.2 93.7 %all-gather.3.cloned.1.call-start = ((), (), s32[]{:S(2)}) async-start(), calls=%async_computation.4 | async-start | bytes 2506752 | tf_op jit(solution)/shard_map/all_gather | solution.py:572
  9.1 5.9 %collective-permute-start.2 = (bf16[21,16,256]{2,1,0:T(8,128)(2,1)S(1)}, bf16[21,16,256]{2,1,0:T(8,128)(2,1)S(1)}, u32[]{:S(2)}, u32[]{:S(2)}) collective-permute-start(bf16[21,16,256]{2,1,0:T(8,128)(2,1)S(1)} %pad_maximum_fusion.2), channel_id=1, source_target_pairs={{0,4},{1,5},{2,6},{3,7},{4,0},{5,1},{6,2},{7,3},{8,12},{9,13},{10,... | collective-permute-start | bytes 516104 | tf_op jit(solution)/shard_map/ppermute | solution.py:42
  17.4 8.0 %copy-start.7 = (s32[4,1]{0,1:T(1,128)S(1)}, s32[4,1]{0,1:T(1,128)}, u32[]{:S(2)}) copy-start(s32[4,1]{0,1:T(1,128)} %param.12) | copy-start | bytes 52
  17.4 8.0 %copy-start.8 = (s32[4]{0:T(128)S(1)}, s32[4]{0:T(128)}, u32[]{:S(2)}) copy-start(s32[4]{0:T(128)} %param.13) | copy-start | bytes 52
  17.4 10.0 %copy-start.4 = (bf16[4,16,16,512]{3,2,1,0:T(8,128)(2,1)S(1)}, bf16[4,16,16,512]{3,2,1,0:T(8,128)(2,1)}, u32[]{:S(2)}) copy-start(bf16[4,16,16,512]{3,2,1,0:T(8,128)(2,1)} %param.11) | copy-start | bytes 3145732
  17.4 10.8 %copy-start.9 = (s32[8]{0:T(128)S(1)}, s32[8]{0:T(128)}, u32[]{:S(2)}) copy-start(s32[8]{0:T(128)} %param.14) | copy-start | bytes 100
  17.4 10.8 %copy-start.10 = (s32[8]{0:T(128)S(1)}, s32[8]{0:T(128)}, u32[]{:S(2)}) copy-start(s32[8]{0:T(128)} %param.15) | copy-start | bytes 100
  17.4 42.0 %all-to-all-start = ((bf16[16,16,16,256]{3,2,1,0:T(8,128)(2,1)}), bf16[16,16,16,256]{3,2,1,0:T(8,128)(2,1)S(1)}, u32[]{:S(2)}, u32[]{:S(2)}) async-start(bf16[16,16,16,256]{3,2,1,0:T(8,128)(2,1)} %broadcast_in_dim.72), calls=%async_computation | async-start | bytes 4194304 | tf_op jit(solution)/shard_map/all_to_all | solution.py:65
  25.5 2.7 %collective-permute-start = (s32[4,2]{0,1:T(2,128)S(1)}, s32[4,2]{0,1:T(2,128)S(1)}, u32[]{:S(2)}, u32[]{:S(2)}) collective-permute-start(s32[4,2]{0,1:T(2,128)S(1)} %pad_add_fusion.2), channel_id=1, source_target_pairs={{0,32},{1,33},{2,34},{3,35},{4,36},{5,37},{6,38},{7,39},{8,40},{9,... | collective-permute-start | bytes 104 | tf_op jit(solution)/shard_map/ppermute | solution.py:42
  27.4 13.5 %collective-permute-start.1 = (bf16[4,16,16,512]{3,2,1,0:T(8,128)(2,1)S(1)}, bf16[4,16,16,512]{3,2,1,0:T(8,128)(2,1)}, u32[]{:S(2)}, u32[]{:S(2)}) collective-permute-start(bf16[4,16,16,512]{3,2,1,0:T(8,128)(2,1)S(1)} %copy-done.4), channel_id=1, source_target_pairs={{0,32},{1,33},{2,34},{3,35},{4,36},{5,37},{6,38},{7,39},{8,40},{9,... | collective-permute-start | bytes 3145736 | tf_op jit(solution)/shard_map/ppermute | solution.py:42
  28.7 19.7 %collective-permute-start.3 = (bf16[4,256,256]{2,1,0:T(8,128)(2,1)}, bf16[4,256,256]{2,1,0:T(8,128)(2,1)}, u32[]{:S(2)}, u32[]{:S(2)}) collective-permute-start(bf16[4,256,256]{2,1,0:T(8,128)(2,1)} %get-tuple-element.53), channel_id=1, source_target_pairs={{0,32},{1,33},{2,34},{3,35},{4,36},{5,37},{6,38},{7,39},{8,40},{9,... | collective-permute-start | bytes 1572872 | tf_op jit(solution)/shard_map/ppermute | solution.py:42
  29.0 19.3 %collective-permute-start.4 = (bf16[4,256,256]{2,1,0:T(8,128)(2,1)}, bf16[4,256,256]{2,1,0:T(8,128)(2,1)}, u32[]{:S(2)}, u32[]{:S(2)}) collective-permute-start(bf16[4,256,256]{2,1,0:T(8,128)(2,1)} %get-tuple-element.54), channel_id=1, source_target_pairs={{0,64},{1,65},{2,66},{3,67},{4,68},{5,69},{6,70},{7,71},{8,72},{9,... | collective-permute-start | bytes 1572872 | tf_op jit(solution)/shard_map/ppermute | solution.py:42
  32.0 23.8 %collective-permute-start.5 = (bf16[4,256,256]{2,1,0:T(8,128)(2,1)}, bf16[4,256,256]{2,1,0:T(8,128)(2,1)}, u32[]{:S(2)}, u32[]{:S(2)}) collective-permute-start(bf16[4,256,256]{2,1,0:T(8,128)(2,1)} %get-tuple-element.55), channel_id=1, source_target_pairs={{0,96},{1,97},{2,98},{3,99},{4,100},{5,101},{6,102},{7,103},{8,104... | collective-permute-start | bytes 1572872 | tf_op jit(solution)/shard_map/ppermute | solution.py:42
  65.0 3.0 %collective-permute-start.6 = (f32[512,512]{1,0:T(8,128)}, f32[512,512]{1,0:T(8,128)S(1)}, u32[]{:S(2)}, u32[]{:S(2)}) collective-permute-start(f32[512,512]{1,0:T(8,128)} %shard_map.142.own), channel_id=1, source_target_pairs={{0,32},{1,33},{2,34},{3,35},{4,36},{5,37},{6,38},{7,39},{8,40},{9,... | collective-permute-start | bytes 3145736 | tf_op jit(solution)/shard_map/ppermute | solution.py:42
  76.3 20.7 %all-to-all-start.1 = ((bf16[16,6,16,256]{3,2,1,0:T(8,128)(2,1)}), bf16[16,6,16,256]{3,2,1,0:T(8,128)(2,1)S(1)}, u32[]{:S(2)}, u32[]{:S(2)}) async-start(bf16[16,6,16,256]{3,2,1,0:T(8,128)(2,1)} %get-tuple-element.61), calls=%async_computation.1 | async-start | bytes 1572864 | tf_op jit(solution)/shard_map/all_to_all | solution.py:65
  97.0 30.9 %all-to-all-start.2 = ((bf16[16,12,16,256]{3,2,1,0:T(8,128)(2,1)}), bf16[16,12,16,256]{3,2,1,0:T(8,128)(2,1)S(1)}, u32[]{:S(2)}, u32[]{:S(2)}) async-start(bf16[16,12,16,256]{3,2,1,0:T(8,128)(2,1)} %shard_map.144), calls=%async_computation.2 | async-start | bytes 3145728 | tf_op jit(solution)/shard_map/all_to_all | solution.py:65
  114.1 4.2 %collective-permute-start.7 = (f32[512,512]{1,0:T(8,128)}, f32[512,512]{1,0:T(8,128)S(1)}, u32[]{:S(2)}, u32[]{:S(2)}) collective-permute-start(f32[512,512]{1,0:T(8,128)} %get-tuple-element.68.own), channel_id=1, source_target_pairs={{0,32},{1,33},{2,34},{3,35},{4,36},{5,37},{6,38},{7,39},{8,40},{9,... | collective-permute-start | bytes 3145736 | tf_op jit(solution)/shard_map/ppermute | solution.py:42
  129.1 45.7 %all-to-all-start.3 = ((bf16[16,16,16,256]{3,2,1,0:T(8,128)(2,1)}), bf16[16,16,16,256]{3,2,1,0:T(8,128)(2,1)S(1)}, u32[]{:S(2)}, u32[]{:S(2)}) async-start(bf16[16,16,16,256]{3,2,1,0:T(8,128)(2,1)} %get-tuple-element.80), calls=%async_computation.3 | async-start | bytes 4194304 | tf_op jit(solution)/shard_map/all_to_all | solution.py:65
  135.8 14.7 %collective-permute-start.10 = (bf16[4,256,256]{2,1,0:T(8,128)(2,1)}, bf16[4,256,256]{2,1,0:T(8,128)(2,1)}, u32[]{:S(2)}, u32[]{:S(2)}) collective-permute-start(bf16[4,256,256]{2,1,0:T(8,128)(2,1)} %get-tuple-element.75), channel_id=1, source_target_pairs={{0,64},{1,65},{2,66},{3,67},{4,68},{5,69},{6,70},{7,71},{8,72},{9,... | collective-permute-start | bytes 1572872 | tf_op jit(solution)/shard_map/ppermute | solution.py:42
  138.8 16.2 %collective-permute-start.8 = (bf16[4,256,256]{2,1,0:T(8,128)(2,1)}, bf16[4,256,256]{2,1,0:T(8,128)(2,1)S(1)}, u32[]{:S(2)}, u32[]{:S(2)}) collective-permute-start(bf16[4,256,256]{2,1,0:T(8,128)(2,1)} %get-tuple-element.73), channel_id=1, source_target_pairs={{0,32},{1,33},{2,34},{3,35},{4,36},{5,37},{6,38},{7,39},{8,40},{9,... | collective-permute-start | bytes 1572872 | tf_op jit(solution)/shard_map/ppermute | solution.py:42
  139.7 22.0 %collective-permute-start.9 = (bf16[4,256,256]{2,1,0:T(8,128)(2,1)}, bf16[4,256,256]{2,1,0:T(8,128)(2,1)}, u32[]{:S(2)}, u32[]{:S(2)}) collective-permute-start(bf16[4,256,256]{2,1,0:T(8,128)(2,1)} %get-tuple-element.74), channel_id=1, source_target_pairs={{0,64},{1,65},{2,66},{3,67},{4,68},{5,69},{6,70},{7,71},{8,72},{9,... | collective-permute-start | bytes 1572872 | tf_op jit(solution)/shard_map/ppermute | solution.py:42
  150.5 11.2 %collective-permute-start.11 = (bf16[4,256,256]{2,1,0:T(8,128)(2,1)}, bf16[4,256,256]{2,1,0:T(8,128)(2,1)}, u32[]{:S(2)}, u32[]{:S(2)}) collective-permute-start(bf16[4,256,256]{2,1,0:T(8,128)(2,1)} %collective-permute-done.10), channel_id=1, source_target_pairs={{0,32},{1,33},{2,34},{3,35},{4,36},{5,37},{6,38},{7,39},{8,40},{9,... | collective-permute-start | bytes 1572872 | tf_op jit(solution)/shard_map/ppermute | solution.py:42
  155.0 20.2 %copy-start.6 = (bf16[4,256,256]{2,1,0:T(8,128)(2,1)}, bf16[4,256,256]{2,1,0:T(8,128)(2,1)S(1)}, u32[]{:S(2)}) copy-start(bf16[4,256,256]{2,1,0:T(8,128)(2,1)S(1)} %collective-permute-done.8.back1) | copy-start | bytes 1572868
  161.8 4.9 %collective-permute-start.14 = (bf16[9,16,256]{2,1,0:T(8,128)(2,1)S(1)}, bf16[9,16,256]{2,1,0:T(8,128)(2,1)S(1)}, u32[]{:S(2)}, u32[]{:S(2)}) collective-permute-start(bf16[9,16,256]{2,1,0:T(8,128)(2,1)S(1)} %get-tuple-element.93), channel_id=1, source_target_pairs={{0,68},{1,69},{2,70},{3,71},{4,64},{5,65},{6,66},{7,67},{8,76},{9,... | collective-permute-start | bytes 221192 | tf_op jit(solution)/shard_map/ppermute | solution.py:42
  164.6 4.7 %collective-permute-start.13 = (bf16[9,16,256]{2,1,0:T(8,128)(2,1)S(1)}, bf16[9,16,256]{2,1,0:T(8,128)(2,1)S(1)}, u32[]{:S(2)}, u32[]{:S(2)}) collective-permute-start(bf16[9,16,256]{2,1,0:T(8,128)(2,1)S(1)} %get-tuple-element.92), channel_id=1, source_target_pairs={{0,64},{1,65},{2,66},{3,67},{4,68},{5,69},{6,70},{7,71},{8,72},{9,... | collective-permute-start | bytes 221192 | tf_op jit(solution)/shard_map/ppermute | solution.py:42
  164.9 4.3 %collective-permute-start.12 = (bf16[9,16,256]{2,1,0:T(8,128)(2,1)S(1)}, bf16[9,16,256]{2,1,0:T(8,128)(2,1)S(1)}, u32[]{:S(2)}, u32[]{:S(2)}) collective-permute-start(bf16[9,16,256]{2,1,0:T(8,128)(2,1)S(1)} %get-tuple-element.93), channel_id=1, source_target_pairs={{0,4},{1,5},{2,6},{3,7},{4,0},{5,1},{6,2},{7,3},{8,12},{9,13},{10,... | collective-permute-start | bytes 221192 | tf_op jit(solution)/shard_map/ppermute | solution.py:42
  169.3 4.0 %collective-permute-start.15 = (f32[9,16,256]{2,1,0:T(8,128)S(1)}, f32[9,16,256]{2,1,0:T(8,128)S(1)}, u32[]{:S(2)}, u32[]{:S(2)}) collective-permute-start(f32[9,16,256]{2,1,0:T(8,128)S(1)} %fusion.4), channel_id=1, source_target_pairs={{0,32},{1,33},{2,34},{3,35},{4,36},{5,37},{6,38},{7,39},{8,40},{9,... | collective-permute-start | bytes 442376 | tf_op jit(solution)/shard_map/ppermute | solution.py:42
  175.3 7.0 %collective-permute-start.18 = (bf16[12,16,256]{2,1,0:T(8,128)(2,1)S(1)}, bf16[12,16,256]{2,1,0:T(8,128)(2,1)S(1)}, u32[]{:S(2)}, u32[]{:S(2)}) collective-permute-start(bf16[12,16,256]{2,1,0:T(8,128)(2,1)S(1)} %get-tuple-element.89), channel_id=1, source_target_pairs={{0,68},{1,69},{2,70},{3,71},{4,64},{5,65},{6,66},{7,67},{8,76},{9,... | collective-permute-start | bytes 294920 | tf_op jit(solution)/shard_map/ppermute | solution.py:42
  176.4 5.8 %collective-permute-start.17 = (bf16[12,16,256]{2,1,0:T(8,128)(2,1)S(1)}, bf16[12,16,256]{2,1,0:T(8,128)(2,1)S(1)}, u32[]{:S(2)}, u32[]{:S(2)}) collective-permute-start(bf16[12,16,256]{2,1,0:T(8,128)(2,1)S(1)} %get-tuple-element.88), channel_id=1, source_target_pairs={{0,64},{1,65},{2,66},{3,67},{4,68},{5,69},{6,70},{7,71},{8,72},{9,... | collective-permute-start | bytes 294920 | tf_op jit(solution)/shard_map/ppermute | solution.py:42
  177.2 5.8 %collective-permute-start.16 = (bf16[12,16,256]{2,1,0:T(8,128)(2,1)S(1)}, bf16[12,16,256]{2,1,0:T(8,128)(2,1)S(1)}, u32[]{:S(2)}, u32[]{:S(2)}) collective-permute-start(bf16[12,16,256]{2,1,0:T(8,128)(2,1)S(1)} %get-tuple-element.89), channel_id=1, source_target_pairs={{0,4},{1,5},{2,6},{3,7},{4,0},{5,1},{6,2},{7,3},{8,12},{9,13},{10,... | collective-permute-start | bytes 294920 | tf_op jit(solution)/shard_map/ppermute | solution.py:42
  183.1 2.6 %collective-permute-start.19 = (f32[12,16,256]{2,1,0:T(8,128)S(1)}, f32[12,16,256]{2,1,0:T(8,128)S(1)}, u32[]{:S(2)}, u32[]{:S(2)}) collective-permute-start(f32[12,16,256]{2,1,0:T(8,128)S(1)} %fusion.2), channel_id=1, source_target_pairs={{0,32},{1,33},{2,34},{3,35},{4,36},{5,37},{6,38},{7,39},{8,40},{9,... | collective-permute-start | bytes 589832 | tf_op jit(solution)/shard_map/ppermute | solution.py:42
  (4 other events, 4.5 us)
Sparse Core Ops, SparseCore 0:
  15.8 62.0 all-gather.2

commit v6 on v4

--- a/solution.py
+++ b/solution.py
@@ -237,7 +237,7 @@
     ).astype(BF)
 
 
-def fold_kernel(extent, meta, cot0, cot1, cot2, cot3, folded, raw, cot, sem):
+def fold_kernel(extent, meta, cot0, cot1, cot2, cot3, folded, turned, raw, cot, sem):
     side = extent // 2
     quarter = side * side
     half = cot.shape[2]
@@ -267,17 +267,19 @@
         return carry
 
     lax.fori_loop(0, images, one, 0)
-
-
-def glow_kernel(loss_scale, folded, pieces, part, up, held, sem):
+    for k in range(4):
+        turned[k] = folded[k].astype(F32).T.astype(BF)
+
+
+def glow_kernel(loss_scale, turned, pieces, part, up, held, sem):
     copy = pltpu.make_async_copy(pieces.at[:, pl.ds(0, 8)], held, sem)
     copy.start()
     copy.wait()
     gather_up(held, up)
     total = None
     for k in range(4):
-        scaled = (folded[k].astype(F32) * loss_scale).astype(BF)
-        term = dot(scaled, up[k], 1, 1)
+        scaled = (turned[k].astype(F32) * loss_scale).astype(BF)
+        term = dot(up[k], scaled, 1, 0)
         total = term if total is None else total + term
     part[...] = total
 
@@ -295,44 +297,39 @@
     grads,
     down,
     turned,
-    sums,
     windows,
     sem,
 ):
-    half = folded.shape[2]
-    copies = [
-        pltpu.make_async_copy(ref, windows.at[part], sem.at[part])
-        for part, ref in enumerate((windows_own, windows_pair))
-    ]
-    for copy in copies:
-        copy.start()
+    _, half, pixels = folded.shape
     rows = grads.shape[2]
-    middle = folded.shape[1] // 2
+    middle = pixels // 2
+
+    def fetch(t):
+        copies = []
+        for k in range(4):
+            v = (k // 2 + t // 3) * 4 + k % 2 + t % 3
+            for part, ref in enumerate((windows_own, windows_pair)):
+                place = k * 2 + part
+                target = windows.at[t % 2, pl.ds(place * middle, middle)]
+                copies.append(pltpu.make_async_copy(ref.at[v], target, sem.at[t % 2, place]))
+        for copy in copies:
+            copy.start()
+        return copies
+
+    coming = fetch(0)
     gather_down(pieces, down)
-    glow[...] = swapped_sum(own, got)
-    kept = jnp.concatenate([mask[...]] * (half // mask.shape[1]), axis=1)
+    glow[...] = jnp.concatenate(
+        [own[:, :middle] + got[:, middle:], own[:, middle:] + got[:, :middle]], axis=1
+    ).astype(BF)
+    kept = jnp.broadcast_to(mask[:1, :], (half, pixels))
     for k in range(4):
-        grad = folded[k].astype(F32) * loss_scale + dot(glow[...], down[k], 1, 1)
-        turned[k] = (grad * kept).T.astype(BF)
-    for copy in copies:
-        copy.wait()
-    seen = set()
-    for v in range(16):
-        p, q = v // 4, v % 4
-        users = [k for k in range(4) if 0 <= p - k // 2 < 3 and 0 <= q - k % 2 < 3]
-        term = None
-        for part in range(2):
-            columns = slice(part * middle, (part + 1) * middle)
-            left = jnp.concatenate([turned[k, :, columns] for k in users])
-            piece = dot(left, windows[part, v], 1, 0)
-            term = piece if term is None else term + piece
-        for place, k in enumerate(users):
-            t = (p - k // 2) * 3 + q - k % 2
-            piece = term[place * half : (place + 1) * half]
-            sums[t] = sums[t] + piece if t in seen else piece
-            seen.add(t)
+        grad = folded[k].astype(F32) * loss_scale + dot(down[k], glow[...], 1, 0)
+        turned[:, k * pixels : (k + 1) * pixels] = (grad * kept).astype(BF)
     for t in range(9):
-        total = sums[t].T.astype(BF)
+        present, coming = coming, fetch(t + 1) if t < 8 else []
+        for copy in present:
+            copy.wait()
+        total = dot(turned[...], windows[t % 2], 1, 0).T.astype(BF)
         for f in range(32):
             z, y, x = f // 8, f // 4 % 2, f % 4
             grads[z * 4 + x, y * 9 + t] = total[f * rows : (f + 1) * rows, :]
@@ -437,7 +434,7 @@
         for f in range(32):
             z, y, x = f // 8, f // 4 % 2, f % 4
             grads[z * 4 + x, y * 4 + k] = grad[f * rows : (f + 1) * rows, :]
-        grad = dot(skip[k].astype(F32).T.astype(BF), glow[...], 1, 0).astype(BF)
+        grad = dot(glow[...], skip[k], 1, 0).T.astype(BF)
         for x in range(4):
             for unit in range(8):
                 side_of, step = unit // 4, unit % 4
@@ -546,17 +543,21 @@
     mask = (place[None, :, None] < height[:, None, None]) & (
         place[None, None, :] < width[:, None, None]
     )
+    mask_lanes = jnp.broadcast_to(mask.astype(F32).reshape(1, low_rows), (8, low_rows))
     mask = jnp.broadcast_to(mask.astype(F32).reshape(low_rows, 1), (low_rows, min(128, half)))
 
     windows_own, residual_own = normed_windows(own_meta, images, norm_gain, norm_shift)
     windows_pair, residual_pair = normed_windows(pair_meta, images_pair, norm_gain, norm_shift)
 
-    ready, mask, windows_own, windows_pair = lax.optimization_barrier(
-        (meta, mask, windows_own, windows_pair)
+    ready, mask, mask_lanes, windows_own, windows_pair = lax.optimization_barrier(
+        (meta, mask, mask_lanes, windows_own, windows_pair)
     )
-    folded = kernel_call(
+    folded, turned = kernel_call(
         functools.partial(fold_kernel, extent),
-        jax.ShapeDtypeStruct((4, low_rows, half), BF),
+        (
+            jax.ShapeDtypeStruct((4, low_rows, half), BF),
+            jax.ShapeDtypeStruct((4, half, low_rows), BF),
+        ),
         flops=0,
         moved_bytes=3 << 20,
         scratch=(
@@ -565,11 +566,11 @@
             pltpu.SemaphoreType.DMA((4,)),
         ),
         in_specs=[SCALARS] + [pl.BlockSpec(memory_space=pl.ANY)] * 4,
-        out_specs=WHOLE,
+        out_specs=(WHOLE, WHOLE),
     )(ready, *arrived)
     glow_part = kernel_call(
         functools.partial(glow_kernel, loss_scale),
-        jax.ShapeDtypeStruct((low_rows, channels), F32),
+        jax.ShapeDtypeStruct((channels, low_rows), F32),
         flops=8 * low_rows * channels * half,
         moved_bytes=3 << 20,
         scratch=(
@@ -579,27 +580,26 @@
         ),
         in_specs=[WHOLE, pl.BlockSpec(memory_space=pl.ANY)],
         out_specs=WHOLE,
-    )(folded, up_down)
+    )(turned, up_down)
     glow_got = send(glow_part, "c")
 
     glow, conv_grads = kernel_call(
         functools.partial(grad_conv_kernel, loss_scale),
         (
-            jax.ShapeDtypeStruct((low_rows, channels), BF),
+            jax.ShapeDtypeStruct((channels, low_rows), BF),
             jax.ShapeDtypeStruct((16, 18, rows, half), BF),
         ),
         flops=80 * low_rows * channels * half,
         moved_bytes=15 << 20,
         scratch=(
             pltpu.VMEM((4, half, channels), BF),
-            pltpu.VMEM((4, half, low_rows), BF),
-            pltpu.VMEM((9, half, channels), F32),
-            pltpu.VMEM((2, *windows_own.shape), BF),
-            pltpu.SemaphoreType.DMA((2,)),
+            pltpu.VMEM((half, 4 * low_rows), BF),
+            pltpu.VMEM((2, 4 * low_rows, channels), BF),
+            pltpu.SemaphoreType.DMA((2, 8)),
         ),
         in_specs=[WHOLE] * 5 + [pl.BlockSpec(memory_space=pl.ANY)] * 2,
         out_specs=(WHOLE, WHOLE),
-    )(mask, glow_part, glow_got, folded, up_down, windows_own, windows_pair)
+    )(mask_lanes, glow_part, glow_got, turned, up_down, windows_own, windows_pair)
     conv_grads = over_plane(conv_grads)
     glow, windows_own, windows_pair = lax.optimization_barrier((glow, windows_own, windows_pair))
 

time: 187 us -> 190 us (1.016)
  Pallas kernels: 61 us -> 63.5 us
    pallas_call x1, Pallas kernels: 12.9 us -> 15 us  [per_device(): kernel_call(functools.partial(grad_conv_kernel, loss_scale), (jax.ShapeDt...]
  transfers between devices with their start and end apart: 19 -> 19, of which waited for: 10 -> 10; matrix products, arithmetic and copies ran while one was open for 4% -> 4% of each run, Pallas kernels for 33% -> 34%
where the time goes in v6:
time: 190 us; the launch traced here: 189 us
  Pallas kernels  63.5 us (33%)
  waiting for transfers between devices  54.2 us (29%)
  starting transfers between devices  40.7 us (21%)
  between operations  14.5 us (8%)
  local copies, waits for them, and re-layouts  12.5 us (7%)
  other arithmetic  4.02 us (2%)
    all_to_all x3, waiting for transfers between devices, over_plane(): lax.all_to_all(blocks, 'fsdp', split_axis=0, concat_axis=0, axis_index_gr...  36.8 us
    ppermute x15, starting transfers between devices, send(): return lax.ppermute(value, AXES, STEP[move])  21.4 us
    all_to_all x3, starting transfers between devices, over_plane(): lax.all_to_all(blocks, 'fsdp', split_axis=0, concat_axis=0, axis_index_gr...  19.3 us
    ppermute x15, waiting for transfers between devices, send(): return lax.ppermute(value, AXES, STEP[move])  17.4 us
    pallas_call x1, Pallas kernels, per_device(): kernel_call(functools.partial(grad_conv_kernel, loss_scale), (jax.ShapeDt...  15 us
    pallas_call x2, Pallas kernels, normed_windows(): kernel_call(functools.partial(norm_kernel, extent), (jax.ShapeDtypeStruct...  13 us
    pallas_call x1, Pallas kernels, per_device(): kernel_call(conv_kernel, (jax.ShapeDtypeStruct((4, low_rows, half), F32),...  12.6 us
    pallas_call x1, Pallas kernels, per_device(): kernel_call(functools.partial(output_kernel, extent, loss_scale), (*(bloc...  8.14 us
  transfers between devices with their start and end apart: 19, of which 10 were waited for; matrix products, arithmetic and copies ran while one was open for 4% of the time, Pallas kernels for 34%

profile of v6, /device:TPU:1, one launch (start us, length us, event | category | flops | bytes accessed | tf_op | source)
XLA Modules:
  0.0 189.4 jit_solution(13505048280291794404)
XLA Ops:
  9.1 2.2 %collective-permute-start.2 = (bf16[21,16,256]{2,1,0:T(8,128)(2,1)S(1)}, bf16[21,16,256]{2,1,0:T(8,128)(2,1)S(1)}, u32[]{:S(2)}, u32[]{:S(2)}) collective-permute-start(bf16[21,16,256]{2,1,0:T(8,128)(2,1)S(1)} %pad_maximum_fusion.1), channel_id=1, source_target_pairs={{0,4},{1,5},{2,6},{3,7},{4,0},{5,1},{6,2},{7,3},{8,12},{9,13},{10,... | collective-permute-start | bytes 516104 | tf_op jit(solution)/shard_map/ppermute | solution.py:41
  11.3 3.0 %shard_map.140 = (bf16[4,256,256]{2,1,0:T(8,128)(2,1)}, bf16[4,256,256]{2,1,0:T(8,128)(2,1)}, bf16[4,256,256]{2,1,0:T(8,128)(2,1)}, bf16[4,256,256]{2,1,0:T(8,128)(2,1)}) custom-call(s32[1]{0:T(128)} %bitcast.number, bf16[8,256,512]{2,1,0:T(8,128)(2,1)} %bitcast.72), custom_call_target="tpu_custom_call" | custom-call | bytes 4194304 | tf_op jit(solution)/shard_map/pallas_call | solution.py:499
  15.8 1.6 broadcast_in_dim.78
  17.4 8.0 %all-to-all-start = ((bf16[16,16,16,256]{3,2,1,0:T(8,128)(2,1)}), bf16[16,16,16,256]{3,2,1,0:T(8,128)(2,1)S(1)}, u32[]{:S(2)}, u32[]{:S(2)}) async-start(bf16[16,16,16,256]{3,2,1,0:T(8,128)(2,1)} %broadcast_in_dim.78), calls=%async_computation | async-start | bytes 4194304 | tf_op jit(solution)/shard_map/all_to_all | solution.py:59
  25.5 1.9 %collective-permute-start = (s32[4,2]{0,1:T(2,128)S(1)}, s32[4,2]{0,1:T(2,128)S(1)}, u32[]{:S(2)}, u32[]{:S(2)}) collective-permute-start(s32[4,2]{0,1:T(2,128)S(1)} %pad_add_fusion.2), channel_id=1, source_target_pairs={{0,32},{1,33},{2,34},{3,35},{4,36},{5,37},{6,38},{7,39},{8,40},{9,... | collective-permute-start | bytes 104 | tf_op jit(solution)/shard_map/ppermute | solution.py:41
  29.0 2.9 %collective-permute-start.4 = (bf16[4,256,256]{2,1,0:T(8,128)(2,1)}, bf16[4,256,256]{2,1,0:T(8,128)(2,1)}, u32[]{:S(2)}, u32[]{:S(2)}) collective-permute-start(bf16[4,256,256]{2,1,0:T(8,128)(2,1)} %get-tuple-element.52), channel_id=1, source_target_pairs={{0,64},{1,65},{2,66},{3,67},{4,68},{5,69},{6,70},{7,71},{8,72},{9,... | collective-permute-start | bytes 1572872 | tf_op jit(solution)/shard_map/ppermute | solution.py:41
  34.4 6.5 %shard_map.138 = (bf16[16,256,512]{2,1,0:T(8,128)(2,1)}, bf16[4,256,256]{2,1,0:T(8,128)(2,1)}) custom-call(s32[32]{0:T(128)} %concatenate.37.meta, bf16[4,256,512]{2,1,0:T(8,128)(2,1)} %bitcast.74, f32[1,512]{1,0:T(1,128)} %bitcast.82, f32[1,512]{1,0:T(1,128)} %bitcast.84), custom_call_target="tpu_custom_call" | custom-call | flops 20971520 | bytes 6291456 | tf_op jit(solution)/shard_map/pallas_call | solution.py:187
  40.9 6.5 %shard_map.139 = (bf16[16,256,512]{2,1,0:T(8,128)(2,1)}, bf16[4,256,256]{2,1,0:T(8,128)(2,1)}) custom-call(s32[32]{0:T(128)} %concatenate.39.meta, bf16[4,256,512]{2,1,0:T(8,128)(2,1)} %bitcast.18.image, f32[1,512]{1,0:T(1,128)} %bitcast.83, f32[1,512]{1,0:T(1,128)} %bitcast.85), custom_call_target="tpu_custom_call" | custom-call | flops 20971520 | bytes 6291456 | tf_op jit(solution)/shard_map/pallas_call | solution.py:187
  48.9 6.9 %collective-permute-done.5.cot3 = bf16[4,256,256]{2,1,0:T(8,128)(2,1)} collective-permute-done((bf16[4,256,256]{2,1,0:T(8,128)(2,1)}, bf16[4,256,256]{2,1,0:T(8,128)(2,1)}, u32[]{:S(2)}, u32[]{:S(2)}) %collective-permute-start.5) | collective-permute-done | bytes 524320 | tf_op jit(solution)/shard_map/ppermute | solution.py:41
  55.7 3.9 %shard_map.141 = (bf16[4,512,256]{2,1,0:T(8,128)(2,1)}, bf16[4,256,512]{2,1,0:T(8,128)(2,1)}) custom-call(s32[32]{0:T(128)} %concatenate.35.meta, bf16[4,256,256]{2,1,0:T(8,128)(2,1)} %get-tuple-element.50.cot0, bf16[4,256,256]{2,1,0:T(8,128)(2,1)} %collective-permute-done.3.cot1, bf16[4,256,256]{2,1,0:T(8,128)(2,1)} %collective-permute-done.4.cot2, ...), custom_call_target="tpu_custom_call" | custom-call | bytes 3145728 | tf_op jit(solution)/shard_map/pallas_call | solution.py:555
  59.7 1.3 copy-done.1
  61.0 4.2 %shard_map.142.own = f32[512,512]{1,0:T(8,128)} custom-call(bf16[4,256,512]{2,1,0:T(8,128)(2,1)} %get-tuple-element.54.turned.folded, bf16[16,16,16,256]{3,2,1,0:T(8,128)(2,1)} %copy-done.1), custom_call_target="tpu_custom_call" | custom-call | flops 536870912 | bytes 3145728 | tf_op jit(solution)/shard_map/pallas_call | solution.py:571
  65.4 2.8 %collective-permute-done.6.got = f32[512,512]{1,0:T(8,128)S(1)} collective-permute-done((f32[512,512]{1,0:T(8,128)}, f32[512,512]{1,0:T(8,128)S(1)}, u32[]{:S(2)}, u32[]{:S(2)}) %collective-permute-start.6) | collective-permute-done | bytes 1048608 | tf_op jit(solution)/shard_map/ppermute | solution.py:41
  68.2 1.0 copy-done.11
  69.1 15.0 %shard_map.143 = (bf16[512,512]{1,0:T(8,128)(2,1)}, bf16[16,18,16,256]{3,2,1,0:T(8,128)(2,1)}) custom-call(f32[8,512]{1,0:T(8,128)} %broadcast_in_dim.75.mask, f32[512,512]{1,0:T(8,128)} %shard_map.142.own, f32[512,512]{1,0:T(8,128)} %copy-done.11, bf16[4,256,512]{2,1,0:T(8,128)(2,1)} %get-tuple-element.54.turned.folded, ...), custom_call_target="tpu_custom_call" | custom-call | flops 5368709120 | bytes 15728640 | tf_op jit(solution)/shard_map/pallas_call | solution.py:586
  84.1 6.9 %all-to-all-start.1 = ((bf16[16,18,16,256]{3,2,1,0:T(8,128)(2,1)}), bf16[16,18,16,256]{3,2,1,0:T(8,128)(2,1)S(1)}, u32[]{:S(2)}, u32[]{:S(2)}) async-start(bf16[16,18,16,256]{3,2,1,0:T(8,128)(2,1)} %get-tuple-element.58), calls=%async_computation.1 | async-start | bytes 4718592 | tf_op jit(solution)/shard_map/all_to_all | solution.py:59
  91.1 12.6 %shard_map.144 = (f32[4,512,256]{2,1,0:T(8,128)}, bf16[4,512,256]{2,1,0:T(8,128)(2,1)}, f32[512,512]{1,0:T(8,128)}) custom-call(f32[512,128]{1,0:T(8,128)} %broadcast_in_dim.74.mask, bf16[16,18,16,256]{3,2,1,0:T(8,128)(2,1)} %bitcast.92, bf16[16,16,16,256]{3,2,1,0:T(8,128)(2,1)} %copy-done.1, bf16[16,256,512]{2,1,0:T(8,128)(2,1)} %get-tuple-element.61.windows_own, ...), custom_call_target="tpu_custom_call" | custom-call | flops 5368709120 | bytes 18874368 | tf_op jit(solution)/shard_map/pallas_call | solution.py:606
  104.1 2.5 %collective-permute-done.7.got = f32[512,512]{1,0:T(8,128)S(1)} collective-permute-done((f32[512,512]{1,0:T(8,128)}, f32[512,512]{1,0:T(8,128)S(1)}, u32[]{:S(2)}, u32[]{:S(2)}) %collective-permute-start.7) | collective-permute-done | bytes 1048608 | tf_op jit(solution)/shard_map/ppermute | solution.py:41
  106.6 1.0 copy-done.2
  107.6 8.1 %shard_map.145 = (bf16[4,256,256]{2,1,0:T(8,128)(2,1)}, bf16[4,256,256]{2,1,0:T(8,128)(2,1)}, bf16[4,256,256]{2,1,0:T(8,128)(2,1)}, bf16[4,256,256]{2,1,0:T(8,128)(2,1)}, bf16[16,16,16,256]{3,2,1,0:T(8,128)(2,1)}) custom-call(s32[32]{0:T(128)} %concatenate.35.meta, f32[512,128]{1,0:T(8,128)} %broadcast_in_dim.74.mask, f32[512,512]{1,0:T(8,128)} %get-tuple-element.65.own, ...), custom_call_target="tpu_custom_call" | custom-call | flops 1610612736 | bytes 14680064 | tf_op jit(solution)/shard_map/pallas_call | solution.py:621
  115.7 11.9 %all-to-all-done.1 = bf16[16,18,16,256]{3,2,1,0:T(8,128)(2,1)S(1)} async-done(((bf16[16,18,16,256]{3,2,1,0:T(8,128)(2,1)}), bf16[16,18,16,256]{3,2,1,0:T(8,128)(2,1)S(1)}, u32[]{:S(2)}, u32[]{:S(2)}) %all-to-all-start.1) | async-done | bytes 2359328 | tf_op jit(solution)/shard_map/all_to_all | solution.py:59
  127.6 4.4 %all-to-all-start.2 = ((bf16[16,16,16,256]{3,2,1,0:T(8,128)(2,1)}), bf16[16,16,16,256]{3,2,1,0:T(8,128)(2,1)}, u32[]{:S(2)}, u32[]{:S(2)}) async-start(bf16[16,16,16,256]{3,2,1,0:T(8,128)(2,1)} %get-tuple-element.70), calls=%async_computation.2 | async-start | bytes 4194304 | tf_op jit(solution)/shard_map/all_to_all | solution.py:59
  132.4 4.2 %collective-permute-start.10 = (bf16[4,256,256]{2,1,0:T(8,128)(2,1)}, bf16[4,256,256]{2,1,0:T(8,128)(2,1)S(1)}, u32[]{:S(2)}, u32[]{:S(2)}) collective-permute-start(bf16[4,256,256]{2,1,0:T(8,128)(2,1)} %get-tuple-element.74), channel_id=1, source_target_pairs={{0,96},{1,97},{2,98},{3,99},{4,100},{5,101},{6,102},{7,103},{8,104... | collective-permute-start | bytes 1572872 | tf_op jit(solution)/shard_map/ppermute | solution.py:41
  136.8 24.9 %all-to-all-done.2 = bf16[16,16,16,256]{3,2,1,0:T(8,128)(2,1)} async-done(((bf16[16,16,16,256]{3,2,1,0:T(8,128)(2,1)}), bf16[16,16,16,256]{3,2,1,0:T(8,128)(2,1)}, u32[]{:S(2)}, u32[]{:S(2)}) %all-to-all-start.2) | async-done | bytes 2097184 | tf_op jit(solution)/shard_map/all_to_all | solution.py:59
  161.6 1.9 %convert_reduce_fusion.1 = f32[16,16,256]{2,1,0:T(8,128)S(1)} fusion(bf16[16,16,16,256]{3,2,1,0:T(8,128)(2,1)} %all-to-all-done.2), kind=kLoop, calls=%fused_computation.1 | loop fusion | flops 2031616 | bytes 2359296 | tf_op jit(solution)/shard_map/reduce_sum | solution.py:643
  163.8 1.4 collective-permute-start.11
  165.2 2.7 %collective-permute-start.12 = (bf16[21,16,256]{2,1,0:T(8,128)(2,1)S(1)}, bf16[21,16,256]{2,1,0:T(8,128)(2,1)S(1)}, u32[]{:S(2)}, u32[]{:S(2)}) collective-permute-start(bf16[21,16,256]{2,1,0:T(8,128)(2,1)S(1)} %get-tuple-element.84), channel_id=1, source_target_pairs={{0,64},{1,65},{2,66},{3,67},{4,68},{5,69},{6,70},{7,71},{8,72},{9,... | collective-permute-start | bytes 516104 | tf_op jit(solution)/shard_map/ppermute | solution.py:41
  167.9 3.6 %shard_map.146 = f32[8,256,512]{2,1,0:T(8,128)} custom-call(s32[1]{0:T(128)} %bitcast.number, bf16[4,256,256]{2,1,0:T(8,128)(2,1)} %get-tuple-element.75.back0, bf16[4,256,256]{2,1,0:T(8,128)(2,1)} %copy-done.5, bf16[4,256,256]{2,1,0:T(8,128)(2,1)} %copy-done.6, bf16[4,256,256]{2,1,0:T(8,128)(2,1)} %copy-done.4), custom_call_target="tpu_custom_call" | custom-call | bytes 6291456 | tf_op jit(solution)/shard_map/pallas_call | solution.py:660
  171.5 1.7 collective-permute-done.12
  173.2 1.1 collective-permute-done.13
  174.5 4.5 %collective-permute-start.14 = (f32[21,16,256]{2,1,0:T(8,128)S(1)}, f32[21,16,256]{2,1,0:T(8,128)S(1)}, u32[]{:S(2)}, u32[]{:S(2)}) collective-permute-start(f32[21,16,256]{2,1,0:T(8,128)S(1)} %fusion.1), channel_id=1, source_target_pairs={{0,32},{1,33},{2,34},{3,35},{4,36},{5,37},{6,38},{7,39},{8,40},{9,... | collective-permute-start | bytes 1032200 | tf_op jit(solution)/shard_map/ppermute | solution.py:41
  178.9 1.3 collective-permute-done.14
  (94 shorter events, 12.6 us)
Async XLA Ops:
  7.2 1.0 copy-start
  7.2 83.9 %all-gather.3.cloned.1.call-start = ((), (), s32[]{:S(2)}) async-start(), calls=%async_computation.3 | async-start | bytes 2506752 | tf_op jit(solution)/shard_map/all_gather | solution.py:515
  9.1 5.9 %collective-permute-start.2 = (bf16[21,16,256]{2,1,0:T(8,128)(2,1)S(1)}, bf16[21,16,256]{2,1,0:T(8,128)(2,1)S(1)}, u32[]{:S(2)}, u32[]{:S(2)}) collective-permute-start(bf16[21,16,256]{2,1,0:T(8,128)(2,1)S(1)} %pad_maximum_fusion.1), channel_id=1, source_target_pairs={{0,4},{1,5},{2,6},{3,7},{4,0},{5,1},{6,2},{7,3},{8,12},{9,13},{10,... | collective-permute-start | bytes 516104 | tf_op jit(solution)/shard_map/ppermute | solution.py:41
  17.4 8.0 %copy-start.7 = (s32[4,1]{0,1:T(1,128)S(1)}, s32[4,1]{0,1:T(1,128)}, u32[]{:S(2)}) copy-start(s32[4,1]{0,1:T(1,128)} %param.12) | copy-start | bytes 52
  17.4 8.0 %copy-start.8 = (s32[4]{0:T(128)S(1)}, s32[4]{0:T(128)}, u32[]{:S(2)}) copy-start(s32[4]{0:T(128)} %param.13) | copy-start | bytes 52
  17.4 10.0 %copy-start.3 = (bf16[4,16,16,512]{3,2,1,0:T(8,128)(2,1)S(1)}, bf16[4,16,16,512]{3,2,1,0:T(8,128)(2,1)}, u32[]{:S(2)}) copy-start(bf16[4,16,16,512]{3,2,1,0:T(8,128)(2,1)} %param.11) | copy-start | bytes 3145732
  17.4 10.8 %copy-start.9 = (s32[8]{0:T(128)S(1)}, s32[8]{0:T(128)}, u32[]{:S(2)}) copy-start(s32[8]{0:T(128)} %param.14) | copy-start | bytes 100
  17.4 10.8 %copy-start.10 = (s32[8]{0:T(128)S(1)}, s32[8]{0:T(128)}, u32[]{:S(2)}) copy-start(s32[8]{0:T(128)} %param.15) | copy-start | bytes 100
  17.4 42.2 %all-to-all-start = ((bf16[16,16,16,256]{3,2,1,0:T(8,128)(2,1)}), bf16[16,16,16,256]{3,2,1,0:T(8,128)(2,1)S(1)}, u32[]{:S(2)}, u32[]{:S(2)}) async-start(bf16[16,16,16,256]{3,2,1,0:T(8,128)(2,1)} %broadcast_in_dim.78), calls=%async_computation | async-start | bytes 4194304 | tf_op jit(solution)/shard_map/all_to_all | solution.py:59
  25.5 2.7 %collective-permute-start = (s32[4,2]{0,1:T(2,128)S(1)}, s32[4,2]{0,1:T(2,128)S(1)}, u32[]{:S(2)}, u32[]{:S(2)}) collective-permute-start(s32[4,2]{0,1:T(2,128)S(1)} %pad_add_fusion.2), channel_id=1, source_target_pairs={{0,32},{1,33},{2,34},{3,35},{4,36},{5,37},{6,38},{7,39},{8,40},{9,... | collective-permute-start | bytes 104 | tf_op jit(solution)/shard_map/ppermute | solution.py:41
  27.4 13.5 %collective-permute-start.1 = (bf16[4,16,16,512]{3,2,1,0:T(8,128)(2,1)S(1)}, bf16[4,16,16,512]{3,2,1,0:T(8,128)(2,1)}, u32[]{:S(2)}, u32[]{:S(2)}) collective-permute-start(bf16[4,16,16,512]{3,2,1,0:T(8,128)(2,1)S(1)} %copy-done.3), channel_id=1, source_target_pairs={{0,32},{1,33},{2,34},{3,35},{4,36},{5,37},{6,38},{7,39},{8,40},{9,... | collective-permute-start | bytes 3145736 | tf_op jit(solution)/shard_map/ppermute | solution.py:41
  28.7 20.2 %collective-permute-start.3 = (bf16[4,256,256]{2,1,0:T(8,128)(2,1)}, bf16[4,256,256]{2,1,0:T(8,128)(2,1)}, u32[]{:S(2)}, u32[]{:S(2)}) collective-permute-start(bf16[4,256,256]{2,1,0:T(8,128)(2,1)} %get-tuple-element.51), channel_id=1, source_target_pairs={{0,32},{1,33},{2,34},{3,35},{4,36},{5,37},{6,38},{7,39},{8,40},{9,... | collective-permute-start | bytes 1572872 | tf_op jit(solution)/shard_map/ppermute | solution.py:41
  29.0 19.8 %collective-permute-start.4 = (bf16[4,256,256]{2,1,0:T(8,128)(2,1)}, bf16[4,256,256]{2,1,0:T(8,128)(2,1)}, u32[]{:S(2)}, u32[]{:S(2)}) collective-permute-start(bf16[4,256,256]{2,1,0:T(8,128)(2,1)} %get-tuple-element.52), channel_id=1, source_target_pairs={{0,64},{1,65},{2,66},{3,67},{4,68},{5,69},{6,70},{7,71},{8,72},{9,... | collective-permute-start | bytes 1572872 | tf_op jit(solution)/shard_map/ppermute | solution.py:41
  32.0 23.8 %collective-permute-start.5 = (bf16[4,256,256]{2,1,0:T(8,128)(2,1)}, bf16[4,256,256]{2,1,0:T(8,128)(2,1)}, u32[]{:S(2)}, u32[]{:S(2)}) collective-permute-start(bf16[4,256,256]{2,1,0:T(8,128)(2,1)} %get-tuple-element.53), channel_id=1, source_target_pairs={{0,96},{1,97},{2,98},{3,99},{4,100},{5,101},{6,102},{7,103},{8,104... | collective-permute-start | bytes 1572872 | tf_op jit(solution)/shard_map/ppermute | solution.py:41
  59.7 1.3 copy-start.1
  65.2 3.0 %collective-permute-start.6 = (f32[512,512]{1,0:T(8,128)}, f32[512,512]{1,0:T(8,128)S(1)}, u32[]{:S(2)}, u32[]{:S(2)}) collective-permute-start(f32[512,512]{1,0:T(8,128)} %shard_map.142.own), channel_id=1, source_target_pairs={{0,32},{1,33},{2,34},{3,35},{4,36},{5,37},{6,38},{7,39},{8,40},{9,... | collective-permute-start | bytes 3145736 | tf_op jit(solution)/shard_map/ppermute | solution.py:41
  68.2 1.0 copy-start.11
  84.1 43.5 %all-to-all-start.1 = ((bf16[16,18,16,256]{3,2,1,0:T(8,128)(2,1)}), bf16[16,18,16,256]{3,2,1,0:T(8,128)(2,1)S(1)}, u32[]{:S(2)}, u32[]{:S(2)}) async-start(bf16[16,18,16,256]{3,2,1,0:T(8,128)(2,1)} %get-tuple-element.58), calls=%async_computation.1 | async-start | bytes 4718592 | tf_op jit(solution)/shard_map/all_to_all | solution.py:59
  103.6 2.9 %collective-permute-start.7 = (f32[512,512]{1,0:T(8,128)}, f32[512,512]{1,0:T(8,128)S(1)}, u32[]{:S(2)}, u32[]{:S(2)}) collective-permute-start(f32[512,512]{1,0:T(8,128)} %get-tuple-element.65.own), channel_id=1, source_target_pairs={{0,32},{1,33},{2,34},{3,35},{4,36},{5,37},{6,38},{7,39},{8,40},{9,... | collective-permute-start | bytes 3145736 | tf_op jit(solution)/shard_map/ppermute | solution.py:41
  106.6 1.0 copy-start.2
  127.6 34.0 %all-to-all-start.2 = ((bf16[16,16,16,256]{3,2,1,0:T(8,128)(2,1)}), bf16[16,16,16,256]{3,2,1,0:T(8,128)(2,1)}, u32[]{:S(2)}, u32[]{:S(2)}) async-start(bf16[16,16,16,256]{3,2,1,0:T(8,128)(2,1)} %get-tuple-element.70), calls=%async_computation.2 | async-start | bytes 4194304 | tf_op jit(solution)/shard_map/all_to_all | solution.py:59
  132.4 31.3 %collective-permute-start.10 = (bf16[4,256,256]{2,1,0:T(8,128)(2,1)}, bf16[4,256,256]{2,1,0:T(8,128)(2,1)S(1)}, u32[]{:S(2)}, u32[]{:S(2)}) collective-permute-start(bf16[4,256,256]{2,1,0:T(8,128)(2,1)} %get-tuple-element.74), channel_id=1, source_target_pairs={{0,96},{1,97},{2,98},{3,99},{4,100},{5,101},{6,102},{7,103},{8,104... | collective-permute-start | bytes 1572872 | tf_op jit(solution)/shard_map/ppermute | solution.py:41
  136.6 27.1 %collective-permute-start.8 = (bf16[4,256,256]{2,1,0:T(8,128)(2,1)}, bf16[4,256,256]{2,1,0:T(8,128)(2,1)S(1)}, u32[]{:S(2)}, u32[]{:S(2)}) collective-permute-start(bf16[4,256,256]{2,1,0:T(8,128)(2,1)} %get-tuple-element.72), channel_id=1, source_target_pairs={{0,32},{1,33},{2,34},{3,35},{4,36},{5,37},{6,38},{7,39},{8,40},{9,... | collective-permute-start | bytes 1572872 | tf_op jit(solution)/shard_map/ppermute | solution.py:41
  136.6 27.1 %collective-permute-start.9 = (bf16[4,256,256]{2,1,0:T(8,128)(2,1)}, bf16[4,256,256]{2,1,0:T(8,128)(2,1)S(1)}, u32[]{:S(2)}, u32[]{:S(2)}) collective-permute-start(bf16[4,256,256]{2,1,0:T(8,128)(2,1)} %get-tuple-element.73), channel_id=1, source_target_pairs={{0,64},{1,65},{2,66},{3,67},{4,68},{5,69},{6,70},{7,71},{8,72},{9,... | collective-permute-start | bytes 1572872 | tf_op jit(solution)/shard_map/ppermute | solution.py:41
  163.7 4.2 %copy-start.4 = (bf16[4,256,256]{2,1,0:T(8,128)(2,1)}, bf16[4,256,256]{2,1,0:T(8,128)(2,1)S(1)}, u32[]{:S(2)}) copy-start(bf16[4,256,256]{2,1,0:T(8,128)(2,1)S(1)} %collective-permute-done.10.back3) | copy-start | bytes 1572868
  163.7 4.2 %copy-start.5 = (bf16[4,256,256]{2,1,0:T(8,128)(2,1)}, bf16[4,256,256]{2,1,0:T(8,128)(2,1)S(1)}, u32[]{:S(2)}) copy-start(bf16[4,256,256]{2,1,0:T(8,128)(2,1)S(1)} %collective-permute-done.8.back1) | copy-start | bytes 1572868
  163.7 4.2 %copy-start.6 = (bf16[4,256,256]{2,1,0:T(8,128)(2,1)}, bf16[4,256,256]{2,1,0:T(8,128)(2,1)S(1)}, u32[]{:S(2)}) copy-start(bf16[4,256,256]{2,1,0:T(8,128)(2,1)S(1)} %collective-permute-done.9.back2) | copy-start | bytes 1572868
  163.8 7.7 %collective-permute-start.11 = (bf16[21,16,256]{2,1,0:T(8,128)(2,1)S(1)}, bf16[21,16,256]{2,1,0:T(8,128)(2,1)S(1)}, u32[]{:S(2)}, u32[]{:S(2)}) collective-permute-start(bf16[21,16,256]{2,1,0:T(8,128)(2,1)S(1)} %get-tuple-element.85), channel_id=1, source_target_pairs={{0,4},{1,5},{2,6},{3,7},{4,0},{5,1},{6,2},{7,3},{8,12},{9,13},{10,... | collective-permute-start | bytes 516104 | tf_op jit(solution)/shard_map/ppermute | solution.py:41
  165.2 8.0 %collective-permute-start.12 = (bf16[21,16,256]{2,1,0:T(8,128)(2,1)S(1)}, bf16[21,16,256]{2,1,0:T(8,128)(2,1)S(1)}, u32[]{:S(2)}, u32[]{:S(2)}) collective-permute-start(bf16[21,16,256]{2,1,0:T(8,128)(2,1)S(1)} %get-tuple-element.84), channel_id=1, source_target_pairs={{0,64},{1,65},{2,66},{3,67},{4,68},{5,69},{6,70},{7,71},{8,72},{9,... | collective-permute-start | bytes 516104 | tf_op jit(solution)/shard_map/ppermute | solution.py:41
  167.9 6.5 %collective-permute-start.13 = (bf16[21,16,256]{2,1,0:T(8,128)(2,1)S(1)}, bf16[21,16,256]{2,1,0:T(8,128)(2,1)S(1)}, u32[]{:S(2)}, u32[]{:S(2)}) collective-permute-start(bf16[21,16,256]{2,1,0:T(8,128)(2,1)S(1)} %get-tuple-element.85), channel_id=1, source_target_pairs={{0,68},{1,69},{2,70},{3,71},{4,64},{5,65},{6,66},{7,67},{8,76},{9,... | collective-permute-start | bytes 516104 | tf_op jit(solution)/shard_map/ppermute | solution.py:41
  174.5 5.7 %collective-permute-start.14 = (f32[21,16,256]{2,1,0:T(8,128)S(1)}, f32[21,16,256]{2,1,0:T(8,128)S(1)}, u32[]{:S(2)}, u32[]{:S(2)}) collective-permute-start(f32[21,16,256]{2,1,0:T(8,128)S(1)} %fusion.1), channel_id=1, source_target_pairs={{0,32},{1,33},{2,34},{3,35},{4,36},{5,37},{6,38},{7,39},{8,40},{9,... | collective-permute-start | bytes 1032200 | tf_op jit(solution)/shard_map/ppermute | solution.py:41
Sparse Core Ops, SparseCore 0:
  15.9 62.1 all-gather.2

commit v7 on v4

--- a/solution.py
+++ b/solution.py
@@ -34,6 +34,8 @@
     "h": moved(lambda h, c, z, y, x: (1 - h, c, z, y, x)),
     "hc": moved(lambda h, c, z, y, x: (1 - h, 1 - c, z, y, x)),
 }
+BY_BITS = [(r >> 3 & 1) * 8 + (r >> 1 & 1) * 4 + (r >> 2 & 1) * 2 + (r & 1) for r in range(16)]
+DIAGONAL = [r % 4 * 4 + (r // 4 + r) % 4 for r in range(16)]
 PLANES = [[z * 8 + y * 4 + x for z in range(4) for x in range(4)] for y in range(2)]
 
 
@@ -55,9 +57,10 @@
     return total, send(total, "c")
 
 
-def over_plane(blocks):
+def over_plane(blocks, order=tuple(range(16))):
+    groups = [[plane[place] for place in order] for plane in PLANES]
     return lax.all_to_all(
-        blocks, "fsdp", split_axis=0, concat_axis=0, axis_index_groups=PLANES, tiled=True
+        blocks, "fsdp", split_axis=0, concat_axis=0, axis_index_groups=groups, tiled=True
     )
 
 
@@ -283,29 +286,9 @@
 
 
 def grad_conv_kernel(
-    loss_scale,
-    mask,
-    own,
-    got,
-    folded,
-    pieces,
-    windows_own,
-    windows_pair,
-    glow,
-    grads,
-    down,
-    turned,
-    sums,
-    windows,
-    sem,
+    loss_scale, mask, own, got, folded, pieces, windows_own, windows_pair, glow, grads, down, turned
 ):
     half = folded.shape[2]
-    copies = [
-        pltpu.make_async_copy(ref, windows.at[part], sem.at[part])
-        for part, ref in enumerate((windows_own, windows_pair))
-    ]
-    for copy in copies:
-        copy.start()
     rows = grads.shape[2]
     middle = folded.shape[1] // 2
     gather_down(pieces, down)
@@ -314,28 +297,17 @@
     for k in range(4):
         grad = folded[k].astype(F32) * loss_scale + dot(glow[...], down[k], 1, 1)
         turned[k] = (grad * kept).T.astype(BF)
-    for copy in copies:
-        copy.wait()
-    seen = set()
-    for v in range(16):
-        p, q = v // 4, v % 4
-        users = [k for k in range(4) if 0 <= p - k // 2 < 3 and 0 <= q - k % 2 < 3]
-        term = None
-        for part in range(2):
-            columns = slice(part * middle, (part + 1) * middle)
-            left = jnp.concatenate([turned[k, :, columns] for k in users])
-            piece = dot(left, windows[part, v], 1, 0)
-            term = piece if term is None else term + piece
-        for place, k in enumerate(users):
-            t = (p - k // 2) * 3 + q - k % 2
-            piece = term[place * half : (place + 1) * half]
-            sums[t] = sums[t] + piece if t in seen else piece
-            seen.add(t)
     for t in range(9):
-        total = sums[t].T.astype(BF)
+        total = None
+        for k in range(4):
+            v = (k // 2 + t // 3) * 4 + k % 2 + t % 3
+            for columns, windows in ((slice(0, middle), windows_own), (slice(middle, None), windows_pair)):
+                term = dot(turned[k, :, columns], windows[v], 1, 0)
+                total = term if total is None else total + term
+        total = total.T.astype(BF)
         for f in range(32):
             z, y, x = f // 8, f // 4 % 2, f % 4
-            grads[z * 4 + x, y * 9 + t] = total[f * rows : (f + 1) * rows, :]
+            grads[BY_BITS.index(z * 4 + x), y * 9 + t] = total[f * rows : (f + 1) * rows, :]
 
 
 def conv_kernel(
@@ -436,13 +408,13 @@
         grad = dot(turned, scaled, 1, 0).astype(BF)
         for f in range(32):
             z, y, x = f // 8, f // 4 % 2, f % 4
-            grads[z * 4 + x, y * 4 + k] = grad[f * rows : (f + 1) * rows, :]
+            grads[DIAGONAL.index(z * 4 + x), y * 4 + k] = grad[f * rows : (f + 1) * rows, :]
         grad = dot(skip[k].astype(F32).T.astype(BF), glow[...], 1, 0).astype(BF)
         for x in range(4):
             for unit in range(8):
                 side_of, step = unit // 4, unit % 4
                 first = (x * 4 + step) * rows
-                grads[k * 4 + x, 8 + unit] = grad[
+                grads[DIAGONAL.index(k * 4 + x), 8 + unit] = grad[
                     first : first + rows, side_of * half : (side_of + 1) * half
                 ]
 
@@ -590,17 +562,11 @@
         ),
         flops=80 * low_rows * channels * half,
         moved_bytes=15 << 20,
-        scratch=(
-            pltpu.VMEM((4, half, channels), BF),
-            pltpu.VMEM((4, half, low_rows), BF),
-            pltpu.VMEM((9, half, channels), F32),
-            pltpu.VMEM((2, *windows_own.shape), BF),
-            pltpu.SemaphoreType.DMA((2,)),
-        ),
-        in_specs=[WHOLE] * 5 + [pl.BlockSpec(memory_space=pl.ANY)] * 2,
+        scratch=(pltpu.VMEM((4, half, channels), BF), pltpu.VMEM((4, half, low_rows), BF)),
+        in_specs=[WHOLE] * 7,
         out_specs=(WHOLE, WHOLE),
     )(mask, glow_part, glow_got, folded, up_down, windows_own, windows_pair)
-    conv_grads = over_plane(conv_grads)
+    conv_grads = over_plane(conv_grads, BY_BITS)
     glow, windows_own, windows_pair = lax.optimization_barrier((glow, windows_own, windows_pair))
 
     wide, skip, low_part = kernel_call(
@@ -637,7 +603,7 @@
         out_specs=(WHOLE,) * 5,
     )(meta, mask, low_part, low_got, wide, skip, glow, folded, up_down)
     returned = over_dp(returning)
-    grads = over_plane(grads)
+    grads = over_plane(grads, DIAGONAL)
 
     conv_sum = jnp.sum(conv_grads.astype(F32), axis=0).reshape(2, 9, rows, half)
     grads_sum = jnp.sum(grads.astype(F32), axis=0)

time: 187 us -> 183 us (0.979)
  waiting for transfers between devices: 54.4 us -> 48.1 us
  starting transfers between devices: 40.8 us -> 42.7 us
    all_to_all x3, waiting for transfers between devices: 36.5 us -> 30.2 us  [over_plane(): lax.all_to_all(blocks, 'fsdp', split_axis=0, concat_axis=0, axis_index_gr...]
  transfers between devices with their start and end apart: 19 -> 19, of which waited for: 10 -> 11; matrix products, arithmetic and copies ran while one was open for 4% -> 4% of each run, Pallas kernels for 33% -> 33%
where the time goes in v7:
time: 183 us; the launch traced here: 182 us
  Pallas kernels  60.5 us (33%)
  waiting for transfers between devices  48.1 us (26%)
  starting transfers between devices  42.7 us (23%)
  between operations  14.4 us (8%)
  local copies, waits for them, and re-layouts  12 us (7%)
  other arithmetic  4.02 us (2%)
    all_to_all x3, waiting for transfers between devices, over_plane(): lax.all_to_all(blocks, 'fsdp', split_axis=0, concat_axis=0, axis_index_gr...  30.2 us
    ppermute x15, starting transfers between devices, send(): return lax.ppermute(value, AXES, STEP[move])  22 us
    all_to_all x3, starting transfers between devices, over_plane(): lax.all_to_all(blocks, 'fsdp', split_axis=0, concat_axis=0, axis_index_gr...  20.7 us
    ppermute x15, waiting for transfers between devices, send(): return lax.ppermute(value, AXES, STEP[move])  17.8 us
    pallas_call x2, Pallas kernels, normed_windows(): kernel_call(functools.partial(norm_kernel, extent), (jax.ShapeDtypeStruct...  13 us
    pallas_call x1, Pallas kernels, per_device(): kernel_call(conv_kernel, (jax.ShapeDtypeStruct((4, low_rows, half), F32),...  12.6 us
    pallas_call x1, Pallas kernels, per_device(): kernel_call(functools.partial(grad_conv_kernel, loss_scale), (jax.ShapeDt...  12.4 us
    pallas_call x1, Pallas kernels, per_device(): kernel_call(functools.partial(output_kernel, extent, loss_scale), (*(bloc...  8.1 us
  transfers between devices with their start and end apart: 19, of which 11 were waited for; matrix products, arithmetic and copies ran while one was open for 4% of the time, Pallas kernels for 33%

profile of v7, /device:TPU:1, one launch (start us, length us, event | category | flops | bytes accessed | tf_op | source)
XLA Modules:
  0.0 181.7 jit_solution(18126180637395532466)
XLA Ops:
  7.2 0.9 reshape.228
  9.1 2.2 %collective-permute-start.2 = (bf16[21,16,256]{2,1,0:T(8,128)(2,1)S(1)}, bf16[21,16,256]{2,1,0:T(8,128)(2,1)S(1)}, u32[]{:S(2)}, u32[]{:S(2)}) collective-permute-start(bf16[21,16,256]{2,1,0:T(8,128)(2,1)S(1)} %pad_maximum_fusion.1), channel_id=1, source_target_pairs={{0,4},{1,5},{2,6},{3,7},{4,0},{5,1},{6,2},{7,3},{8,12},{9,13},{10,... | collective-permute-start | bytes 516104 | tf_op jit(solution)/shard_map/ppermute | solution.py:43
  11.3 3.1 %shard_map.140 = (bf16[4,256,256]{2,1,0:T(8,128)(2,1)}, bf16[4,256,256]{2,1,0:T(8,128)(2,1)}, bf16[4,256,256]{2,1,0:T(8,128)(2,1)}, bf16[4,256,256]{2,1,0:T(8,128)(2,1)}) custom-call(s32[1]{0:T(128)} %bitcast.number, bf16[8,256,512]{2,1,0:T(8,128)(2,1)} %bitcast.72), custom_call_target="tpu_custom_call" | custom-call | bytes 4194304 | tf_op jit(solution)/shard_map/pallas_call | solution.py:474
  15.8 1.6 broadcast_in_dim.72
  17.4 8.0 %all-to-all-start = ((bf16[16,16,16,256]{3,2,1,0:T(8,128)(2,1)}), bf16[16,16,16,256]{3,2,1,0:T(8,128)(2,1)S(1)}, u32[]{:S(2)}, u32[]{:S(2)}) async-start(bf16[16,16,16,256]{3,2,1,0:T(8,128)(2,1)} %broadcast_in_dim.72), calls=%async_computation | async-start | bytes 4194304 | tf_op jit(solution)/shard_map/all_to_all | solution.py:62
  25.5 1.9 %collective-permute-start = (s32[4,2]{0,1:T(2,128)S(1)}, s32[4,2]{0,1:T(2,128)S(1)}, u32[]{:S(2)}, u32[]{:S(2)}) collective-permute-start(s32[4,2]{0,1:T(2,128)S(1)} %pad_add_fusion.2), channel_id=1, source_target_pairs={{0,32},{1,33},{2,34},{3,35},{4,36},{5,37},{6,38},{7,39},{8,40},{9,... | collective-permute-start | bytes 104 | tf_op jit(solution)/shard_map/ppermute | solution.py:43
  29.0 2.9 %collective-permute-start.4 = (bf16[4,256,256]{2,1,0:T(8,128)(2,1)}, bf16[4,256,256]{2,1,0:T(8,128)(2,1)}, u32[]{:S(2)}, u32[]{:S(2)}) collective-permute-start(bf16[4,256,256]{2,1,0:T(8,128)(2,1)} %get-tuple-element.49), channel_id=1, source_target_pairs={{0,64},{1,65},{2,66},{3,67},{4,68},{5,69},{6,70},{7,71},{8,72},{9,... | collective-permute-start | bytes 1572872 | tf_op jit(solution)/shard_map/ppermute | solution.py:43
  34.5 6.5 %shard_map.138 = (bf16[16,256,512]{2,1,0:T(8,128)(2,1)}, bf16[4,256,256]{2,1,0:T(8,128)(2,1)}) custom-call(s32[32]{0:T(128)} %concatenate.37.meta, bf16[4,256,512]{2,1,0:T(8,128)(2,1)} %bitcast.74, f32[1,512]{1,0:T(1,128)} %bitcast.82, f32[1,512]{1,0:T(1,128)} %bitcast.84), custom_call_target="tpu_custom_call" | custom-call | flops 20971520 | bytes 6291456 | tf_op jit(solution)/shard_map/pallas_call | solution.py:190
  41.0 6.5 %shard_map.139 = (bf16[16,256,512]{2,1,0:T(8,128)(2,1)}, bf16[4,256,256]{2,1,0:T(8,128)(2,1)}) custom-call(s32[32]{0:T(128)} %concatenate.39.meta, bf16[4,256,512]{2,1,0:T(8,128)(2,1)} %bitcast.18.image, f32[1,512]{1,0:T(1,128)} %bitcast.83, f32[1,512]{1,0:T(1,128)} %bitcast.85), custom_call_target="tpu_custom_call" | custom-call | flops 20971520 | bytes 6291456 | tf_op jit(solution)/shard_map/pallas_call | solution.py:190
  48.3 7.4 %collective-permute-done.5.cot3 = bf16[4,256,256]{2,1,0:T(8,128)(2,1)} collective-permute-done((bf16[4,256,256]{2,1,0:T(8,128)(2,1)}, bf16[4,256,256]{2,1,0:T(8,128)(2,1)}, u32[]{:S(2)}, u32[]{:S(2)}) %collective-permute-start.5) | collective-permute-done | bytes 524320 | tf_op jit(solution)/shard_map/ppermute | solution.py:43
  55.8 3.6 %shard_map.141.folded = bf16[4,512,256]{2,1,0:T(8,128)(2,1)} custom-call(s32[32]{0:T(128)} %concatenate.35.meta, bf16[4,256,256]{2,1,0:T(8,128)(2,1)} %get-tuple-element.47.cot0, bf16[4,256,256]{2,1,0:T(8,128)(2,1)} %collective-permute-done.3.cot1, bf16[4,256,256]{2,1,0:T(8,128)(2,1)} %collective-permute-done.4.cot2, ...), custom_call_target="tpu_custom_call" | custom-call | bytes 3145728 | tf_op jit(solution)/shard_map/pallas_call | solution.py:529
  59.4 1.3 copy-done.1
  60.7 4.2 %shard_map.142.own = f32[512,512]{1,0:T(8,128)} custom-call(bf16[4,512,256]{2,1,0:T(8,128)(2,1)} %shard_map.141.folded, bf16[16,16,16,256]{3,2,1,0:T(8,128)(2,1)} %copy-done.1), custom_call_target="tpu_custom_call" | custom-call | flops 536870912 | bytes 3145728 | tf_op jit(solution)/shard_map/pallas_call | solution.py:542
  65.0 2.8 %collective-permute-done.6.got = f32[512,512]{1,0:T(8,128)S(1)} collective-permute-done((f32[512,512]{1,0:T(8,128)}, f32[512,512]{1,0:T(8,128)S(1)}, u32[]{:S(2)}, u32[]{:S(2)}) %collective-permute-start.6) | collective-permute-done | bytes 1048608 | tf_op jit(solution)/shard_map/ppermute | solution.py:43
  67.8 1.0 copy-done.11
  68.8 12.4 %shard_map.143 = (bf16[512,512]{1,0:T(8,128)(2,1)}, bf16[16,18,16,256]{3,2,1,0:T(8,128)(2,1)}) custom-call(f32[512,128]{1,0:T(8,128)} %broadcast_in_dim.69.mask, f32[512,512]{1,0:T(8,128)} %shard_map.142.own, f32[512,512]{1,0:T(8,128)} %copy-done.11, bf16[4,512,256]{2,1,0:T(8,128)(2,1)} %shard_map.141.folded, bf16[16,16,16,256]{3,2,1,0:T(8,128)(2,1)} %copy-done.1, ...), custom_call_target="tpu_custom_call" | custom-call | flops 5368709120 | bytes 15728640 | tf_op jit(solution)/shard_map/pallas_call | solution.py:557
  81.2 6.9 %all-to-all-start.1 = ((bf16[16,18,16,256]{3,2,1,0:T(8,128)(2,1)}), bf16[16,18,16,256]{3,2,1,0:T(8,128)(2,1)S(1)}, u32[]{:S(2)}, u32[]{:S(2)}) async-start(bf16[16,18,16,256]{3,2,1,0:T(8,128)(2,1)} %get-tuple-element.54), calls=%async_computation.1 | async-start | bytes 4718592 | tf_op jit(solution)/shard_map/all_to_all | solution.py:62
  88.2 12.6 %shard_map.144 = (f32[4,512,256]{2,1,0:T(8,128)}, bf16[4,512,256]{2,1,0:T(8,128)(2,1)}, f32[512,512]{1,0:T(8,128)}) custom-call(f32[512,128]{1,0:T(8,128)} %broadcast_in_dim.69.mask, bf16[16,18,16,256]{3,2,1,0:T(8,128)(2,1)} %bitcast.92, bf16[16,16,16,256]{3,2,1,0:T(8,128)(2,1)} %copy-done.1, bf16[16,256,512]{2,1,0:T(8,128)(2,1)} %get-tuple-element.56.windows_own, ...), custom_call_target="tpu_custom_call" | custom-call | flops 5368709120 | bytes 18874368 | tf_op jit(solution)/shard_map/pallas_call | solution.py:572
  101.2 2.5 %collective-permute-done.7.got = f32[512,512]{1,0:T(8,128)S(1)} collective-permute-done((f32[512,512]{1,0:T(8,128)}, f32[512,512]{1,0:T(8,128)S(1)}, u32[]{:S(2)}, u32[]{:S(2)}) %collective-permute-start.7) | collective-permute-done | bytes 1048608 | tf_op jit(solution)/shard_map/ppermute | solution.py:43
  103.7 1.0 copy-done.2
  104.7 8.1 %shard_map.145 = (bf16[4,256,256]{2,1,0:T(8,128)(2,1)}, bf16[4,256,256]{2,1,0:T(8,128)(2,1)}, bf16[4,256,256]{2,1,0:T(8,128)(2,1)}, bf16[4,256,256]{2,1,0:T(8,128)(2,1)}, bf16[16,16,16,256]{3,2,1,0:T(8,128)(2,1)}) custom-call(s32[32]{0:T(128)} %concatenate.35.meta, f32[512,128]{1,0:T(8,128)} %broadcast_in_dim.69.mask, f32[512,512]{1,0:T(8,128)} %get-tuple-element.60.own, ...), custom_call_target="tpu_custom_call" | custom-call | flops 1610612736 | bytes 14680064 | tf_op jit(solution)/shard_map/pallas_call | solution.py:587
  112.8 8.8 %all-to-all-done.1 = bf16[16,18,16,256]{3,2,1,0:T(8,128)(2,1)S(1)} async-done(((bf16[16,18,16,256]{3,2,1,0:T(8,128)(2,1)}), bf16[16,18,16,256]{3,2,1,0:T(8,128)(2,1)S(1)}, u32[]{:S(2)}, u32[]{:S(2)}) %all-to-all-start.1) | async-done | bytes 2359328 | tf_op jit(solution)/shard_map/all_to_all | solution.py:62
  121.6 5.8 %all-to-all-start.2 = ((bf16[16,16,16,256]{3,2,1,0:T(8,128)(2,1)}), bf16[16,16,16,256]{3,2,1,0:T(8,128)(2,1)}, u32[]{:S(2)}, u32[]{:S(2)}) async-start(bf16[16,16,16,256]{3,2,1,0:T(8,128)(2,1)} %get-tuple-element.64), calls=%async_computation.2 | async-start | bytes 4194304 | tf_op jit(solution)/shard_map/all_to_all | solution.py:62
  127.7 4.4 %collective-permute-start.10 = (bf16[4,256,256]{2,1,0:T(8,128)(2,1)}, bf16[4,256,256]{2,1,0:T(8,128)(2,1)S(1)}, u32[]{:S(2)}, u32[]{:S(2)}) collective-permute-start(bf16[4,256,256]{2,1,0:T(8,128)(2,1)} %get-tuple-element.68), channel_id=1, source_target_pairs={{0,96},{1,97},{2,98},{3,99},{4,100},{5,101},{6,102},{7,103},{8,104... | collective-permute-start | bytes 1572872 | tf_op jit(solution)/shard_map/ppermute | solution.py:43
  132.3 21.4 %all-to-all-done.2 = bf16[16,16,16,256]{3,2,1,0:T(8,128)(2,1)} async-done(((bf16[16,16,16,256]{3,2,1,0:T(8,128)(2,1)}), bf16[16,16,16,256]{3,2,1,0:T(8,128)(2,1)}, u32[]{:S(2)}, u32[]{:S(2)}) %all-to-all-start.2) | async-done | bytes 2097184 | tf_op jit(solution)/shard_map/all_to_all | solution.py:62
  153.8 1.9 %convert_reduce_fusion.1 = f32[16,16,256]{2,1,0:T(8,128)S(1)} fusion(bf16[16,16,16,256]{3,2,1,0:T(8,128)(2,1)} %all-to-all-done.2), kind=kLoop, calls=%fused_computation.1 | loop fusion | flops 2031616 | bytes 2359296 | tf_op jit(solution)/shard_map/reduce_sum | solution.py:609
  156.1 1.1 collective-permute-start.11
  157.2 2.6 %collective-permute-start.12 = (bf16[21,16,256]{2,1,0:T(8,128)(2,1)S(1)}, bf16[21,16,256]{2,1,0:T(8,128)(2,1)S(1)}, u32[]{:S(2)}, u32[]{:S(2)}) collective-permute-start(bf16[21,16,256]{2,1,0:T(8,128)(2,1)S(1)} %get-tuple-element.78), channel_id=1, source_target_pairs={{0,64},{1,65},{2,66},{3,67},{4,68},{5,69},{6,70},{7,71},{8,72},{9,... | collective-permute-start | bytes 516104 | tf_op jit(solution)/shard_map/ppermute | solution.py:43
  160.0 3.6 %shard_map.146 = f32[8,256,512]{2,1,0:T(8,128)} custom-call(s32[1]{0:T(128)} %bitcast.number, bf16[4,256,256]{2,1,0:T(8,128)(2,1)} %get-tuple-element.69.back0, bf16[4,256,256]{2,1,0:T(8,128)(2,1)} %copy-done.5, bf16[4,256,256]{2,1,0:T(8,128)(2,1)} %copy-done.6, bf16[4,256,256]{2,1,0:T(8,128)(2,1)} %copy-done.4), custom_call_target="tpu_custom_call" | custom-call | bytes 6291456 | tf_op jit(solution)/shard_map/pallas_call | solution.py:626
  164.5 1.7 collective-permute-done.13
  166.3 4.9 %collective-permute-start.14 = (f32[21,16,256]{2,1,0:T(8,128)S(1)}, f32[21,16,256]{2,1,0:T(8,128)S(1)}, u32[]{:S(2)}, u32[]{:S(2)}) collective-permute-start(f32[21,16,256]{2,1,0:T(8,128)S(1)} %fusion.1), channel_id=1, source_target_pairs={{0,32},{1,33},{2,34},{3,35},{4,36},{5,37},{6,38},{7,39},{8,40},{9,... | collective-permute-start | bytes 1032200 | tf_op jit(solution)/shard_map/ppermute | solution.py:43
  171.2 1.3 collective-permute-done.14
  (93 shorter events, 12.5 us)
Async XLA Ops:
  7.2 1.0 copy-start
  7.2 81.0 %all-gather.3.cloned.1.call-start = ((), (), s32[]{:S(2)}) async-start(), calls=%async_computation.3 | async-start | bytes 2506752 | tf_op jit(solution)/shard_map/all_gather | solution.py:490
  9.1 5.9 %collective-permute-start.2 = (bf16[21,16,256]{2,1,0:T(8,128)(2,1)S(1)}, bf16[21,16,256]{2,1,0:T(8,128)(2,1)S(1)}, u32[]{:S(2)}, u32[]{:S(2)}) collective-permute-start(bf16[21,16,256]{2,1,0:T(8,128)(2,1)S(1)} %pad_maximum_fusion.1), channel_id=1, source_target_pairs={{0,4},{1,5},{2,6},{3,7},{4,0},{5,1},{6,2},{7,3},{8,12},{9,13},{10,... | collective-permute-start | bytes 516104 | tf_op jit(solution)/shard_map/ppermute | solution.py:43
  17.4 8.0 %copy-start.7 = (s32[4,1]{0,1:T(1,128)S(1)}, s32[4,1]{0,1:T(1,128)}, u32[]{:S(2)}) copy-start(s32[4,1]{0,1:T(1,128)} %param.12) | copy-start | bytes 52
  17.4 8.0 %copy-start.8 = (s32[4]{0:T(128)S(1)}, s32[4]{0:T(128)}, u32[]{:S(2)}) copy-start(s32[4]{0:T(128)} %param.13) | copy-start | bytes 52
  17.4 10.0 %copy-start.3 = (bf16[4,16,16,512]{3,2,1,0:T(8,128)(2,1)S(1)}, bf16[4,16,16,512]{3,2,1,0:T(8,128)(2,1)}, u32[]{:S(2)}) copy-start(bf16[4,16,16,512]{3,2,1,0:T(8,128)(2,1)} %param.11) | copy-start | bytes 3145732
  17.4 10.8 %copy-start.9 = (s32[8]{0:T(128)S(1)}, s32[8]{0:T(128)}, u32[]{:S(2)}) copy-start(s32[8]{0:T(128)} %param.14) | copy-start | bytes 100
  17.4 10.8 %copy-start.10 = (s32[8]{0:T(128)S(1)}, s32[8]{0:T(128)}, u32[]{:S(2)}) copy-start(s32[8]{0:T(128)} %param.15) | copy-start | bytes 100
  17.4 41.9 %all-to-all-start = ((bf16[16,16,16,256]{3,2,1,0:T(8,128)(2,1)}), bf16[16,16,16,256]{3,2,1,0:T(8,128)(2,1)S(1)}, u32[]{:S(2)}, u32[]{:S(2)}) async-start(bf16[16,16,16,256]{3,2,1,0:T(8,128)(2,1)} %broadcast_in_dim.72), calls=%async_computation | async-start | bytes 4194304 | tf_op jit(solution)/shard_map/all_to_all | solution.py:62
  25.5 2.7 %collective-permute-start = (s32[4,2]{0,1:T(2,128)S(1)}, s32[4,2]{0,1:T(2,128)S(1)}, u32[]{:S(2)}, u32[]{:S(2)}) collective-permute-start(s32[4,2]{0,1:T(2,128)S(1)} %pad_add_fusion.2), channel_id=1, source_target_pairs={{0,32},{1,33},{2,34},{3,35},{4,36},{5,37},{6,38},{7,39},{8,40},{9,... | collective-permute-start | bytes 104 | tf_op jit(solution)/shard_map/ppermute | solution.py:43
  27.4 13.6 %collective-permute-start.1 = (bf16[4,16,16,512]{3,2,1,0:T(8,128)(2,1)S(1)}, bf16[4,16,16,512]{3,2,1,0:T(8,128)(2,1)}, u32[]{:S(2)}, u32[]{:S(2)}) collective-permute-start(bf16[4,16,16,512]{3,2,1,0:T(8,128)(2,1)S(1)} %copy-done.3), channel_id=1, source_target_pairs={{0,32},{1,33},{2,34},{3,35},{4,36},{5,37},{6,38},{7,39},{8,40},{9,... | collective-permute-start | bytes 3145736 | tf_op jit(solution)/shard_map/ppermute | solution.py:43
  28.7 19.6 %collective-permute-start.3 = (bf16[4,256,256]{2,1,0:T(8,128)(2,1)}, bf16[4,256,256]{2,1,0:T(8,128)(2,1)}, u32[]{:S(2)}, u32[]{:S(2)}) collective-permute-start(bf16[4,256,256]{2,1,0:T(8,128)(2,1)} %get-tuple-element.48), channel_id=1, source_target_pairs={{0,32},{1,33},{2,34},{3,35},{4,36},{5,37},{6,38},{7,39},{8,40},{9,... | collective-permute-start | bytes 1572872 | tf_op jit(solution)/shard_map/ppermute | solution.py:43
  29.0 19.3 %collective-permute-start.4 = (bf16[4,256,256]{2,1,0:T(8,128)(2,1)}, bf16[4,256,256]{2,1,0:T(8,128)(2,1)}, u32[]{:S(2)}, u32[]{:S(2)}) collective-permute-start(bf16[4,256,256]{2,1,0:T(8,128)(2,1)} %get-tuple-element.49), channel_id=1, source_target_pairs={{0,64},{1,65},{2,66},{3,67},{4,68},{5,69},{6,70},{7,71},{8,72},{9,... | collective-permute-start | bytes 1572872 | tf_op jit(solution)/shard_map/ppermute | solution.py:43
  32.0 23.8 %collective-permute-start.5 = (bf16[4,256,256]{2,1,0:T(8,128)(2,1)}, bf16[4,256,256]{2,1,0:T(8,128)(2,1)}, u32[]{:S(2)}, u32[]{:S(2)}) collective-permute-start(bf16[4,256,256]{2,1,0:T(8,128)(2,1)} %get-tuple-element.50), channel_id=1, source_target_pairs={{0,96},{1,97},{2,98},{3,99},{4,100},{5,101},{6,102},{7,103},{8,104... | collective-permute-start | bytes 1572872 | tf_op jit(solution)/shard_map/ppermute | solution.py:43
  59.3 1.3 copy-start.1
  64.8 3.0 %collective-permute-start.6 = (f32[512,512]{1,0:T(8,128)}, f32[512,512]{1,0:T(8,128)S(1)}, u32[]{:S(2)}, u32[]{:S(2)}) collective-permute-start(f32[512,512]{1,0:T(8,128)} %shard_map.142.own), channel_id=1, source_target_pairs={{0,32},{1,33},{2,34},{3,35},{4,36},{5,37},{6,38},{7,39},{8,40},{9,... | collective-permute-start | bytes 3145736 | tf_op jit(solution)/shard_map/ppermute | solution.py:43
  67.8 1.0 copy-start.11
  81.2 40.4 %all-to-all-start.1 = ((bf16[16,18,16,256]{3,2,1,0:T(8,128)(2,1)}), bf16[16,18,16,256]{3,2,1,0:T(8,128)(2,1)S(1)}, u32[]{:S(2)}, u32[]{:S(2)}) async-start(bf16[16,18,16,256]{3,2,1,0:T(8,128)(2,1)} %get-tuple-element.54), calls=%async_computation.1 | async-start | bytes 4718592 | tf_op jit(solution)/shard_map/all_to_all | solution.py:62
  100.7 3.0 %collective-permute-start.7 = (f32[512,512]{1,0:T(8,128)}, f32[512,512]{1,0:T(8,128)S(1)}, u32[]{:S(2)}, u32[]{:S(2)}) collective-permute-start(f32[512,512]{1,0:T(8,128)} %get-tuple-element.60.own), channel_id=1, source_target_pairs={{0,32},{1,33},{2,34},{3,35},{4,36},{5,37},{6,38},{7,39},{8,40},{9,... | collective-permute-start | bytes 3145736 | tf_op jit(solution)/shard_map/ppermute | solution.py:43
  103.7 1.0 copy-start.2
  121.6 32.2 %all-to-all-start.2 = ((bf16[16,16,16,256]{3,2,1,0:T(8,128)(2,1)}), bf16[16,16,16,256]{3,2,1,0:T(8,128)(2,1)}, u32[]{:S(2)}, u32[]{:S(2)}) async-start(bf16[16,16,16,256]{3,2,1,0:T(8,128)(2,1)} %get-tuple-element.64), calls=%async_computation.2 | async-start | bytes 4194304 | tf_op jit(solution)/shard_map/all_to_all | solution.py:62
  127.7 28.1 %collective-permute-start.10 = (bf16[4,256,256]{2,1,0:T(8,128)(2,1)}, bf16[4,256,256]{2,1,0:T(8,128)(2,1)S(1)}, u32[]{:S(2)}, u32[]{:S(2)}) collective-permute-start(bf16[4,256,256]{2,1,0:T(8,128)(2,1)} %get-tuple-element.68), channel_id=1, source_target_pairs={{0,96},{1,97},{2,98},{3,99},{4,100},{5,101},{6,102},{7,103},{8,104... | collective-permute-start | bytes 1572872 | tf_op jit(solution)/shard_map/ppermute | solution.py:43
  132.1 23.7 %collective-permute-start.8 = (bf16[4,256,256]{2,1,0:T(8,128)(2,1)}, bf16[4,256,256]{2,1,0:T(8,128)(2,1)S(1)}, u32[]{:S(2)}, u32[]{:S(2)}) collective-permute-start(bf16[4,256,256]{2,1,0:T(8,128)(2,1)} %get-tuple-element.66), channel_id=1, source_target_pairs={{0,32},{1,33},{2,34},{3,35},{4,36},{5,37},{6,38},{7,39},{8,40},{9,... | collective-permute-start | bytes 1572872 | tf_op jit(solution)/shard_map/ppermute | solution.py:43
  132.1 23.9 %collective-permute-start.9 = (bf16[4,256,256]{2,1,0:T(8,128)(2,1)}, bf16[4,256,256]{2,1,0:T(8,128)(2,1)S(1)}, u32[]{:S(2)}, u32[]{:S(2)}) collective-permute-start(bf16[4,256,256]{2,1,0:T(8,128)(2,1)} %get-tuple-element.67), channel_id=1, source_target_pairs={{0,64},{1,65},{2,66},{3,67},{4,68},{5,69},{6,70},{7,71},{8,72},{9,... | collective-permute-start | bytes 1572872 | tf_op jit(solution)/shard_map/ppermute | solution.py:43
  155.8 4.2 %copy-start.4 = (bf16[4,256,256]{2,1,0:T(8,128)(2,1)}, bf16[4,256,256]{2,1,0:T(8,128)(2,1)S(1)}, u32[]{:S(2)}) copy-start(bf16[4,256,256]{2,1,0:T(8,128)(2,1)S(1)} %collective-permute-done.10.back3) | copy-start | bytes 1572868
  155.8 4.2 %copy-start.5 = (bf16[4,256,256]{2,1,0:T(8,128)(2,1)}, bf16[4,256,256]{2,1,0:T(8,128)(2,1)S(1)}, u32[]{:S(2)}) copy-start(bf16[4,256,256]{2,1,0:T(8,128)(2,1)S(1)} %collective-permute-done.8.back1) | copy-start | bytes 1572868
  156.0 4.0 %copy-start.6 = (bf16[4,256,256]{2,1,0:T(8,128)(2,1)}, bf16[4,256,256]{2,1,0:T(8,128)(2,1)S(1)}, u32[]{:S(2)}) copy-start(bf16[4,256,256]{2,1,0:T(8,128)(2,1)S(1)} %collective-permute-done.9.back2) | copy-start | bytes 1572868
  156.1 7.6 %collective-permute-start.11 = (bf16[21,16,256]{2,1,0:T(8,128)(2,1)S(1)}, bf16[21,16,256]{2,1,0:T(8,128)(2,1)S(1)}, u32[]{:S(2)}, u32[]{:S(2)}) collective-permute-start(bf16[21,16,256]{2,1,0:T(8,128)(2,1)S(1)} %get-tuple-element.79), channel_id=1, source_target_pairs={{0,4},{1,5},{2,6},{3,7},{4,0},{5,1},{6,2},{7,3},{8,12},{9,13},{10,... | collective-permute-start | bytes 516104 | tf_op jit(solution)/shard_map/ppermute | solution.py:43
  157.2 7.3 %collective-permute-start.12 = (bf16[21,16,256]{2,1,0:T(8,128)(2,1)S(1)}, bf16[21,16,256]{2,1,0:T(8,128)(2,1)S(1)}, u32[]{:S(2)}, u32[]{:S(2)}) collective-permute-start(bf16[21,16,256]{2,1,0:T(8,128)(2,1)S(1)} %get-tuple-element.78), channel_id=1, source_target_pairs={{0,64},{1,65},{2,66},{3,67},{4,68},{5,69},{6,70},{7,71},{8,72},{9,... | collective-permute-start | bytes 516104 | tf_op jit(solution)/shard_map/ppermute | solution.py:43
  159.7 6.5 %collective-permute-start.13 = (bf16[21,16,256]{2,1,0:T(8,128)(2,1)S(1)}, bf16[21,16,256]{2,1,0:T(8,128)(2,1)S(1)}, u32[]{:S(2)}, u32[]{:S(2)}) collective-permute-start(bf16[21,16,256]{2,1,0:T(8,128)(2,1)S(1)} %get-tuple-element.79), channel_id=1, source_target_pairs={{0,68},{1,69},{2,70},{3,71},{4,64},{5,65},{6,66},{7,67},{8,76},{9,... | collective-permute-start | bytes 516104 | tf_op jit(solution)/shard_map/ppermute | solution.py:43
  166.3 6.2 %collective-permute-start.14 = (f32[21,16,256]{2,1,0:T(8,128)S(1)}, f32[21,16,256]{2,1,0:T(8,128)S(1)}, u32[]{:S(2)}, u32[]{:S(2)}) collective-permute-start(f32[21,16,256]{2,1,0:T(8,128)S(1)} %fusion.1), channel_id=1, source_target_pairs={{0,32},{1,33},{2,34},{3,35},{4,36},{5,37},{6,38},{7,39},{8,40},{9,... | collective-permute-start | bytes 1032200 | tf_op jit(solution)/shard_map/ppermute | solution.py:43
Sparse Core Ops, SparseCore 0:
  15.9 62.0 all-gather.2

commit v8 on v1

--- a/solution.py
+++ b/solution.py
@@ -34,6 +34,8 @@
     "h": moved(lambda h, c, z, y, x: (1 - h, c, z, y, x)),
     "hc": moved(lambda h, c, z, y, x: (1 - h, 1 - c, z, y, x)),
 }
+BY_BITS = [(r >> 3 & 1) * 8 + (r >> 1 & 1) * 4 + (r >> 2 & 1) * 2 + (r & 1) for r in range(16)]
+DIAGONAL = [r % 4 * 4 + (r // 4 + r) % 4 for r in range(16)]
 PLANES = [[z * 8 + y * 4 + x for z in range(4) for x in range(4)] for y in range(2)]
 
 
@@ -55,9 +57,10 @@
     return total, send(total, "c")
 
 
-def over_plane(blocks):
+def over_plane(blocks, order=tuple(range(16))):
+    groups = [[plane[place] for place in order] for plane in PLANES]
     return lax.all_to_all(
-        blocks, "fsdp", split_axis=0, concat_axis=0, axis_index_groups=PLANES, tiled=True
+        blocks, "fsdp", split_axis=0, concat_axis=0, axis_index_groups=groups, tiled=True
     )
 
 
@@ -215,7 +218,7 @@
     for f in range(32):
         z, y, x = f // 8, f // 4 % 2, f % 4
         for k in range(4):
-            up[k, f * rows : (f + 1) * rows, :] = pieces[z * 4 + x, y * 4 + k]
+            up[k, f * rows : (f + 1) * rows, :] = pieces[BY_BITS.index(z * 4 + x), y * 4 + k]
 
 
 def gather_down(pieces, down):
@@ -226,7 +229,7 @@
                 side, step = unit // 4, unit % 4
                 first = (x * 4 + step) * rows
                 down[z, first : first + rows, side * half : (side + 1) * half] = pieces[
-                    z * 4 + x, 8 + unit
+                    BY_BITS.index(z * 4 + x), 8 + unit
                 ]
 
 
@@ -300,7 +303,7 @@
         total = total.T.astype(BF)
         for f in range(32):
             z, y, x = f // 8, f // 4 % 2, f % 4
-            grads[z * 4 + x, y * 9 + t] = total[f * rows : (f + 1) * rows, :]
+            grads[BY_BITS.index(z * 4 + x), y * 9 + t] = total[f * rows : (f + 1) * rows, :]
 
 
 def conv_kernel(
@@ -401,13 +404,13 @@
         grad = dot(turned, scaled, 1, 0).astype(BF)
         for f in range(32):
             z, y, x = f // 8, f // 4 % 2, f % 4
-            grads[z * 4 + x, y * 4 + k] = grad[f * rows : (f + 1) * rows, :]
+            grads[DIAGONAL.index(z * 4 + x), y * 4 + k] = grad[f * rows : (f + 1) * rows, :]
         grad = dot(skip[k].astype(F32).T.astype(BF), glow[...], 1, 0).astype(BF)
         for x in range(4):
             for unit in range(8):
                 side_of, step = unit // 4, unit % 4
                 first = (x * 4 + step) * rows
-                grads[k * 4 + x, 8 + unit] = grad[
+                grads[DIAGONAL.index(k * 4 + x), 8 + unit] = grad[
                     first : first + rows, side_of * half : (side_of + 1) * half
                 ]
 
@@ -479,7 +482,7 @@
     down_kept = jnp.where(core == 0, first[4:12], second[4:12])
     up_down = jnp.concatenate([first[:4], second[:4], down_kept])
     conv_two = jnp.concatenate([first[12:], second[12:]])
-    up_down = over_plane(jnp.broadcast_to(up_down, (16, *up_down.shape)))
+    up_down = over_plane(jnp.broadcast_to(up_down, (16, *up_down.shape)), BY_BITS)
     conv_two = lax.all_gather(conv_two, "fsdp", axis_index_groups=PLANES)
 
     images_pair = send(images, "c")
@@ -516,7 +519,9 @@
     windows_own, residual_own = normed_windows(own_meta, images, norm_gain, norm_shift)
     windows_pair, residual_pair = normed_windows(pair_meta, images_pair, norm_gain, norm_shift)
 
-    ready, windows_own, windows_pair = lax.optimization_barrier((meta, windows_own, windows_pair))
+    ready, mask, windows_own, windows_pair = lax.optimization_barrier(
+        (meta, mask, windows_own, windows_pair)
+    )
     folded, glow_part = kernel_call(
         functools.partial(glow_kernel, extent, loss_scale),
         (
@@ -548,7 +553,7 @@
         in_specs=[WHOLE] * 7,
         out_specs=(WHOLE, WHOLE),
     )(mask, glow_part, glow_got, folded, up_down, windows_own, windows_pair)
-    conv_grads = over_plane(conv_grads)
+    conv_grads = over_plane(conv_grads, BY_BITS)
     glow, windows_own, windows_pair = lax.optimization_barrier((glow, windows_own, windows_pair))
 
     wide, skip, low_part = kernel_call(
@@ -585,23 +590,24 @@
         out_specs=(WHOLE,) * 5,
     )(meta, mask, low_part, low_got, wide, skip, glow, folded, up_down)
     returned = over_dp(returning)
-    grads = over_plane(grads)
+    grads = over_plane(grads, DIAGONAL)
 
     conv_sum = jnp.sum(conv_grads.astype(F32), axis=0).reshape(2, 9, rows, half)
-    conv_sum, returned = lax.optimization_barrier((conv_sum, returned))
-
-    def by_core(own, pair):
-        return jnp.where(core == 0, jnp.stack([own, pair]), jnp.stack([pair, own]))
-
-    out_conv = by_core(*over_column(conv_sum, y)).transpose(2, 1, 0, 3)
-    out_conv = out_conv.reshape(rows, 9, channels)
     grads_sum = jnp.sum(grads.astype(F32), axis=0)
     up_sum, down_sum = grads_sum[:8].reshape(2, 4, rows, half), grads_sum[8:]
-    shares = jnp.concatenate([up_sum, jnp.broadcast_to(down_sum, (2, *down_sum.shape))], axis=1)
-    shares, out_conv = lax.optimization_barrier((shares, out_conv))
+    down_sum = jnp.broadcast_to(down_sum, (2, *down_sum.shape))
+    shares = jnp.concatenate([conv_sum, up_sum, down_sum], axis=1)
+    shares, returned = lax.optimization_barrier((shares, returned))
     own, pair = over_column(shares, y)
-    out_up = by_core(own[:4], pair[:4]).transpose(2, 1, 0, 3).reshape(rows, 4 * channels)
-    out_down = jnp.where(y == core, own[4:], pair[4:])
+
+    def by_core(first, last):
+        parts = (own[first:last], pair[first:last])
+        both = jnp.where(core == 0, jnp.stack(parts), jnp.stack(parts[::-1]))
+        return both.transpose(2, 1, 0, 3)
+
+    out_conv = by_core(0, 9).reshape(rows, 9, channels)
+    out_up = by_core(9, 13).reshape(rows, 4 * channels)
+    out_down = jnp.where(y == core, own[13:], pair[13:])
     out_down = out_down.reshape(2, 4 * rows, half).transpose(1, 0, 2).reshape(4 * rows, channels)
 
     block_out = kernel_call(

time: 189 us -> 180 us (0.952)
  waiting for transfers between devices: 56.4 us -> 47.5 us
    ppermute x19 -> x15, waiting for transfers between devices: 43.8 us -> 17.7 us  [send(): return lax.ppermute(value, AXES, STEP[move])]
    all_to_all x3, waiting for transfers between devices: 12.6 us -> 29.8 us  [over_plane(): lax.all_to_all(blocks, 'fsdp', split_axis=0, concat_axis=0, axis_index_gr...]
    ppermute x19 -> x15, starting transfers between devices: 27.2 us -> 25.6 us  [send(): return lax.ppermute(value, AXES, STEP[move])]
  transfers between devices with their start and end apart: 23 -> 19, of which waited for: 14 -> 11; matrix products, arithmetic and copies ran while one was open for 4% -> 4% of each run, Pallas kernels for 31% -> 32%
where the time goes in v8:
time: 180 us; the launch traced here: 179 us
  Pallas kernels  58 us (32%)
  waiting for transfers between devices  47.5 us (26%)
  starting transfers between devices  43.2 us (24%)
  between operations  14.4 us (8%)
  local copies, waits for them, and re-layouts  12 us (7%)
  other arithmetic  4.03 us (2%)
    all_to_all x3, waiting for transfers between devices, over_plane(): lax.all_to_all(blocks, 'fsdp', split_axis=0, concat_axis=0, axis_index_gr...  29.8 us
    ppermute x15, starting transfers between devices, send(): return lax.ppermute(value, AXES, STEP[move])  25.6 us
    ppermute x15, waiting for transfers between devices, send(): return lax.ppermute(value, AXES, STEP[move])  17.7 us
    all_to_all x3, starting transfers between devices, over_plane(): lax.all_to_all(blocks, 'fsdp', split_axis=0, concat_axis=0, axis_index_gr...  17.6 us
    pallas_call x2, Pallas kernels, normed_windows(): kernel_call(functools.partial(norm_kernel, extent), (jax.ShapeDtypeStruct...  13 us
    pallas_call x1, Pallas kernels, per_device(): kernel_call(conv_kernel, (jax.ShapeDtypeStruct((4, low_rows, half), F32),...  12.6 us
    pallas_call x1, Pallas kernels, per_device(): kernel_call(functools.partial(grad_conv_kernel, loss_scale), (jax.ShapeDt...  12.4 us
    pallas_call x1, Pallas kernels, per_device(): kernel_call(functools.partial(output_kernel, extent, loss_scale), (*(bloc...  8.12 us
  transfers between devices with their start and end apart: 19, of which 11 were waited for; matrix products, arithmetic and copies ran while one was open for 4% of the time, Pallas kernels for 32%

profile of v8, /device:TPU:1, one launch (start us, length us, event | category | flops | bytes accessed | tf_op | source)
XLA Modules:
  0.0 179.2 jit_solution(16318835806717305911)
XLA Ops:
  7.2 0.9 reshape.228
  9.1 2.2 %collective-permute-start.2 = (bf16[21,16,256]{2,1,0:T(8,128)(2,1)S(1)}, bf16[21,16,256]{2,1,0:T(8,128)(2,1)S(1)}, u32[]{:S(2)}, u32[]{:S(2)}) collective-permute-start(bf16[21,16,256]{2,1,0:T(8,128)(2,1)S(1)} %pad_maximum_fusion.1), channel_id=1, source_target_pairs={{0,4},{1,5},{2,6},{3,7},{4,0},{5,1},{6,2},{7,3},{8,12},{9,13},{10,... | collective-permute-start | bytes 516104 | tf_op jit(solution)/shard_map/ppermute | solution.py:43
  11.3 3.1 %shard_map.140 = (bf16[4,256,256]{2,1,0:T(8,128)(2,1)}, bf16[4,256,256]{2,1,0:T(8,128)(2,1)}, bf16[4,256,256]{2,1,0:T(8,128)(2,1)}, bf16[4,256,256]{2,1,0:T(8,128)(2,1)}) custom-call(s32[1]{0:T(128)} %bitcast.number, bf16[8,256,512]{2,1,0:T(8,128)(2,1)} %bitcast.72), custom_call_target="tpu_custom_call" | custom-call | bytes 4194304 | tf_op jit(solution)/shard_map/pallas_call | solution.py:470
  15.8 1.6 broadcast_in_dim.72
  17.4 8.0 %all-to-all-start = ((bf16[16,16,16,256]{3,2,1,0:T(8,128)(2,1)}), bf16[16,16,16,256]{3,2,1,0:T(8,128)(2,1)S(1)}, u32[]{:S(2)}, u32[]{:S(2)}) async-start(bf16[16,16,16,256]{3,2,1,0:T(8,128)(2,1)} %broadcast_in_dim.72), calls=%async_computation | async-start | bytes 4194304 | tf_op jit(solution)/shard_map/all_to_all | solution.py:62
  25.5 1.9 %collective-permute-start = (s32[4,2]{0,1:T(2,128)S(1)}, s32[4,2]{0,1:T(2,128)S(1)}, u32[]{:S(2)}, u32[]{:S(2)}) collective-permute-start(s32[4,2]{0,1:T(2,128)S(1)} %pad_add_fusion.2), channel_id=1, source_target_pairs={{0,32},{1,33},{2,34},{3,35},{4,36},{5,37},{6,38},{7,39},{8,40},{9,... | collective-permute-start | bytes 104 | tf_op jit(solution)/shard_map/ppermute | solution.py:43
  29.1 2.9 %collective-permute-start.4 = (bf16[4,256,256]{2,1,0:T(8,128)(2,1)}, bf16[4,256,256]{2,1,0:T(8,128)(2,1)}, u32[]{:S(2)}, u32[]{:S(2)}) collective-permute-start(bf16[4,256,256]{2,1,0:T(8,128)(2,1)} %get-tuple-element.51), channel_id=1, source_target_pairs={{0,64},{1,65},{2,66},{3,67},{4,68},{5,69},{6,70},{7,71},{8,72},{9,... | collective-permute-start | bytes 1572872 | tf_op jit(solution)/shard_map/ppermute | solution.py:43
  34.5 6.5 %shard_map.138 = (bf16[16,256,512]{2,1,0:T(8,128)(2,1)}, bf16[4,256,256]{2,1,0:T(8,128)(2,1)}) custom-call(s32[32]{0:T(128)} %concatenate.37.meta, bf16[4,256,512]{2,1,0:T(8,128)(2,1)} %bitcast.74, f32[1,512]{1,0:T(1,128)} %bitcast.82, f32[1,512]{1,0:T(1,128)} %bitcast.84), custom_call_target="tpu_custom_call" | custom-call | flops 20971520 | bytes 6291456 | tf_op jit(solution)/shard_map/pallas_call | solution.py:190
  41.0 6.6 %shard_map.139 = (bf16[16,256,512]{2,1,0:T(8,128)(2,1)}, bf16[4,256,256]{2,1,0:T(8,128)(2,1)}) custom-call(s32[32]{0:T(128)} %concatenate.39.meta, bf16[4,256,512]{2,1,0:T(8,128)(2,1)} %bitcast.18.image, f32[1,512]{1,0:T(1,128)} %bitcast.83, f32[1,512]{1,0:T(1,128)} %bitcast.85), custom_call_target="tpu_custom_call" | custom-call | flops 20971520 | bytes 6291456 | tf_op jit(solution)/shard_map/pallas_call | solution.py:190
  48.4 7.4 %collective-permute-done.5.cot3 = bf16[4,256,256]{2,1,0:T(8,128)(2,1)} collective-permute-done((bf16[4,256,256]{2,1,0:T(8,128)(2,1)}, bf16[4,256,256]{2,1,0:T(8,128)(2,1)}, u32[]{:S(2)}, u32[]{:S(2)}) %collective-permute-start.5) | collective-permute-done | bytes 524320 | tf_op jit(solution)/shard_map/ppermute | solution.py:43
  55.8 1.3 copy-done.1
  57.1 5.2 %shard_map.141 = (bf16[4,512,256]{2,1,0:T(8,128)(2,1)}, f32[512,512]{1,0:T(8,128)}) custom-call(s32[32]{0:T(128)} %concatenate.35.meta, bf16[4,256,256]{2,1,0:T(8,128)(2,1)} %get-tuple-element.49.cot0, bf16[4,256,256]{2,1,0:T(8,128)(2,1)} %collective-permute-done.3.cot1, bf16[4,256,256]{2,1,0:T(8,128)(2,1)} %collective-permute-done.4.cot2, ...), custom_call_target="tpu_custom_call" | custom-call | flops 536870912 | bytes 5242880 | tf_op jit(solution)/shard_map/pallas_call | solution.py:525
  62.3 3.8 %collective-permute-start.6 = (f32[512,512]{1,0:T(8,128)}, f32[512,512]{1,0:T(8,128)S(1)}, u32[]{:S(2)}, u32[]{:S(2)}) collective-permute-start(f32[512,512]{1,0:T(8,128)} %get-tuple-element.54.own), channel_id=1, source_target_pairs={{0,32},{1,33},{2,34},{3,35},{4,36},{5,37},{6,38},{7,39},{8,40},{9,... | collective-permute-start | bytes 3145736 | tf_op jit(solution)/shard_map/ppermute | solution.py:43
  66.1 2.5 %collective-permute-done.6.got = f32[512,512]{1,0:T(8,128)S(1)} collective-permute-done((f32[512,512]{1,0:T(8,128)}, f32[512,512]{1,0:T(8,128)S(1)}, u32[]{:S(2)}, u32[]{:S(2)}) %collective-permute-start.6) | collective-permute-done | bytes 1048608 | tf_op jit(solution)/shard_map/ppermute | solution.py:43
  68.6 1.0 copy-done.11
  69.6 12.4 %shard_map.142 = (bf16[512,512]{1,0:T(8,128)(2,1)}, bf16[16,18,16,256]{3,2,1,0:T(8,128)(2,1)}) custom-call(f32[512,128]{1,0:T(8,128)} %broadcast_in_dim.69.mask, f32[512,512]{1,0:T(8,128)} %get-tuple-element.54.own, f32[512,512]{1,0:T(8,128)} %copy-done.11, bf16[4,512,256]{2,1,0:T(8,128)(2,1)} %get-tuple-element.55.folded, ...), custom_call_target="tpu_custom_call" | custom-call | flops 5368709120 | bytes 15728640 | tf_op jit(solution)/shard_map/pallas_call | solution.py:544
  82.0 3.9 %all-to-all-start.1 = ((bf16[16,18,16,256]{3,2,1,0:T(8,128)(2,1)}), bf16[16,18,16,256]{3,2,1,0:T(8,128)(2,1)S(1)}, u32[]{:S(2)}, u32[]{:S(2)}) async-start(bf16[16,18,16,256]{3,2,1,0:T(8,128)(2,1)} %get-tuple-element.58), calls=%async_computation.1 | async-start | bytes 4718592 | tf_op jit(solution)/shard_map/all_to_all | solution.py:62
  86.0 12.6 %shard_map.143 = (f32[4,512,256]{2,1,0:T(8,128)}, bf16[4,512,256]{2,1,0:T(8,128)(2,1)}, f32[512,512]{1,0:T(8,128)}) custom-call(f32[512,128]{1,0:T(8,128)} %broadcast_in_dim.69.mask, bf16[16,18,16,256]{3,2,1,0:T(8,128)(2,1)} %bitcast.92, bf16[16,16,16,256]{3,2,1,0:T(8,128)(2,1)} %copy-done.1, bf16[16,256,512]{2,1,0:T(8,128)(2,1)} %get-tuple-element.60.windows_own, ...), custom_call_target="tpu_custom_call" | custom-call | flops 5368709120 | bytes 18874368 | tf_op jit(solution)/shard_map/pallas_call | solution.py:559
  98.9 2.5 %collective-permute-done.7.got = f32[512,512]{1,0:T(8,128)S(1)} collective-permute-done((f32[512,512]{1,0:T(8,128)}, f32[512,512]{1,0:T(8,128)S(1)}, u32[]{:S(2)}, u32[]{:S(2)}) %collective-permute-start.7) | collective-permute-done | bytes 1048608 | tf_op jit(solution)/shard_map/ppermute | solution.py:43
  101.4 1.0 copy-done.2
  102.4 8.1 %shard_map.144 = (bf16[4,256,256]{2,1,0:T(8,128)(2,1)}, bf16[4,256,256]{2,1,0:T(8,128)(2,1)}, bf16[4,256,256]{2,1,0:T(8,128)(2,1)}, bf16[4,256,256]{2,1,0:T(8,128)(2,1)}, bf16[16,16,16,256]{3,2,1,0:T(8,128)(2,1)}) custom-call(s32[32]{0:T(128)} %concatenate.35.meta, f32[512,128]{1,0:T(8,128)} %broadcast_in_dim.69.mask, f32[512,512]{1,0:T(8,128)} %get-tuple-element.64.own, ...), custom_call_target="tpu_custom_call" | custom-call | flops 1610612736 | bytes 14680064 | tf_op jit(solution)/shard_map/pallas_call | solution.py:574
  110.5 8.6 %all-to-all-done.1 = bf16[16,18,16,256]{3,2,1,0:T(8,128)(2,1)S(1)} async-done(((bf16[16,18,16,256]{3,2,1,0:T(8,128)(2,1)}), bf16[16,18,16,256]{3,2,1,0:T(8,128)(2,1)S(1)}, u32[]{:S(2)}, u32[]{:S(2)}) %all-to-all-start.1) | async-done | bytes 2359328 | tf_op jit(solution)/shard_map/all_to_all | solution.py:62
  119.1 5.7 %all-to-all-start.2 = ((bf16[16,16,16,256]{3,2,1,0:T(8,128)(2,1)}), bf16[16,16,16,256]{3,2,1,0:T(8,128)(2,1)}, u32[]{:S(2)}, u32[]{:S(2)}) async-start(bf16[16,16,16,256]{3,2,1,0:T(8,128)(2,1)} %get-tuple-element.68), calls=%async_computation.2 | async-start | bytes 4194304 | tf_op jit(solution)/shard_map/all_to_all | solution.py:62
  125.1 4.5 %collective-permute-start.10 = (bf16[4,256,256]{2,1,0:T(8,128)(2,1)}, bf16[4,256,256]{2,1,0:T(8,128)(2,1)S(1)}, u32[]{:S(2)}, u32[]{:S(2)}) collective-permute-start(bf16[4,256,256]{2,1,0:T(8,128)(2,1)} %get-tuple-element.72), channel_id=1, source_target_pairs={{0,96},{1,97},{2,98},{3,99},{4,100},{5,101},{6,102},{7,103},{8,104... | collective-permute-start | bytes 1572872 | tf_op jit(solution)/shard_map/ppermute | solution.py:43
  129.8 21.2 %all-to-all-done.2 = bf16[16,16,16,256]{3,2,1,0:T(8,128)(2,1)} async-done(((bf16[16,16,16,256]{3,2,1,0:T(8,128)(2,1)}), bf16[16,16,16,256]{3,2,1,0:T(8,128)(2,1)}, u32[]{:S(2)}, u32[]{:S(2)}) %all-to-all-start.2) | async-done | bytes 2097184 | tf_op jit(solution)/shard_map/all_to_all | solution.py:62
  151.0 1.9 %convert_reduce_fusion.1 = f32[16,16,256]{2,1,0:T(8,128)S(1)} fusion(bf16[16,16,16,256]{3,2,1,0:T(8,128)(2,1)} %all-to-all-done.2), kind=kLoop, calls=%fused_computation.1 | loop fusion | flops 2031616 | bytes 2359296 | tf_op jit(solution)/shard_map/reduce_sum | solution.py:596
  153.5 1.1 collective-permute-start.11
  154.5 2.6 %collective-permute-start.12 = (bf16[21,16,256]{2,1,0:T(8,128)(2,1)S(1)}, bf16[21,16,256]{2,1,0:T(8,128)(2,1)S(1)}, u32[]{:S(2)}, u32[]{:S(2)}) collective-permute-start(bf16[21,16,256]{2,1,0:T(8,128)(2,1)S(1)} %get-tuple-element.82), channel_id=1, source_target_pairs={{0,64},{1,65},{2,66},{3,67},{4,68},{5,69},{6,70},{7,71},{8,72},{9,... | collective-permute-start | bytes 516104 | tf_op jit(solution)/shard_map/ppermute | solution.py:43
  157.4 3.6 %shard_map.145 = f32[8,256,512]{2,1,0:T(8,128)} custom-call(s32[1]{0:T(128)} %bitcast.number, bf16[4,256,256]{2,1,0:T(8,128)(2,1)} %get-tuple-element.73.back0, bf16[4,256,256]{2,1,0:T(8,128)(2,1)} %copy-done.5, bf16[4,256,256]{2,1,0:T(8,128)(2,1)} %copy-done.6, bf16[4,256,256]{2,1,0:T(8,128)(2,1)} %copy-done.4), custom_call_target="tpu_custom_call" | custom-call | bytes 6291456 | tf_op jit(solution)/shard_map/pallas_call | solution.py:613
  161.9 1.7 collective-permute-done.13
  163.7 5.0 %collective-permute-start.14 = (f32[21,16,256]{2,1,0:T(8,128)S(1)}, f32[21,16,256]{2,1,0:T(8,128)S(1)}, u32[]{:S(2)}, u32[]{:S(2)}) collective-permute-start(f32[21,16,256]{2,1,0:T(8,128)S(1)} %fusion.1), channel_id=1, source_target_pairs={{0,32},{1,33},{2,34},{3,35},{4,36},{5,37},{6,38},{7,39},{8,40},{9,... | collective-permute-start | bytes 1032200 | tf_op jit(solution)/shard_map/ppermute | solution.py:43
  168.7 1.3 collective-permute-done.14
  (94 shorter events, 12.4 us)
Async XLA Ops:
  7.2 1.0 copy-start
  7.2 78.8 %all-gather.3.cloned.1.call-start = ((), (), s32[]{:S(2)}) async-start(), calls=%async_computation.3 | async-start | bytes 2506752 | tf_op jit(solution)/shard_map/all_gather | solution.py:486
  9.1 5.9 %collective-permute-start.2 = (bf16[21,16,256]{2,1,0:T(8,128)(2,1)S(1)}, bf16[21,16,256]{2,1,0:T(8,128)(2,1)S(1)}, u32[]{:S(2)}, u32[]{:S(2)}) collective-permute-start(bf16[21,16,256]{2,1,0:T(8,128)(2,1)S(1)} %pad_maximum_fusion.1), channel_id=1, source_target_pairs={{0,4},{1,5},{2,6},{3,7},{4,0},{5,1},{6,2},{7,3},{8,12},{9,13},{10,... | collective-permute-start | bytes 516104 | tf_op jit(solution)/shard_map/ppermute | solution.py:43
  17.4 8.0 %copy-start.7 = (s32[4,1]{0,1:T(1,128)S(1)}, s32[4,1]{0,1:T(1,128)}, u32[]{:S(2)}) copy-start(s32[4,1]{0,1:T(1,128)} %param.12) | copy-start | bytes 52
  17.4 8.0 %copy-start.8 = (s32[4]{0:T(128)S(1)}, s32[4]{0:T(128)}, u32[]{:S(2)}) copy-start(s32[4]{0:T(128)} %param.13) | copy-start | bytes 52
  17.4 10.0 %copy-start.3 = (bf16[4,16,16,512]{3,2,1,0:T(8,128)(2,1)S(1)}, bf16[4,16,16,512]{3,2,1,0:T(8,128)(2,1)}, u32[]{:S(2)}) copy-start(bf16[4,16,16,512]{3,2,1,0:T(8,128)(2,1)} %param.11) | copy-start | bytes 3145732
  17.4 10.8 %copy-start.9 = (s32[8]{0:T(128)S(1)}, s32[8]{0:T(128)}, u32[]{:S(2)}) copy-start(s32[8]{0:T(128)} %param.14) | copy-start | bytes 100
  17.4 10.8 %copy-start.10 = (s32[8]{0:T(128)S(1)}, s32[8]{0:T(128)}, u32[]{:S(2)}) copy-start(s32[8]{0:T(128)} %param.15) | copy-start | bytes 100
  17.4 38.3 %all-to-all-start = ((bf16[16,16,16,256]{3,2,1,0:T(8,128)(2,1)}), bf16[16,16,16,256]{3,2,1,0:T(8,128)(2,1)S(1)}, u32[]{:S(2)}, u32[]{:S(2)}) async-start(bf16[16,16,16,256]{3,2,1,0:T(8,128)(2,1)} %broadcast_in_dim.72), calls=%async_computation | async-start | bytes 4194304 | tf_op jit(solution)/shard_map/all_to_all | solution.py:62
  25.5 2.7 %collective-permute-start = (s32[4,2]{0,1:T(2,128)S(1)}, s32[4,2]{0,1:T(2,128)S(1)}, u32[]{:S(2)}, u32[]{:S(2)}) collective-permute-start(s32[4,2]{0,1:T(2,128)S(1)} %pad_add_fusion.2), channel_id=1, source_target_pairs={{0,32},{1,33},{2,34},{3,35},{4,36},{5,37},{6,38},{7,39},{8,40},{9,... | collective-permute-start | bytes 104 | tf_op jit(solution)/shard_map/ppermute | solution.py:43
  27.4 13.6 %collective-permute-start.1 = (bf16[4,16,16,512]{3,2,1,0:T(8,128)(2,1)S(1)}, bf16[4,16,16,512]{3,2,1,0:T(8,128)(2,1)}, u32[]{:S(2)}, u32[]{:S(2)}) collective-permute-start(bf16[4,16,16,512]{3,2,1,0:T(8,128)(2,1)S(1)} %copy-done.3), channel_id=1, source_target_pairs={{0,32},{1,33},{2,34},{3,35},{4,36},{5,37},{6,38},{7,39},{8,40},{9,... | collective-permute-start | bytes 3145736 | tf_op jit(solution)/shard_map/ppermute | solution.py:43
  28.7 19.7 %collective-permute-start.3 = (bf16[4,256,256]{2,1,0:T(8,128)(2,1)}, bf16[4,256,256]{2,1,0:T(8,128)(2,1)}, u32[]{:S(2)}, u32[]{:S(2)}) collective-permute-start(bf16[4,256,256]{2,1,0:T(8,128)(2,1)} %get-tuple-element.50), channel_id=1, source_target_pairs={{0,32},{1,33},{2,34},{3,35},{4,36},{5,37},{6,38},{7,39},{8,40},{9,... | collective-permute-start | bytes 1572872 | tf_op jit(solution)/shard_map/ppermute | solution.py:43
  29.1 19.3 %collective-permute-start.4 = (bf16[4,256,256]{2,1,0:T(8,128)(2,1)}, bf16[4,256,256]{2,1,0:T(8,128)(2,1)}, u32[]{:S(2)}, u32[]{:S(2)}) collective-permute-start(bf16[4,256,256]{2,1,0:T(8,128)(2,1)} %get-tuple-element.51), channel_id=1, source_target_pairs={{0,64},{1,65},{2,66},{3,67},{4,68},{5,69},{6,70},{7,71},{8,72},{9,... | collective-permute-start | bytes 1572872 | tf_op jit(solution)/shard_map/ppermute | solution.py:43
  32.0 23.8 %collective-permute-start.5 = (bf16[4,256,256]{2,1,0:T(8,128)(2,1)}, bf16[4,256,256]{2,1,0:T(8,128)(2,1)}, u32[]{:S(2)}, u32[]{:S(2)}) collective-permute-start(bf16[4,256,256]{2,1,0:T(8,128)(2,1)} %get-tuple-element.52), channel_id=1, source_target_pairs={{0,96},{1,97},{2,98},{3,99},{4,100},{5,101},{6,102},{7,103},{8,104... | collective-permute-start | bytes 1572872 | tf_op jit(solution)/shard_map/ppermute | solution.py:43
  55.8 1.3 copy-start.1
  62.3 6.3 %collective-permute-start.6 = (f32[512,512]{1,0:T(8,128)}, f32[512,512]{1,0:T(8,128)S(1)}, u32[]{:S(2)}, u32[]{:S(2)}) collective-permute-start(f32[512,512]{1,0:T(8,128)} %get-tuple-element.54.own), channel_id=1, source_target_pairs={{0,32},{1,33},{2,34},{3,35},{4,36},{5,37},{6,38},{7,39},{8,40},{9,... | collective-permute-start | bytes 3145736 | tf_op jit(solution)/shard_map/ppermute | solution.py:43
  68.6 1.0 copy-start.11
  82.0 37.1 %all-to-all-start.1 = ((bf16[16,18,16,256]{3,2,1,0:T(8,128)(2,1)}), bf16[16,18,16,256]{3,2,1,0:T(8,128)(2,1)S(1)}, u32[]{:S(2)}, u32[]{:S(2)}) async-start(bf16[16,18,16,256]{3,2,1,0:T(8,128)(2,1)} %get-tuple-element.58), calls=%async_computation.1 | async-start | bytes 4718592 | tf_op jit(solution)/shard_map/all_to_all | solution.py:62
  98.5 2.9 %collective-permute-start.7 = (f32[512,512]{1,0:T(8,128)}, f32[512,512]{1,0:T(8,128)S(1)}, u32[]{:S(2)}, u32[]{:S(2)}) collective-permute-start(f32[512,512]{1,0:T(8,128)} %get-tuple-element.64.own), channel_id=1, source_target_pairs={{0,32},{1,33},{2,34},{3,35},{4,36},{5,37},{6,38},{7,39},{8,40},{9,... | collective-permute-start | bytes 3145736 | tf_op jit(solution)/shard_map/ppermute | solution.py:43
  101.4 1.0 copy-start.2
  119.1 31.9 %all-to-all-start.2 = ((bf16[16,16,16,256]{3,2,1,0:T(8,128)(2,1)}), bf16[16,16,16,256]{3,2,1,0:T(8,128)(2,1)}, u32[]{:S(2)}, u32[]{:S(2)}) async-start(bf16[16,16,16,256]{3,2,1,0:T(8,128)(2,1)} %get-tuple-element.68), calls=%async_computation.2 | async-start | bytes 4194304 | tf_op jit(solution)/shard_map/all_to_all | solution.py:62
  124.7 4.9 %copy-start.12 = (bf16[4,256,256]{2,1,0:T(8,128)(2,1)S(1)}, bf16[4,256,256]{2,1,0:T(8,128)(2,1)}, u32[]{:S(2)}) copy-start(bf16[4,256,256]{2,1,0:T(8,128)(2,1)} %get-tuple-element.71) | copy-start | bytes 1572868
  125.1 27.9 %collective-permute-start.10 = (bf16[4,256,256]{2,1,0:T(8,128)(2,1)}, bf16[4,256,256]{2,1,0:T(8,128)(2,1)S(1)}, u32[]{:S(2)}, u32[]{:S(2)}) collective-permute-start(bf16[4,256,256]{2,1,0:T(8,128)(2,1)} %get-tuple-element.72), channel_id=1, source_target_pairs={{0,96},{1,97},{2,98},{3,99},{4,100},{5,101},{6,102},{7,103},{8,104... | collective-permute-start | bytes 1572872 | tf_op jit(solution)/shard_map/ppermute | solution.py:43
  129.6 23.4 %collective-permute-start.8 = (bf16[4,256,256]{2,1,0:T(8,128)(2,1)}, bf16[4,256,256]{2,1,0:T(8,128)(2,1)S(1)}, u32[]{:S(2)}, u32[]{:S(2)}) collective-permute-start(bf16[4,256,256]{2,1,0:T(8,128)(2,1)} %get-tuple-element.70), channel_id=1, source_target_pairs={{0,32},{1,33},{2,34},{3,35},{4,36},{5,37},{6,38},{7,39},{8,40},{9,... | collective-permute-start | bytes 1572872 | tf_op jit(solution)/shard_map/ppermute | solution.py:43
  129.6 23.8 %collective-permute-start.9 = (bf16[4,256,256]{2,1,0:T(8,128)(2,1)S(1)}, bf16[4,256,256]{2,1,0:T(8,128)(2,1)S(1)}, u32[]{:S(2)}, u32[]{:S(2)}) collective-permute-start(bf16[4,256,256]{2,1,0:T(8,128)(2,1)S(1)} %copy-done.12), channel_id=1, source_target_pairs={{0,64},{1,65},{2,66},{3,67},{4,68},{5,69},{6,70},{7,71},{8,72},{9,... | collective-permute-start | bytes 1572872 | tf_op jit(solution)/shard_map/ppermute | solution.py:43
  153.0 4.4 %copy-start.4 = (bf16[4,256,256]{2,1,0:T(8,128)(2,1)}, bf16[4,256,256]{2,1,0:T(8,128)(2,1)S(1)}, u32[]{:S(2)}) copy-start(bf16[4,256,256]{2,1,0:T(8,128)(2,1)S(1)} %collective-permute-done.10.back3) | copy-start | bytes 1572868
  153.1 4.3 %copy-start.5 = (bf16[4,256,256]{2,1,0:T(8,128)(2,1)}, bf16[4,256,256]{2,1,0:T(8,128)(2,1)S(1)}, u32[]{:S(2)}) copy-start(bf16[4,256,256]{2,1,0:T(8,128)(2,1)S(1)} %collective-permute-done.8.back1) | copy-start | bytes 1572868
  153.4 4.0 %copy-start.6 = (bf16[4,256,256]{2,1,0:T(8,128)(2,1)}, bf16[4,256,256]{2,1,0:T(8,128)(2,1)S(1)}, u32[]{:S(2)}) copy-start(bf16[4,256,256]{2,1,0:T(8,128)(2,1)S(1)} %collective-permute-done.9.back2) | copy-start | bytes 1572868
  153.5 7.6 %collective-permute-start.11 = (bf16[21,16,256]{2,1,0:T(8,128)(2,1)S(1)}, bf16[21,16,256]{2,1,0:T(8,128)(2,1)S(1)}, u32[]{:S(2)}, u32[]{:S(2)}) collective-permute-start(bf16[21,16,256]{2,1,0:T(8,128)(2,1)S(1)} %get-tuple-element.83), channel_id=1, source_target_pairs={{0,4},{1,5},{2,6},{3,7},{4,0},{5,1},{6,2},{7,3},{8,12},{9,13},{10,... | collective-permute-start | bytes 516104 | tf_op jit(solution)/shard_map/ppermute | solution.py:43
  154.5 7.4 %collective-permute-start.12 = (bf16[21,16,256]{2,1,0:T(8,128)(2,1)S(1)}, bf16[21,16,256]{2,1,0:T(8,128)(2,1)S(1)}, u32[]{:S(2)}, u32[]{:S(2)}) collective-permute-start(bf16[21,16,256]{2,1,0:T(8,128)(2,1)S(1)} %get-tuple-element.82), channel_id=1, source_target_pairs={{0,64},{1,65},{2,66},{3,67},{4,68},{5,69},{6,70},{7,71},{8,72},{9,... | collective-permute-start | bytes 516104 | tf_op jit(solution)/shard_map/ppermute | solution.py:43
  157.2 6.5 %collective-permute-start.13 = (bf16[21,16,256]{2,1,0:T(8,128)(2,1)S(1)}, bf16[21,16,256]{2,1,0:T(8,128)(2,1)S(1)}, u32[]{:S(2)}, u32[]{:S(2)}) collective-permute-start(bf16[21,16,256]{2,1,0:T(8,128)(2,1)S(1)} %get-tuple-element.83), channel_id=1, source_target_pairs={{0,68},{1,69},{2,70},{3,71},{4,64},{5,65},{6,66},{7,67},{8,76},{9,... | collective-permute-start | bytes 516104 | tf_op jit(solution)/shard_map/ppermute | solution.py:43
  163.7 6.2 %collective-permute-start.14 = (f32[21,16,256]{2,1,0:T(8,128)S(1)}, f32[21,16,256]{2,1,0:T(8,128)S(1)}, u32[]{:S(2)}, u32[]{:S(2)}) collective-permute-start(f32[21,16,256]{2,1,0:T(8,128)S(1)} %fusion.1), channel_id=1, source_target_pairs={{0,32},{1,33},{2,34},{3,35},{4,36},{5,37},{6,38},{7,39},{8,40},{9,... | collective-permute-start | bytes 1032200 | tf_op jit(solution)/shard_map/ppermute | solution.py:43
Sparse Core Ops, SparseCore 0:
  15.9 63.1 all-gather.2

commit v9 on v8

--- a/solution.py
+++ b/solution.py
@@ -218,7 +218,7 @@
     for f in range(32):
         z, y, x = f // 8, f // 4 % 2, f % 4
         for k in range(4):
-            up[k, f * rows : (f + 1) * rows, :] = pieces[BY_BITS.index(z * 4 + x), y * 4 + k]
+            up[k, f * rows : (f + 1) * rows, :] = pieces[DIAGONAL.index(z * 4 + x), y * 4 + k]
 
 
 def gather_down(pieces, down):
@@ -229,7 +229,7 @@
                 side, step = unit // 4, unit % 4
                 first = (x * 4 + step) * rows
                 down[z, first : first + rows, side * half : (side + 1) * half] = pieces[
-                    BY_BITS.index(z * 4 + x), 8 + unit
+                    DIAGONAL.index(z * 4 + x), 8 + unit
                 ]
 
 
@@ -482,7 +482,7 @@
     down_kept = jnp.where(core == 0, first[4:12], second[4:12])
     up_down = jnp.concatenate([first[:4], second[:4], down_kept])
     conv_two = jnp.concatenate([first[12:], second[12:]])
-    up_down = over_plane(jnp.broadcast_to(up_down, (16, *up_down.shape)), BY_BITS)
+    up_down = over_plane(jnp.broadcast_to(up_down, (16, *up_down.shape)), DIAGONAL)
     conv_two = lax.all_gather(conv_two, "fsdp", axis_index_groups=PLANES)
 
     images_pair = send(images, "c")

time: 180 us -> 181 us (level)
    ppermute x15, starting transfers between devices: 25.6 us -> 23 us  [send(): return lax.ppermute(value, AXES, STEP[move])]
    all_to_all x3, starting transfers between devices: 17.6 us -> 20 us  [over_plane(): lax.all_to_all(blocks, 'fsdp', split_axis=0, concat_axis=0, axis_index_gr...]
  transfers between devices with their start and end apart: 19 -> 19, of which waited for: 11 -> 10; matrix products, arithmetic and copies ran while one was open for 4% -> 4% of each run, Pallas kernels for 32% -> 32%
where the time goes in v9:
time: 181 us; the launch traced here: 180 us
  Pallas kernels  57.8 us (32%)
  waiting for transfers between devices  48.6 us (27%)
  starting transfers between devices  43.1 us (24%)
  between operations  14.4 us (8%)
  local copies, waits for them, and re-layouts  12 us (7%)
  other arithmetic  4.03 us (2%)
    all_to_all x3, waiting for transfers between devices, over_plane(): lax.all_to_all(blocks, 'fsdp', split_axis=0, concat_axis=0, axis_index_gr...  30.7 us
    ppermute x15, starting transfers between devices, send(): return lax.ppermute(value, AXES, STEP[move])  23 us
    all_to_all x3, starting transfers between devices, over_plane(): lax.all_to_all(blocks, 'fsdp', split_axis=0, concat_axis=0, axis_index_gr...  20 us
    ppermute x15, waiting for transfers between devices, send(): return lax.ppermute(value, AXES, STEP[move])  17.8 us
    pallas_call x2, Pallas kernels, normed_windows(): kernel_call(functools.partial(norm_kernel, extent), (jax.ShapeDtypeStruct...  13.1 us
    pallas_call x1, Pallas kernels, per_device(): kernel_call(conv_kernel, (jax.ShapeDtypeStruct((4, low_rows, half), F32),...  12.6 us
    pallas_call x1, Pallas kernels, per_device(): kernel_call(functools.partial(grad_conv_kernel, loss_scale), (jax.ShapeDt...  12.2 us
    pallas_call x1, Pallas kernels, per_device(): kernel_call(functools.partial(output_kernel, extent, loss_scale), (*(bloc...  8.12 us
  transfers between devices with their start and end apart: 19, of which 10 were waited for; matrix products, arithmetic and copies ran while one was open for 4% of the time, Pallas kernels for 32%

profile of v9, /device:TPU:1, one launch (start us, length us, event | category | flops | bytes accessed | tf_op | source)
XLA Modules:
  0.0 180.0 jit_solution(12723150264262009087)
XLA Ops:
  9.1 2.2 %collective-permute-start.2 = (bf16[21,16,256]{2,1,0:T(8,128)(2,1)S(1)}, bf16[21,16,256]{2,1,0:T(8,128)(2,1)S(1)}, u32[]{:S(2)}, u32[]{:S(2)}) collective-permute-start(bf16[21,16,256]{2,1,0:T(8,128)(2,1)S(1)} %pad_maximum_fusion.1), channel_id=1, source_target_pairs={{0,4},{1,5},{2,6},{3,7},{4,0},{5,1},{6,2},{7,3},{8,12},{9,13},{10,... | collective-permute-start | bytes 516104 | tf_op jit(solution)/shard_map/ppermute | solution.py:43
  11.3 3.1 %shard_map.140 = (bf16[4,256,256]{2,1,0:T(8,128)(2,1)}, bf16[4,256,256]{2,1,0:T(8,128)(2,1)}, bf16[4,256,256]{2,1,0:T(8,128)(2,1)}, bf16[4,256,256]{2,1,0:T(8,128)(2,1)}) custom-call(s32[1]{0:T(128)} %bitcast.number, bf16[8,256,512]{2,1,0:T(8,128)(2,1)} %bitcast.72), custom_call_target="tpu_custom_call" | custom-call | bytes 4194304 | tf_op jit(solution)/shard_map/pallas_call | solution.py:470
  15.8 1.6 broadcast_in_dim.72
  17.4 8.0 %all-to-all-start = ((bf16[16,16,16,256]{3,2,1,0:T(8,128)(2,1)}), bf16[16,16,16,256]{3,2,1,0:T(8,128)(2,1)S(1)}, u32[]{:S(2)}, u32[]{:S(2)}) async-start(bf16[16,16,16,256]{3,2,1,0:T(8,128)(2,1)} %broadcast_in_dim.72), calls=%async_computation | async-start | bytes 4194304 | tf_op jit(solution)/shard_map/all_to_all | solution.py:62
  25.5 1.9 %collective-permute-start = (s32[4,2]{0,1:T(2,128)S(1)}, s32[4,2]{0,1:T(2,128)S(1)}, u32[]{:S(2)}, u32[]{:S(2)}) collective-permute-start(s32[4,2]{0,1:T(2,128)S(1)} %pad_add_fusion.2), channel_id=1, source_target_pairs={{0,32},{1,33},{2,34},{3,35},{4,36},{5,37},{6,38},{7,39},{8,40},{9,... | collective-permute-start | bytes 104 | tf_op jit(solution)/shard_map/ppermute | solution.py:43
  29.1 2.9 %collective-permute-start.4 = (bf16[4,256,256]{2,1,0:T(8,128)(2,1)}, bf16[4,256,256]{2,1,0:T(8,128)(2,1)}, u32[]{:S(2)}, u32[]{:S(2)}) collective-permute-start(bf16[4,256,256]{2,1,0:T(8,128)(2,1)} %get-tuple-element.51), channel_id=1, source_target_pairs={{0,64},{1,65},{2,66},{3,67},{4,68},{5,69},{6,70},{7,71},{8,72},{9,... | collective-permute-start | bytes 1572872 | tf_op jit(solution)/shard_map/ppermute | solution.py:43
  34.5 6.5 %shard_map.138 = (bf16[16,256,512]{2,1,0:T(8,128)(2,1)}, bf16[4,256,256]{2,1,0:T(8,128)(2,1)}) custom-call(s32[32]{0:T(128)} %concatenate.37.meta, bf16[4,256,512]{2,1,0:T(8,128)(2,1)} %bitcast.74, f32[1,512]{1,0:T(1,128)} %bitcast.82, f32[1,512]{1,0:T(1,128)} %bitcast.84), custom_call_target="tpu_custom_call" | custom-call | flops 20971520 | bytes 6291456 | tf_op jit(solution)/shard_map/pallas_call | solution.py:190
  41.0 6.6 %shard_map.139 = (bf16[16,256,512]{2,1,0:T(8,128)(2,1)}, bf16[4,256,256]{2,1,0:T(8,128)(2,1)}) custom-call(s32[32]{0:T(128)} %concatenate.39.meta, bf16[4,256,512]{2,1,0:T(8,128)(2,1)} %bitcast.18.image, f32[1,512]{1,0:T(1,128)} %bitcast.83, f32[1,512]{1,0:T(1,128)} %bitcast.85), custom_call_target="tpu_custom_call" | custom-call | flops 20971520 | bytes 6291456 | tf_op jit(solution)/shard_map/pallas_call | solution.py:190
  48.4 7.6 %collective-permute-done.5.cot3 = bf16[4,256,256]{2,1,0:T(8,128)(2,1)} collective-permute-done((bf16[4,256,256]{2,1,0:T(8,128)(2,1)}, bf16[4,256,256]{2,1,0:T(8,128)(2,1)}, u32[]{:S(2)}, u32[]{:S(2)}) %collective-permute-start.5) | collective-permute-done | bytes 524320 | tf_op jit(solution)/shard_map/ppermute | solution.py:43
  56.0 1.3 copy-done.1
  57.3 5.2 %shard_map.141 = (bf16[4,512,256]{2,1,0:T(8,128)(2,1)}, f32[512,512]{1,0:T(8,128)}) custom-call(s32[32]{0:T(128)} %concatenate.35.meta, bf16[4,256,256]{2,1,0:T(8,128)(2,1)} %get-tuple-element.49.cot0, bf16[4,256,256]{2,1,0:T(8,128)(2,1)} %collective-permute-done.3.cot1, bf16[4,256,256]{2,1,0:T(8,128)(2,1)} %collective-permute-done.4.cot2, ...), custom_call_target="tpu_custom_call" | custom-call | flops 536870912 | bytes 5242880 | tf_op jit(solution)/shard_map/pallas_call | solution.py:525
  62.5 1.5 collective-permute-start.6
  64.0 2.5 %collective-permute-done.6.got = f32[512,512]{1,0:T(8,128)S(1)} collective-permute-done((f32[512,512]{1,0:T(8,128)}, f32[512,512]{1,0:T(8,128)S(1)}, u32[]{:S(2)}, u32[]{:S(2)}) %collective-permute-start.6) | collective-permute-done | bytes 1048608 | tf_op jit(solution)/shard_map/ppermute | solution.py:43
  66.5 1.0 copy-done.11
  67.6 12.2 %shard_map.142 = (bf16[512,512]{1,0:T(8,128)(2,1)}, bf16[16,18,16,256]{3,2,1,0:T(8,128)(2,1)}) custom-call(f32[512,128]{1,0:T(8,128)} %broadcast_in_dim.69.mask, f32[512,512]{1,0:T(8,128)} %get-tuple-element.54.own, f32[512,512]{1,0:T(8,128)} %copy-done.11, bf16[4,512,256]{2,1,0:T(8,128)(2,1)} %get-tuple-element.55.folded, ...), custom_call_target="tpu_custom_call" | custom-call | flops 5368709120 | bytes 15728640 | tf_op jit(solution)/shard_map/pallas_call | solution.py:544
  79.7 5.9 %all-to-all-start.1 = ((bf16[16,18,16,256]{3,2,1,0:T(8,128)(2,1)}), bf16[16,18,16,256]{3,2,1,0:T(8,128)(2,1)S(1)}, u32[]{:S(2)}, u32[]{:S(2)}) async-start(bf16[16,18,16,256]{3,2,1,0:T(8,128)(2,1)} %get-tuple-element.58), calls=%async_computation.1 | async-start | bytes 4718592 | tf_op jit(solution)/shard_map/all_to_all | solution.py:62
  85.7 12.6 %shard_map.143 = (f32[4,512,256]{2,1,0:T(8,128)}, bf16[4,512,256]{2,1,0:T(8,128)(2,1)}, f32[512,512]{1,0:T(8,128)}) custom-call(f32[512,128]{1,0:T(8,128)} %broadcast_in_dim.69.mask, bf16[16,18,16,256]{3,2,1,0:T(8,128)(2,1)} %bitcast.92, bf16[16,16,16,256]{3,2,1,0:T(8,128)(2,1)} %copy-done.1, bf16[16,256,512]{2,1,0:T(8,128)(2,1)} %get-tuple-element.60.windows_own, ...), custom_call_target="tpu_custom_call" | custom-call | flops 5368709120 | bytes 18874368 | tf_op jit(solution)/shard_map/pallas_call | solution.py:559
  98.7 2.5 %collective-permute-done.7.got = f32[512,512]{1,0:T(8,128)S(1)} collective-permute-done((f32[512,512]{1,0:T(8,128)}, f32[512,512]{1,0:T(8,128)S(1)}, u32[]{:S(2)}, u32[]{:S(2)}) %collective-permute-start.7) | collective-permute-done | bytes 1048608 | tf_op jit(solution)/shard_map/ppermute | solution.py:43
  101.2 1.0 copy-done.2
  102.2 8.1 %shard_map.144 = (bf16[4,256,256]{2,1,0:T(8,128)(2,1)}, bf16[4,256,256]{2,1,0:T(8,128)(2,1)}, bf16[4,256,256]{2,1,0:T(8,128)(2,1)}, bf16[4,256,256]{2,1,0:T(8,128)(2,1)}, bf16[16,16,16,256]{3,2,1,0:T(8,128)(2,1)}) custom-call(s32[32]{0:T(128)} %concatenate.35.meta, f32[512,128]{1,0:T(8,128)} %broadcast_in_dim.69.mask, f32[512,512]{1,0:T(8,128)} %get-tuple-element.64.own, ...), custom_call_target="tpu_custom_call" | custom-call | flops 1610612736 | bytes 14680064 | tf_op jit(solution)/shard_map/pallas_call | solution.py:574
  110.3 9.0 %all-to-all-done.1 = bf16[16,18,16,256]{3,2,1,0:T(8,128)(2,1)S(1)} async-done(((bf16[16,18,16,256]{3,2,1,0:T(8,128)(2,1)}), bf16[16,18,16,256]{3,2,1,0:T(8,128)(2,1)S(1)}, u32[]{:S(2)}, u32[]{:S(2)}) %all-to-all-start.1) | async-done | bytes 2359328 | tf_op jit(solution)/shard_map/all_to_all | solution.py:62
  119.3 6.1 %all-to-all-start.2 = ((bf16[16,16,16,256]{3,2,1,0:T(8,128)(2,1)}), bf16[16,16,16,256]{3,2,1,0:T(8,128)(2,1)}, u32[]{:S(2)}, u32[]{:S(2)}) async-start(bf16[16,16,16,256]{3,2,1,0:T(8,128)(2,1)} %get-tuple-element.68), calls=%async_computation.2 | async-start | bytes 4194304 | tf_op jit(solution)/shard_map/all_to_all | solution.py:62
  125.8 4.4 %collective-permute-start.10 = (bf16[4,256,256]{2,1,0:T(8,128)(2,1)}, bf16[4,256,256]{2,1,0:T(8,128)(2,1)S(1)}, u32[]{:S(2)}, u32[]{:S(2)}) collective-permute-start(bf16[4,256,256]{2,1,0:T(8,128)(2,1)} %get-tuple-element.72), channel_id=1, source_target_pairs={{0,96},{1,97},{2,98},{3,99},{4,100},{5,101},{6,102},{7,103},{8,104... | collective-permute-start | bytes 1572872 | tf_op jit(solution)/shard_map/ppermute | solution.py:43
  130.4 21.7 %all-to-all-done.2 = bf16[16,16,16,256]{3,2,1,0:T(8,128)(2,1)} async-done(((bf16[16,16,16,256]{3,2,1,0:T(8,128)(2,1)}), bf16[16,16,16,256]{3,2,1,0:T(8,128)(2,1)}, u32[]{:S(2)}, u32[]{:S(2)}) %all-to-all-start.2) | async-done | bytes 2097184 | tf_op jit(solution)/shard_map/all_to_all | solution.py:62
  152.1 1.9 %convert_reduce_fusion.1 = f32[16,16,256]{2,1,0:T(8,128)S(1)} fusion(bf16[16,16,16,256]{3,2,1,0:T(8,128)(2,1)} %all-to-all-done.2), kind=kLoop, calls=%fused_computation.1 | loop fusion | flops 2031616 | bytes 2359296 | tf_op jit(solution)/shard_map/reduce_sum | solution.py:596
  154.2 1.4 collective-permute-start.11
  155.6 2.6 %collective-permute-start.12 = (bf16[21,16,256]{2,1,0:T(8,128)(2,1)S(1)}, bf16[21,16,256]{2,1,0:T(8,128)(2,1)S(1)}, u32[]{:S(2)}, u32[]{:S(2)}) collective-permute-start(bf16[21,16,256]{2,1,0:T(8,128)(2,1)S(1)} %get-tuple-element.82), channel_id=1, source_target_pairs={{0,64},{1,65},{2,66},{3,67},{4,68},{5,69},{6,70},{7,71},{8,72},{9,... | collective-permute-start | bytes 516104 | tf_op jit(solution)/shard_map/ppermute | solution.py:43
  158.2 3.6 %shard_map.145 = f32[8,256,512]{2,1,0:T(8,128)} custom-call(s32[1]{0:T(128)} %bitcast.number, bf16[4,256,256]{2,1,0:T(8,128)(2,1)} %get-tuple-element.73.back0, bf16[4,256,256]{2,1,0:T(8,128)(2,1)} %copy-done.5, bf16[4,256,256]{2,1,0:T(8,128)(2,1)} %copy-done.6, bf16[4,256,256]{2,1,0:T(8,128)(2,1)} %copy-done.4), custom_call_target="tpu_custom_call" | custom-call | bytes 6291456 | tf_op jit(solution)/shard_map/pallas_call | solution.py:613
  161.9 1.1 collective-permute-done.12
  163.0 1.7 collective-permute-done.13
  164.8 4.7 %collective-permute-start.14 = (f32[21,16,256]{2,1,0:T(8,128)S(1)}, f32[21,16,256]{2,1,0:T(8,128)S(1)}, u32[]{:S(2)}, u32[]{:S(2)}) collective-permute-start(f32[21,16,256]{2,1,0:T(8,128)S(1)} %fusion.1), channel_id=1, source_target_pairs={{0,32},{1,33},{2,34},{3,35},{4,36},{5,37},{6,38},{7,39},{8,40},{9,... | collective-permute-start | bytes 1032200 | tf_op jit(solution)/shard_map/ppermute | solution.py:43
  169.5 1.3 collective-permute-done.14
  (94 shorter events, 11.8 us)
Async XLA Ops:
  7.2 1.0 copy-start
  7.2 78.5 %all-gather.3.cloned.1.call-start = ((), (), s32[]{:S(2)}) async-start(), calls=%async_computation.3 | async-start | bytes 2506752 | tf_op jit(solution)/shard_map/all_gather | solution.py:486
  9.1 5.9 %collective-permute-start.2 = (bf16[21,16,256]{2,1,0:T(8,128)(2,1)S(1)}, bf16[21,16,256]{2,1,0:T(8,128)(2,1)S(1)}, u32[]{:S(2)}, u32[]{:S(2)}) collective-permute-start(bf16[21,16,256]{2,1,0:T(8,128)(2,1)S(1)} %pad_maximum_fusion.1), channel_id=1, source_target_pairs={{0,4},{1,5},{2,6},{3,7},{4,0},{5,1},{6,2},{7,3},{8,12},{9,13},{10,... | collective-permute-start | bytes 516104 | tf_op jit(solution)/shard_map/ppermute | solution.py:43
  17.4 8.0 %copy-start.7 = (s32[4,1]{0,1:T(1,128)S(1)}, s32[4,1]{0,1:T(1,128)}, u32[]{:S(2)}) copy-start(s32[4,1]{0,1:T(1,128)} %param.12) | copy-start | bytes 52
  17.4 8.0 %copy-start.8 = (s32[4]{0:T(128)S(1)}, s32[4]{0:T(128)}, u32[]{:S(2)}) copy-start(s32[4]{0:T(128)} %param.13) | copy-start | bytes 52
  17.4 10.0 %copy-start.3 = (bf16[4,16,16,512]{3,2,1,0:T(8,128)(2,1)S(1)}, bf16[4,16,16,512]{3,2,1,0:T(8,128)(2,1)}, u32[]{:S(2)}) copy-start(bf16[4,16,16,512]{3,2,1,0:T(8,128)(2,1)} %param.11) | copy-start | bytes 3145732
  17.4 10.8 %copy-start.9 = (s32[8]{0:T(128)S(1)}, s32[8]{0:T(128)}, u32[]{:S(2)}) copy-start(s32[8]{0:T(128)} %param.14) | copy-start | bytes 100
  17.4 10.8 %copy-start.10 = (s32[8]{0:T(128)S(1)}, s32[8]{0:T(128)}, u32[]{:S(2)}) copy-start(s32[8]{0:T(128)} %param.15) | copy-start | bytes 100
  17.4 38.5 %all-to-all-start = ((bf16[16,16,16,256]{3,2,1,0:T(8,128)(2,1)}), bf16[16,16,16,256]{3,2,1,0:T(8,128)(2,1)S(1)}, u32[]{:S(2)}, u32[]{:S(2)}) async-start(bf16[16,16,16,256]{3,2,1,0:T(8,128)(2,1)} %broadcast_in_dim.72), calls=%async_computation | async-start | bytes 4194304 | tf_op jit(solution)/shard_map/all_to_all | solution.py:62
  25.5 2.7 %collective-permute-start = (s32[4,2]{0,1:T(2,128)S(1)}, s32[4,2]{0,1:T(2,128)S(1)}, u32[]{:S(2)}, u32[]{:S(2)}) collective-permute-start(s32[4,2]{0,1:T(2,128)S(1)} %pad_add_fusion.2), channel_id=1, source_target_pairs={{0,32},{1,33},{2,34},{3,35},{4,36},{5,37},{6,38},{7,39},{8,40},{9,... | collective-permute-start | bytes 104 | tf_op jit(solution)/shard_map/ppermute | solution.py:43
  27.4 13.6 %collective-permute-start.1 = (bf16[4,16,16,512]{3,2,1,0:T(8,128)(2,1)S(1)}, bf16[4,16,16,512]{3,2,1,0:T(8,128)(2,1)}, u32[]{:S(2)}, u32[]{:S(2)}) collective-permute-start(bf16[4,16,16,512]{3,2,1,0:T(8,128)(2,1)S(1)} %copy-done.3), channel_id=1, source_target_pairs={{0,32},{1,33},{2,34},{3,35},{4,36},{5,37},{6,38},{7,39},{8,40},{9,... | collective-permute-start | bytes 3145736 | tf_op jit(solution)/shard_map/ppermute | solution.py:43
  28.7 19.7 %collective-permute-start.3 = (bf16[4,256,256]{2,1,0:T(8,128)(2,1)}, bf16[4,256,256]{2,1,0:T(8,128)(2,1)}, u32[]{:S(2)}, u32[]{:S(2)}) collective-permute-start(bf16[4,256,256]{2,1,0:T(8,128)(2,1)} %get-tuple-element.50), channel_id=1, source_target_pairs={{0,32},{1,33},{2,34},{3,35},{4,36},{5,37},{6,38},{7,39},{8,40},{9,... | collective-permute-start | bytes 1572872 | tf_op jit(solution)/shard_map/ppermute | solution.py:43
  29.1 19.3 %collective-permute-start.4 = (bf16[4,256,256]{2,1,0:T(8,128)(2,1)}, bf16[4,256,256]{2,1,0:T(8,128)(2,1)}, u32[]{:S(2)}, u32[]{:S(2)}) collective-permute-start(bf16[4,256,256]{2,1,0:T(8,128)(2,1)} %get-tuple-element.51), channel_id=1, source_target_pairs={{0,64},{1,65},{2,66},{3,67},{4,68},{5,69},{6,70},{7,71},{8,72},{9,... | collective-permute-start | bytes 1572872 | tf_op jit(solution)/shard_map/ppermute | solution.py:43
  32.0 24.0 %collective-permute-start.5 = (bf16[4,256,256]{2,1,0:T(8,128)(2,1)}, bf16[4,256,256]{2,1,0:T(8,128)(2,1)}, u32[]{:S(2)}, u32[]{:S(2)}) collective-permute-start(bf16[4,256,256]{2,1,0:T(8,128)(2,1)} %get-tuple-element.52), channel_id=1, source_target_pairs={{0,96},{1,97},{2,98},{3,99},{4,100},{5,101},{6,102},{7,103},{8,104... | collective-permute-start | bytes 1572872 | tf_op jit(solution)/shard_map/ppermute | solution.py:43
  56.0 1.3 copy-start.1
  62.5 4.0 %collective-permute-start.6 = (f32[512,512]{1,0:T(8,128)}, f32[512,512]{1,0:T(8,128)S(1)}, u32[]{:S(2)}, u32[]{:S(2)}) collective-permute-start(f32[512,512]{1,0:T(8,128)} %get-tuple-element.54.own), channel_id=1, source_target_pairs={{0,32},{1,33},{2,34},{3,35},{4,36},{5,37},{6,38},{7,39},{8,40},{9,... | collective-permute-start | bytes 3145736 | tf_op jit(solution)/shard_map/ppermute | solution.py:43
  66.5 1.0 copy-start.11
  79.7 39.6 %all-to-all-start.1 = ((bf16[16,18,16,256]{3,2,1,0:T(8,128)(2,1)}), bf16[16,18,16,256]{3,2,1,0:T(8,128)(2,1)S(1)}, u32[]{:S(2)}, u32[]{:S(2)}) async-start(bf16[16,18,16,256]{3,2,1,0:T(8,128)(2,1)} %get-tuple-element.58), calls=%async_computation.1 | async-start | bytes 4718592 | tf_op jit(solution)/shard_map/all_to_all | solution.py:62
  98.3 2.9 %collective-permute-start.7 = (f32[512,512]{1,0:T(8,128)}, f32[512,512]{1,0:T(8,128)S(1)}, u32[]{:S(2)}, u32[]{:S(2)}) collective-permute-start(f32[512,512]{1,0:T(8,128)} %get-tuple-element.64.own), channel_id=1, source_target_pairs={{0,32},{1,33},{2,34},{3,35},{4,36},{5,37},{6,38},{7,39},{8,40},{9,... | collective-permute-start | bytes 3145736 | tf_op jit(solution)/shard_map/ppermute | solution.py:43
  101.2 1.0 copy-start.2
  119.3 32.7 %all-to-all-start.2 = ((bf16[16,16,16,256]{3,2,1,0:T(8,128)(2,1)}), bf16[16,16,16,256]{3,2,1,0:T(8,128)(2,1)}, u32[]{:S(2)}, u32[]{:S(2)}) async-start(bf16[16,16,16,256]{3,2,1,0:T(8,128)(2,1)} %get-tuple-element.68), calls=%async_computation.2 | async-start | bytes 4194304 | tf_op jit(solution)/shard_map/all_to_all | solution.py:62
  125.4 4.7 %copy-start.12 = (bf16[4,256,256]{2,1,0:T(8,128)(2,1)S(1)}, bf16[4,256,256]{2,1,0:T(8,128)(2,1)}, u32[]{:S(2)}) copy-start(bf16[4,256,256]{2,1,0:T(8,128)(2,1)} %get-tuple-element.71) | copy-start | bytes 1572868
  125.8 28.3 %collective-permute-start.10 = (bf16[4,256,256]{2,1,0:T(8,128)(2,1)}, bf16[4,256,256]{2,1,0:T(8,128)(2,1)S(1)}, u32[]{:S(2)}, u32[]{:S(2)}) collective-permute-start(bf16[4,256,256]{2,1,0:T(8,128)(2,1)} %get-tuple-element.72), channel_id=1, source_target_pairs={{0,96},{1,97},{2,98},{3,99},{4,100},{5,101},{6,102},{7,103},{8,104... | collective-permute-start | bytes 1572872 | tf_op jit(solution)/shard_map/ppermute | solution.py:43
  130.1 24.0 %collective-permute-start.8 = (bf16[4,256,256]{2,1,0:T(8,128)(2,1)}, bf16[4,256,256]{2,1,0:T(8,128)(2,1)S(1)}, u32[]{:S(2)}, u32[]{:S(2)}) collective-permute-start(bf16[4,256,256]{2,1,0:T(8,128)(2,1)} %get-tuple-element.70), channel_id=1, source_target_pairs={{0,32},{1,33},{2,34},{3,35},{4,36},{5,37},{6,38},{7,39},{8,40},{9,... | collective-permute-start | bytes 1572872 | tf_op jit(solution)/shard_map/ppermute | solution.py:43
  130.1 24.0 %collective-permute-start.9 = (bf16[4,256,256]{2,1,0:T(8,128)(2,1)S(1)}, bf16[4,256,256]{2,1,0:T(8,128)(2,1)S(1)}, u32[]{:S(2)}, u32[]{:S(2)}) collective-permute-start(bf16[4,256,256]{2,1,0:T(8,128)(2,1)S(1)} %copy-done.12), channel_id=1, source_target_pairs={{0,64},{1,65},{2,66},{3,67},{4,68},{5,69},{6,70},{7,71},{8,72},{9,... | collective-permute-start | bytes 1572872 | tf_op jit(solution)/shard_map/ppermute | solution.py:43
  154.1 4.1 %copy-start.4 = (bf16[4,256,256]{2,1,0:T(8,128)(2,1)}, bf16[4,256,256]{2,1,0:T(8,128)(2,1)S(1)}, u32[]{:S(2)}) copy-start(bf16[4,256,256]{2,1,0:T(8,128)(2,1)S(1)} %collective-permute-done.10.back3) | copy-start | bytes 1572868
  154.1 4.1 %copy-start.5 = (bf16[4,256,256]{2,1,0:T(8,128)(2,1)}, bf16[4,256,256]{2,1,0:T(8,128)(2,1)S(1)}, u32[]{:S(2)}) copy-start(bf16[4,256,256]{2,1,0:T(8,128)(2,1)S(1)} %collective-permute-done.8.back1) | copy-start | bytes 1572868
  154.1 4.1 %copy-start.6 = (bf16[4,256,256]{2,1,0:T(8,128)(2,1)}, bf16[4,256,256]{2,1,0:T(8,128)(2,1)S(1)}, u32[]{:S(2)}) copy-start(bf16[4,256,256]{2,1,0:T(8,128)(2,1)S(1)} %collective-permute-done.9.back2) | copy-start | bytes 1572868
  154.2 7.7 %collective-permute-start.11 = (bf16[21,16,256]{2,1,0:T(8,128)(2,1)S(1)}, bf16[21,16,256]{2,1,0:T(8,128)(2,1)S(1)}, u32[]{:S(2)}, u32[]{:S(2)}) collective-permute-start(bf16[21,16,256]{2,1,0:T(8,128)(2,1)S(1)} %get-tuple-element.83), channel_id=1, source_target_pairs={{0,4},{1,5},{2,6},{3,7},{4,0},{5,1},{6,2},{7,3},{8,12},{9,13},{10,... | collective-permute-start | bytes 516104 | tf_op jit(solution)/shard_map/ppermute | solution.py:43
  155.6 7.4 %collective-permute-start.12 = (bf16[21,16,256]{2,1,0:T(8,128)(2,1)S(1)}, bf16[21,16,256]{2,1,0:T(8,128)(2,1)S(1)}, u32[]{:S(2)}, u32[]{:S(2)}) collective-permute-start(bf16[21,16,256]{2,1,0:T(8,128)(2,1)S(1)} %get-tuple-element.82), channel_id=1, source_target_pairs={{0,64},{1,65},{2,66},{3,67},{4,68},{5,69},{6,70},{7,71},{8,72},{9,... | collective-permute-start | bytes 516104 | tf_op jit(solution)/shard_map/ppermute | solution.py:43
  158.2 6.5 %collective-permute-start.13 = (bf16[21,16,256]{2,1,0:T(8,128)(2,1)S(1)}, bf16[21,16,256]{2,1,0:T(8,128)(2,1)S(1)}, u32[]{:S(2)}, u32[]{:S(2)}) collective-permute-start(bf16[21,16,256]{2,1,0:T(8,128)(2,1)S(1)} %get-tuple-element.83), channel_id=1, source_target_pairs={{0,68},{1,69},{2,70},{3,71},{4,64},{5,65},{6,66},{7,67},{8,76},{9,... | collective-permute-start | bytes 516104 | tf_op jit(solution)/shard_map/ppermute | solution.py:43
  164.8 6.0 %collective-permute-start.14 = (f32[21,16,256]{2,1,0:T(8,128)S(1)}, f32[21,16,256]{2,1,0:T(8,128)S(1)}, u32[]{:S(2)}, u32[]{:S(2)}) collective-permute-start(f32[21,16,256]{2,1,0:T(8,128)S(1)} %fusion.1), channel_id=1, source_target_pairs={{0,32},{1,33},{2,34},{3,35},{4,36},{5,37},{6,38},{7,39},{8,40},{9,... | collective-permute-start | bytes 1032200 | tf_op jit(solution)/shard_map/ppermute | solution.py:43
Sparse Core Ops, SparseCore 0:
  15.9 65.9 all-gather.2
